TPU v7x, 32 devices: a whole 2x2x4 slice. The times are simulated.
32 devices in a mesh: arrays: 2 (over y), tm: 8 (over z, x), chan: 2 (over core).
Axes of the slice: x: 2, y: 2, z: 4, core: 2. Of those that a mesh axis runs over, the one named last changes fastest.
Arguments:
- spectra: bfloat16 [128, 256, 2, 128], P(('arrays', 'tm'), 'chan'), parts along dimension 0, may hold values from -40 to 40
- offsets: int32 [128], P(('arrays', 'tm')), parts along dimension 0, may hold values from 0 to 63
- channel_group: int32 [512], P(('arrays', 'chan')), parts along dimension 0, may hold values from 0 to 7
Outputs:
- stack: float32 [128, 48, 128], P(('arrays', 'tm', 'chan')), parts along dimension 0
There are 2 independent parts, one for each index of `arrays`. A program takes and returns all parts, laid end to end along the dimension named above; each array names one. Nothing has to cross between parts.
All inputs are finite; a program needn't handle non-finite values.
Results may differ from a plain program's by a relative error of at most 0.0075.
Values may be sent and summed in bfloat16 or wider, within the bound.
No kernel may reach another device: no remote copies, remote signals or barrier semaphores. Data moves between devices by JAX's collectives and lax.ppermute only.
A program may use at most 64 MiB of HBM per device.

v0:
```python
import math

import jax
import jax.numpy as jnp
from jax import lax
from jax.sharding import PartitionSpec as P

LAGS = 128
GROUPS = 8
SPAN = 6


epsilon = 1e-05


def shifted(value, axis, steps):
    count = lax.axis_size(axis)
    initial, last = (max(0, -steps), min(count, count - steps))
    return lax.ppermute(value, axis, [(source, source + steps) for source in range(initial, last)])


def lag_table(freq_bins, lag_count):
    frequency = jnp.arange(freq_bins, dtype=jnp.int32)[:, None]
    lag_shift = jnp.arange(lag_count, dtype=jnp.int32)[None, :] - lag_count // 2
    phase_turns = jnp.mod(frequency * lag_shift, 2 * freq_bins).astype(jnp.float32)
    phase_angle = jnp.pi * phase_turns / freq_bins
    normaliser = 1.0 / math.sqrt(freq_bins)
    lag_rows = jnp.concatenate(
        [jnp.cos(phase_angle) * normaliser, -jnp.sin(phase_angle) * normaliser], axis=0
    )
    return lag_rows.astype(jnp.bfloat16)


def align_spectra(spectra, offsets, scales):
    freq_bins = spectra.shape[3]
    frequency = jnp.arange(freq_bins, dtype=jnp.int32)[None, :]
    phase_turns = jnp.mod(offsets[:, None] * frequency, 2 * freq_bins).astype(jnp.float32)
    phase_angle = jnp.pi * phase_turns / freq_bins
    cosine = jnp.cos(phase_angle)[:, None, :]
    sine_part = jnp.sin(phase_angle)[:, None, :]
    real_part = spectra[:, :, 0, :].astype(jnp.float32)
    imag_part = spectra[:, :, 1, :].astype(jnp.float32)
    weight = scales[:, :, None]
    out_real = weight * (real_part * cosine + imag_part * sine_part)
    out_imag = weight * (imag_part * cosine - real_part * sine_part)
    return jnp.stack([out_real, out_imag], axis=2).astype(jnp.bfloat16)


def window_terms(current, band_rows, lag_rows):
    left_real = current[None, :, 0, :].astype(jnp.float32)
    left_imag = current[None, :, 1, :].astype(jnp.float32)
    right_real = band_rows[:, :, 0, :].astype(jnp.float32)
    right_imag = band_rows[:, :, 1, :].astype(jnp.float32)
    prod_real = left_real * right_real + left_imag * right_imag
    prod_imag = left_imag * right_real - left_real * right_imag
    cross_spec = jnp.stack([prod_real, prod_imag], axis=2).astype(jnp.bfloat16)
    flattened = cross_spec.reshape(band_rows.shape[0] * band_rows.shape[1], 2 * band_rows.shape[3])
    lagged = jnp.dot(flattened, lag_rows, preferred_element_type=jnp.float32)
    lagged = lagged.reshape(band_rows.shape[0], band_rows.shape[1], lag_rows.shape[1])
    return jnp.sum(lagged * lagged, axis=1)


def shards(spectra, offsets, channel_group):
    windows = spectra.shape[0]
    local_chans = spectra.shape[1]
    freq_bins = spectra.shape[3]
    chan_count = lax.axis_size("chan")
    channels = local_chans * chan_count
    onehot = (channel_group[:, None] == jnp.arange(GROUPS, dtype=jnp.int32)[None, :]).astype(
        jnp.float32
    )
    chan_power = jnp.sum(jnp.square(spectra.astype(jnp.float32)), axis=(2, 3))
    partial_value = jnp.dot(chan_power, onehot, precision=lax.Precision.HIGHEST)
    group_total = lax.psum(partial_value, "chan")
    energy = group_total * (GROUPS / (freq_bins * channels))
    scales = jnp.dot(lax.rsqrt(energy + epsilon), onehot.T, precision=lax.Precision.HIGHEST)
    aligned = align_spectra(spectra, offsets, scales)
    earlier = []
    carried = aligned
    for distance in range(SPAN):
        carried = shifted(carried, "tm", 1)
        earlier.append(carried)
    buffer = jnp.concatenate(earlier[::-1] + [aligned], axis=0)
    lag_rows = lag_table(freq_bins, LAGS)
    band_len = SPAN * windows

    def one_window(window):
        current = lax.dynamic_index_in_dim(aligned, window, 0, keepdims=False)
        band_rows = lax.dynamic_slice_in_dim(buffer, window, band_len, 0)
        return window_terms(current, band_rows, lag_rows) * (1.0 / channels)

    return lax.psum_scatter(
        lax.map(
            one_window, jnp.arange(lax.axis_size("chan") * (windows // chan_count), dtype=jnp.int32)
        ).astype(jnp.bfloat16),
        "chan",
        scatter_dimension=0,
        tiled=True,
    ).astype(jnp.float32)


def solution(mesh):
    placed = (P(("arrays", "tm"), "chan", None, None), P(("arrays", "tm")), P(("arrays", "chan")))
    return jax.shard_map(
        shards,
        mesh=mesh,
        in_specs=placed,
        out_specs=P(("arrays", "tm", "chan"), None, None),
        check_vma=False,
    )
```

profile of v0, /device:TPU:0, one launch (start us, length us, event | category | flops | bytes accessed | tf_op | source)
XLA Modules:
  0.0 234.0 jit_solution(17120011980369295450)
XLA Ops:
  8.8 3.1 %multiply_reduce_fusion.1 = f32[8,128]{1,0:T(8,128)S(1)} fusion(bf16[8,128,2,128]{3,2,1,0:T(2,128)(2,1)} %param.5), kind=kLoop, calls=%fused_computation.17 | loop fusion | flops 785408 | bytes 528384 | tf_op jit(solution)/shard_map/reduce_sum | solution.py:72
  17.4 4.8 %collective-permute-start = (bf16[8,128,2,128]{3,1,2,0:T(8,128)(2,1)S(1)}, bf16[8,128,2,128]{3,1,2,0:T(8,128)(2,1)S(1)}, u32[]{:S(2)}, u32[]{:S(2)}) collective-permute-start(bf16[8,128,2,128]{3,1,2,0:T(8,128)(2,1)S(1)} %pad_maximum_fusion.1), channel_id=1, source_target_pairs={{0,2},{2,4},{4,6},{6,8},{8,10},{10,12},{12,14},{1,3},{3,5},{5,7},{... | collective-permute-start | bytes 1572872 | tf_op jit(solution)/shard_map/ppermute | solution.py:19
  22.2 11.5 %collective-permute-done = bf16[8,128,2,128]{3,1,2,0:T(8,128)(2,1)S(1)} collective-permute-done((bf16[8,128,2,128]{3,1,2,0:T(8,128)(2,1)S(1)}, bf16[8,128,2,128]{3,1,2,0:T(8,128)(2,1)S(1)}, u32[]{:S(2)}, u32[]{:S(2)}) %collective-permute-start) | collective-permute-done | bytes 524320 | tf_op jit(solution)/shard_map/ppermute | solution.py:19
  33.7 4.4 %collective-permute-start.1 = (bf16[8,128,2,128]{3,1,2,0:T(8,128)(2,1)S(1)}, bf16[8,128,2,128]{3,1,2,0:T(8,128)(2,1)S(1)}, u32[]{:S(2)}, u32[]{:S(2)}) collective-permute-start(bf16[8,128,2,128]{3,1,2,0:T(8,128)(2,1)S(1)} %collective-permute-done), channel_id=1, source_target_pairs={{0,2},{2,4},{4,6},{6,8},{8,10},{10,12},{12,14},{1,3},{3,5},{5,7},{... | collective-permute-start | bytes 1572872 | tf_op jit(solution)/shard_map/ppermute | solution.py:19
  38.1 10.6 %collective-permute-done.1 = bf16[8,128,2,128]{3,1,2,0:T(8,128)(2,1)S(1)} collective-permute-done((bf16[8,128,2,128]{3,1,2,0:T(8,128)(2,1)S(1)}, bf16[8,128,2,128]{3,1,2,0:T(8,128)(2,1)S(1)}, u32[]{:S(2)}, u32[]{:S(2)}) %collective-permute-start.1) | collective-permute-done | bytes 524320 | tf_op jit(solution)/shard_map/ppermute | solution.py:19
  48.7 4.4 %collective-permute-start.2 = (bf16[8,128,2,128]{3,1,2,0:T(8,128)(2,1)S(1)}, bf16[8,128,2,128]{3,1,2,0:T(8,128)(2,1)S(1)}, u32[]{:S(2)}, u32[]{:S(2)}) collective-permute-start(bf16[8,128,2,128]{3,1,2,0:T(8,128)(2,1)S(1)} %collective-permute-done.1), channel_id=1, source_target_pairs={{0,2},{2,4},{4,6},{6,8},{8,10},{10,12},{12,14},{1,3},{3,5},{5,7},{... | collective-permute-start | bytes 1572872 | tf_op jit(solution)/shard_map/ppermute | solution.py:19
  53.1 9.7 %collective-permute-done.2 = bf16[8,128,2,128]{3,1,2,0:T(8,128)(2,1)S(1)} collective-permute-done((bf16[8,128,2,128]{3,1,2,0:T(8,128)(2,1)S(1)}, bf16[8,128,2,128]{3,1,2,0:T(8,128)(2,1)S(1)}, u32[]{:S(2)}, u32[]{:S(2)}) %collective-permute-start.2) | collective-permute-done | bytes 524320 | tf_op jit(solution)/shard_map/ppermute | solution.py:19
  62.8 5.3 %collective-permute-start.3 = (bf16[8,128,2,128]{3,1,2,0:T(8,128)(2,1)S(1)}, bf16[8,128,2,128]{3,1,2,0:T(8,128)(2,1)S(1)}, u32[]{:S(2)}, u32[]{:S(2)}) collective-permute-start(bf16[8,128,2,128]{3,1,2,0:T(8,128)(2,1)S(1)} %collective-permute-done.2), channel_id=1, source_target_pairs={{0,2},{2,4},{4,6},{6,8},{8,10},{10,12},{12,14},{1,3},{3,5},{5,7},{... | collective-permute-start | bytes 1572872 | tf_op jit(solution)/shard_map/ppermute | solution.py:19
  68.1 8.8 %collective-permute-done.3 = bf16[8,128,2,128]{3,1,2,0:T(8,128)(2,1)S(1)} collective-permute-done((bf16[8,128,2,128]{3,1,2,0:T(8,128)(2,1)S(1)}, bf16[8,128,2,128]{3,1,2,0:T(8,128)(2,1)S(1)}, u32[]{:S(2)}, u32[]{:S(2)}) %collective-permute-start.3) | collective-permute-done | bytes 524320 | tf_op jit(solution)/shard_map/ppermute | solution.py:19
  76.9 6.1 %collective-permute-start.4 = (bf16[8,128,2,128]{3,1,2,0:T(8,128)(2,1)S(1)}, bf16[8,128,2,128]{3,1,2,0:T(8,128)(2,1)}, u32[]{:S(2)}, u32[]{:S(2)}) collective-permute-start(bf16[8,128,2,128]{3,1,2,0:T(8,128)(2,1)S(1)} %collective-permute-done.3), channel_id=1, source_target_pairs={{0,2},{2,4},{4,6},{6,8},{8,10},{10,12},{12,14},{1,3},{3,5},{5,7},{... | collective-permute-start | bytes 1572872 | tf_op jit(solution)/shard_map/ppermute | solution.py:19
  83.0 7.1 %collective-permute-done.4 = bf16[8,128,2,128]{3,1,2,0:T(8,128)(2,1)} collective-permute-done((bf16[8,128,2,128]{3,1,2,0:T(8,128)(2,1)S(1)}, bf16[8,128,2,128]{3,1,2,0:T(8,128)(2,1)}, u32[]{:S(2)}, u32[]{:S(2)}) %collective-permute-start.4) | collective-permute-done | bytes 524320 | tf_op jit(solution)/shard_map/ppermute | solution.py:19
  90.1 6.1 %collective-permute-start.5 = (bf16[8,128,2,128]{3,1,2,0:T(8,128)(2,1)}, bf16[8,128,2,128]{3,1,2,0:T(8,128)(2,1)}, u32[]{:S(2)}, u32[]{:S(2)}) collective-permute-start(bf16[8,128,2,128]{3,1,2,0:T(8,128)(2,1)} %collective-permute-done.4), channel_id=1, source_target_pairs={{0,2},{2,4},{4,6},{6,8},{8,10},{10,12},{12,14},{1,3},{3,5},{5,7},{... | collective-permute-start | bytes 1572872 | tf_op jit(solution)/shard_map/ppermute | solution.py:19
  96.5 6.2 %collective-permute-done.5 = bf16[8,128,2,128]{3,1,2,0:T(8,128)(2,1)} collective-permute-done((bf16[8,128,2,128]{3,1,2,0:T(8,128)(2,1)}, bf16[8,128,2,128]{3,1,2,0:T(8,128)(2,1)}, u32[]{:S(2)}, u32[]{:S(2)}) %collective-permute-start.5) | collective-permute-done | bytes 524320 | tf_op jit(solution)/shard_map/ppermute | solution.py:19
  107.1 106.2 %while.10 = (s32[]{:T(128)}, bf16[8,48,128]{2,1,0:T(8,128)(2,1)S(1)}, s32[8]{0:T(128)S(1)}, bf16[8,128,2,128]{3,1,2,0:T(8,128)(2,1)S(1)}, bf16[56,128,2,128]{3,1...) while((s32[]{:T(128)}, ...), condition=%wide.region_4.5_spmd, body=%wide.region_2.4_spmd.sunk | while | flops 413696000 | bytes 26812680 | solution.py:93
  110.8 3.3 %fusion.48 = (bf16[48,128,1,128]{3,1,2,0:T(8,128)(2,1)S(1)}, bf16[48,128,1,128]{3,1,2,0:T(8,128)(2,1)S(1)}) fusion(f32[128,128]{1,0:T(8,128)S(1)} %get-tuple-element.103, f32[128,128]{1,0:T(8,128)S(1)} %get-tuple-element.104, bf16[56,128,2,128]{3,1,2,0:T(8,128)(2,1)} %get-tuple-element.133, s32[]{:T(128)S(6)} %select_n.52, s32[]{:T(128)S(6)} %add.104), kind=kLoop, calls=%fused_computation.5.clone.1 | loop fusion | flops 7864320 | bytes 6422536 | tf_op jit(solution)/shard_map/convert.2
  124.1 3.3 %fusion.48 = (bf16[48,128,1,128]{3,1,2,0:T(8,128)(2,1)S(1)}, bf16[48,128,1,128]{3,1,2,0:T(8,128)(2,1)S(1)}) fusion(f32[128,128]{1,0:T(8,128)S(1)} %get-tuple-element.103, f32[128,128]{1,0:T(8,128)S(1)} %get-tuple-element.104, bf16[56,128,2,128]{3,1,2,0:T(8,128)(2,1)} %get-tuple-element.133, s32[]{:T(128)S(6)} %select_n.52, s32[]{:T(128)S(6)} %add.104), kind=kLoop, calls=%fused_computation.5.clone.1 | loop fusion | flops 7864320 | bytes 6422536 | tf_op jit(solution)/shard_map/convert.2
  137.4 3.3 %fusion.48 = (bf16[48,128,1,128]{3,1,2,0:T(8,128)(2,1)S(1)}, bf16[48,128,1,128]{3,1,2,0:T(8,128)(2,1)S(1)}) fusion(f32[128,128]{1,0:T(8,128)S(1)} %get-tuple-element.103, f32[128,128]{1,0:T(8,128)S(1)} %get-tuple-element.104, bf16[56,128,2,128]{3,1,2,0:T(8,128)(2,1)} %get-tuple-element.133, s32[]{:T(128)S(6)} %select_n.52, s32[]{:T(128)S(6)} %add.104), kind=kLoop, calls=%fused_computation.5.clone.1 | loop fusion | flops 7864320 | bytes 6422536 | tf_op jit(solution)/shard_map/convert.2
  150.7 3.3 %fusion.48 = (bf16[48,128,1,128]{3,1,2,0:T(8,128)(2,1)S(1)}, bf16[48,128,1,128]{3,1,2,0:T(8,128)(2,1)S(1)}) fusion(f32[128,128]{1,0:T(8,128)S(1)} %get-tuple-element.103, f32[128,128]{1,0:T(8,128)S(1)} %get-tuple-element.104, bf16[56,128,2,128]{3,1,2,0:T(8,128)(2,1)} %get-tuple-element.133, s32[]{:T(128)S(6)} %select_n.52, s32[]{:T(128)S(6)} %add.104), kind=kLoop, calls=%fused_computation.5.clone.1 | loop fusion | flops 7864320 | bytes 6422536 | tf_op jit(solution)/shard_map/convert.2
  163.9 3.3 %fusion.48 = (bf16[48,128,1,128]{3,1,2,0:T(8,128)(2,1)S(1)}, bf16[48,128,1,128]{3,1,2,0:T(8,128)(2,1)S(1)}) fusion(f32[128,128]{1,0:T(8,128)S(1)} %get-tuple-element.103, f32[128,128]{1,0:T(8,128)S(1)} %get-tuple-element.104, bf16[56,128,2,128]{3,1,2,0:T(8,128)(2,1)} %get-tuple-element.133, s32[]{:T(128)S(6)} %select_n.52, s32[]{:T(128)S(6)} %add.104), kind=kLoop, calls=%fused_computation.5.clone.1 | loop fusion | flops 7864320 | bytes 6422536 | tf_op jit(solution)/shard_map/convert.2
  170.4 3.0 %multiply_reduce_fusion.3 = f32[48,128]{1,0:T(8,128)S(1)} fusion(bf16[48,128,256]{1,2,0:T(8,128)(2,1)} %bitcast.35, bf16[256,128]{1,0:T(8,128)(2,1)S(1)} %get-tuple-element.134), kind=kOutput, calls=%fused_computation.9.clone.1 | convolution fusion | flops 404219904 | bytes 3235840 | tf_op jit(solution)/shard_map/while/body/eval_jaxpr/dot_general | solution.py:58
  177.2 3.3 %fusion.48 = (bf16[48,128,1,128]{3,1,2,0:T(8,128)(2,1)S(1)}, bf16[48,128,1,128]{3,1,2,0:T(8,128)(2,1)S(1)}) fusion(f32[128,128]{1,0:T(8,128)S(1)} %get-tuple-element.103, f32[128,128]{1,0:T(8,128)S(1)} %get-tuple-element.104, bf16[56,128,2,128]{3,1,2,0:T(8,128)(2,1)} %get-tuple-element.133, s32[]{:T(128)S(6)} %select_n.52, s32[]{:T(128)S(6)} %add.104), kind=kLoop, calls=%fused_computation.5.clone.1 | loop fusion | flops 7864320 | bytes 6422536 | tf_op jit(solution)/shard_map/convert.2
  190.5 3.3 %fusion.48 = (bf16[48,128,1,128]{3,1,2,0:T(8,128)(2,1)S(1)}, bf16[48,128,1,128]{3,1,2,0:T(8,128)(2,1)S(1)}) fusion(f32[128,128]{1,0:T(8,128)S(1)} %get-tuple-element.103, f32[128,128]{1,0:T(8,128)S(1)} %get-tuple-element.104, bf16[56,128,2,128]{3,1,2,0:T(8,128)(2,1)} %get-tuple-element.133, s32[]{:T(128)S(6)} %select_n.52, s32[]{:T(128)S(6)} %add.104), kind=kLoop, calls=%fused_computation.5.clone.1 | loop fusion | flops 7864320 | bytes 6422536 | tf_op jit(solution)/shard_map/convert.2
  203.8 3.3 %fusion.48 = (bf16[48,128,1,128]{3,1,2,0:T(8,128)(2,1)S(1)}, bf16[48,128,1,128]{3,1,2,0:T(8,128)(2,1)S(1)}) fusion(f32[128,128]{1,0:T(8,128)S(1)} %get-tuple-element.103, f32[128,128]{1,0:T(8,128)S(1)} %get-tuple-element.104, bf16[56,128,2,128]{3,1,2,0:T(8,128)(2,1)} %get-tuple-element.133, s32[]{:T(128)S(6)} %select_n.52, s32[]{:T(128)S(6)} %add.104), kind=kLoop, calls=%fused_computation.5.clone.1 | loop fusion | flops 7864320 | bytes 6422536 | tf_op jit(solution)/shard_map/convert.2
  213.9 11.8 %reduce-scatter.2.cloned.1.call-done = bf16[4,48,128]{2,1,0:T(8,128)(2,1)} async-done(((bf16[8,48,128]{2,1,0:T(8,128)(2,1)}), bf16[4,48,128]{2,1,0:T(8,128)(2,1)}) %reduce-scatter.2.cloned.1.call-update) | async-done | bytes 49168 | tf_op jit(solution)/shard_map/reduce_scatter | solution.py:92
  (113 shorter events, 66.2 us)
Async XLA Ops:
  6.5 219.2 %reduce-scatter.2.cloned.1.call-start = ((), (), s32[]{:S(2)}) async-start(), calls=%async_computation.1 | async-start | bytes 147456 | tf_op jit(solution)/shard_map/reduce_scatter | solution.py:92
  17.4 16.2 %collective-permute-start = (bf16[8,128,2,128]{3,1,2,0:T(8,128)(2,1)S(1)}, bf16[8,128,2,128]{3,1,2,0:T(8,128)(2,1)S(1)}, u32[]{:S(2)}, u32[]{:S(2)}) collective-permute-start(bf16[8,128,2,128]{3,1,2,0:T(8,128)(2,1)S(1)} %pad_maximum_fusion.1), channel_id=1, source_target_pairs={{0,2},{2,4},{4,6},{6,8},{8,10},{10,12},{12,14},{1,3},{3,5},{5,7},{... | collective-permute-start | bytes 1572872 | tf_op jit(solution)/shard_map/ppermute | solution.py:19
  33.7 15.0 %collective-permute-start.1 = (bf16[8,128,2,128]{3,1,2,0:T(8,128)(2,1)S(1)}, bf16[8,128,2,128]{3,1,2,0:T(8,128)(2,1)S(1)}, u32[]{:S(2)}, u32[]{:S(2)}) collective-permute-start(bf16[8,128,2,128]{3,1,2,0:T(8,128)(2,1)S(1)} %collective-permute-done), channel_id=1, source_target_pairs={{0,2},{2,4},{4,6},{6,8},{8,10},{10,12},{12,14},{1,3},{3,5},{5,7},{... | collective-permute-start | bytes 1572872 | tf_op jit(solution)/shard_map/ppermute | solution.py:19
  48.7 14.1 %collective-permute-start.2 = (bf16[8,128,2,128]{3,1,2,0:T(8,128)(2,1)S(1)}, bf16[8,128,2,128]{3,1,2,0:T(8,128)(2,1)S(1)}, u32[]{:S(2)}, u32[]{:S(2)}) collective-permute-start(bf16[8,128,2,128]{3,1,2,0:T(8,128)(2,1)S(1)} %collective-permute-done.1), channel_id=1, source_target_pairs={{0,2},{2,4},{4,6},{6,8},{8,10},{10,12},{12,14},{1,3},{3,5},{5,7},{... | collective-permute-start | bytes 1572872 | tf_op jit(solution)/shard_map/ppermute | solution.py:19
  62.8 14.1 %collective-permute-start.3 = (bf16[8,128,2,128]{3,1,2,0:T(8,128)(2,1)S(1)}, bf16[8,128,2,128]{3,1,2,0:T(8,128)(2,1)S(1)}, u32[]{:S(2)}, u32[]{:S(2)}) collective-permute-start(bf16[8,128,2,128]{3,1,2,0:T(8,128)(2,1)S(1)} %collective-permute-done.2), channel_id=1, source_target_pairs={{0,2},{2,4},{4,6},{6,8},{8,10},{10,12},{12,14},{1,3},{3,5},{5,7},{... | collective-permute-start | bytes 1572872 | tf_op jit(solution)/shard_map/ppermute | solution.py:19
  76.9 13.2 %collective-permute-start.4 = (bf16[8,128,2,128]{3,1,2,0:T(8,128)(2,1)S(1)}, bf16[8,128,2,128]{3,1,2,0:T(8,128)(2,1)}, u32[]{:S(2)}, u32[]{:S(2)}) collective-permute-start(bf16[8,128,2,128]{3,1,2,0:T(8,128)(2,1)S(1)} %collective-permute-done.3), channel_id=1, source_target_pairs={{0,2},{2,4},{4,6},{6,8},{8,10},{10,12},{12,14},{1,3},{3,5},{5,7},{... | collective-permute-start | bytes 1572872 | tf_op jit(solution)/shard_map/ppermute | solution.py:19
  90.1 12.6 %collective-permute-start.5 = (bf16[8,128,2,128]{3,1,2,0:T(8,128)(2,1)}, bf16[8,128,2,128]{3,1,2,0:T(8,128)(2,1)}, u32[]{:S(2)}, u32[]{:S(2)}) collective-permute-start(bf16[8,128,2,128]{3,1,2,0:T(8,128)(2,1)} %collective-permute-done.4), channel_id=1, source_target_pairs={{0,2},{2,4},{4,6},{6,8},{8,10},{10,12},{12,14},{1,3},{3,5},{5,7},{... | collective-permute-start | bytes 1572872 | tf_op jit(solution)/shard_map/ppermute | solution.py:19
  105.3 1.8 copy-start
  107.1 7.1 %copy-start.1 = (bf16[8,128,2,128]{3,1,2,0:T(8,128)(2,1)}, bf16[8,128,2,128]{3,1,2,0:T(8,128)(2,1)S(1)}, u32[]{:S(2)}) copy-start(bf16[8,128,2,128]{3,1,2,0:T(8,128)(2,1)S(1)} %get-tuple-element.132) | copy-start | bytes 1572868 | tf_op jit(solution)/shard_map/while
  117.3 3.0 %copy-start.2 = (bf16[8,128,2,128]{3,1,2,0:T(8,128)(2,1)S(1)}, bf16[8,128,2,128]{3,1,2,0:T(8,128)(2,1)}, u32[]{:S(2)}) copy-start(bf16[8,128,2,128]{3,1,2,0:T(8,128)(2,1)} %copy-done.1) | copy-start | bytes 1572868 | tf_op jit(solution)/shard_map/while
  120.3 7.1 %copy-start.1 = (bf16[8,128,2,128]{3,1,2,0:T(8,128)(2,1)}, bf16[8,128,2,128]{3,1,2,0:T(8,128)(2,1)S(1)}, u32[]{:S(2)}) copy-start(bf16[8,128,2,128]{3,1,2,0:T(8,128)(2,1)S(1)} %get-tuple-element.132) | copy-start | bytes 1572868 | tf_op jit(solution)/shard_map/while
  130.5 3.0 %copy-start.2 = (bf16[8,128,2,128]{3,1,2,0:T(8,128)(2,1)S(1)}, bf16[8,128,2,128]{3,1,2,0:T(8,128)(2,1)}, u32[]{:S(2)}) copy-start(bf16[8,128,2,128]{3,1,2,0:T(8,128)(2,1)} %copy-done.1) | copy-start | bytes 1572868 | tf_op jit(solution)/shard_map/while
  133.6 7.1 %copy-start.1 = (bf16[8,128,2,128]{3,1,2,0:T(8,128)(2,1)}, bf16[8,128,2,128]{3,1,2,0:T(8,128)(2,1)S(1)}, u32[]{:S(2)}) copy-start(bf16[8,128,2,128]{3,1,2,0:T(8,128)(2,1)S(1)} %get-tuple-element.132) | copy-start | bytes 1572868 | tf_op jit(solution)/shard_map/while
  143.8 3.0 %copy-start.2 = (bf16[8,128,2,128]{3,1,2,0:T(8,128)(2,1)S(1)}, bf16[8,128,2,128]{3,1,2,0:T(8,128)(2,1)}, u32[]{:S(2)}) copy-start(bf16[8,128,2,128]{3,1,2,0:T(8,128)(2,1)} %copy-done.1) | copy-start | bytes 1572868 | tf_op jit(solution)/shard_map/while
  146.9 7.1 %copy-start.1 = (bf16[8,128,2,128]{3,1,2,0:T(8,128)(2,1)}, bf16[8,128,2,128]{3,1,2,0:T(8,128)(2,1)S(1)}, u32[]{:S(2)}) copy-start(bf16[8,128,2,128]{3,1,2,0:T(8,128)(2,1)S(1)} %get-tuple-element.132) | copy-start | bytes 1572868 | tf_op jit(solution)/shard_map/while
  157.1 3.0 %copy-start.2 = (bf16[8,128,2,128]{3,1,2,0:T(8,128)(2,1)S(1)}, bf16[8,128,2,128]{3,1,2,0:T(8,128)(2,1)}, u32[]{:S(2)}) copy-start(bf16[8,128,2,128]{3,1,2,0:T(8,128)(2,1)} %copy-done.1) | copy-start | bytes 1572868 | tf_op jit(solution)/shard_map/while
  160.1 7.1 %copy-start.1 = (bf16[8,128,2,128]{3,1,2,0:T(8,128)(2,1)}, bf16[8,128,2,128]{3,1,2,0:T(8,128)(2,1)S(1)}, u32[]{:S(2)}) copy-start(bf16[8,128,2,128]{3,1,2,0:T(8,128)(2,1)S(1)} %get-tuple-element.132) | copy-start | bytes 1572868 | tf_op jit(solution)/shard_map/while
  170.4 3.0 %copy-start.2 = (bf16[8,128,2,128]{3,1,2,0:T(8,128)(2,1)S(1)}, bf16[8,128,2,128]{3,1,2,0:T(8,128)(2,1)}, u32[]{:S(2)}) copy-start(bf16[8,128,2,128]{3,1,2,0:T(8,128)(2,1)} %copy-done.1) | copy-start | bytes 1572868 | tf_op jit(solution)/shard_map/while
  173.4 7.1 %copy-start.1 = (bf16[8,128,2,128]{3,1,2,0:T(8,128)(2,1)}, bf16[8,128,2,128]{3,1,2,0:T(8,128)(2,1)S(1)}, u32[]{:S(2)}) copy-start(bf16[8,128,2,128]{3,1,2,0:T(8,128)(2,1)S(1)} %get-tuple-element.132) | copy-start | bytes 1572868 | tf_op jit(solution)/shard_map/while
  183.6 3.0 %copy-start.2 = (bf16[8,128,2,128]{3,1,2,0:T(8,128)(2,1)S(1)}, bf16[8,128,2,128]{3,1,2,0:T(8,128)(2,1)}, u32[]{:S(2)}) copy-start(bf16[8,128,2,128]{3,1,2,0:T(8,128)(2,1)} %copy-done.1) | copy-start | bytes 1572868 | tf_op jit(solution)/shard_map/while
  186.7 7.1 %copy-start.1 = (bf16[8,128,2,128]{3,1,2,0:T(8,128)(2,1)}, bf16[8,128,2,128]{3,1,2,0:T(8,128)(2,1)S(1)}, u32[]{:S(2)}) copy-start(bf16[8,128,2,128]{3,1,2,0:T(8,128)(2,1)S(1)} %get-tuple-element.132) | copy-start | bytes 1572868 | tf_op jit(solution)/shard_map/while
  196.9 3.0 %copy-start.2 = (bf16[8,128,2,128]{3,1,2,0:T(8,128)(2,1)S(1)}, bf16[8,128,2,128]{3,1,2,0:T(8,128)(2,1)}, u32[]{:S(2)}) copy-start(bf16[8,128,2,128]{3,1,2,0:T(8,128)(2,1)} %copy-done.1) | copy-start | bytes 1572868 | tf_op jit(solution)/shard_map/while
  200.0 7.1 %copy-start.1 = (bf16[8,128,2,128]{3,1,2,0:T(8,128)(2,1)}, bf16[8,128,2,128]{3,1,2,0:T(8,128)(2,1)S(1)}, u32[]{:S(2)}) copy-start(bf16[8,128,2,128]{3,1,2,0:T(8,128)(2,1)S(1)} %get-tuple-element.132) | copy-start | bytes 1572868 | tf_op jit(solution)/shard_map/while
  210.2 3.0 %copy-start.2 = (bf16[8,128,2,128]{3,1,2,0:T(8,128)(2,1)S(1)}, bf16[8,128,2,128]{3,1,2,0:T(8,128)(2,1)}, u32[]{:S(2)}) copy-start(bf16[8,128,2,128]{3,1,2,0:T(8,128)(2,1)} %copy-done.1) | copy-start | bytes 1572868 | tf_op jit(solution)/shard_map/while
  (1 other events, 0.6 us)
Sparse Core Ops, SparseCore 0:
  214.0 11.6 reduce-scatter.1
where the time goes:
time: 235 us; the launch traced here: 234 us
  waiting for transfers between devices  65.7 us (28%)
  local copies, waits for them, and re-layouts  35.3 us (15%)
  other arithmetic  35 us (15%)
  starting transfers between devices  31 us (13%)
  matrix products  25.6 us (11%)
  loops' own time  25.3 us (11%)
  between operations  13.5 us (6%)
  blocking collectives  2.59 us (1%)
    ppermute x6, waiting for transfers between devices, shifted(): lax.ppermute(value, axis, [(source, source + steps) for source in range(i...  53.9 us
    ppermute x6, starting transfers between devices, shifted(): lax.ppermute(value, axis, [(source, source + steps) for source in range(i...  31 us
    another operation x10, other arithmetic  26.8 us
    another operation x1, loops' own time, shards(): lax.map(one_window, jnp.arange(lax.axis_size('chan') * (windows // chan_c...  25.3 us
    dot_general x8, matrix products, window_terms(): lagged = jnp.dot(flattened, lag_rows, preferred_element_type=jnp.float32)  23.9 us
    another operation x8, local copies, waits for them, and re-layouts, window_terms(): cross_spec = jnp.stack([prod_real, prod_imag], axis=2).astype(jnp.bfloat16)  22.6 us
    reduce_scatter x1, waiting for transfers between devices, shards(): lax.psum_scatter(lax.map(one_window, jnp.arange(lax.axis_size('chan') * (...  11.8 us
    dynamic_slice x8, local copies, waits for them, and re-layouts, shards(): lax.map(one_window, jnp.arange(lax.axis_size('chan') * (windows // chan_c...  5.37 us
  transfers between devices with their start and end apart: 7, of which 7 were waited for; matrix products, arithmetic and copies ran while one was open for 0% of the time, Pallas kernels for 0%

commit v1 on v0

v1 whole, which is shorter than its diff:
```python
import functools
import math

import jax
import jax.numpy as jnp
from jax import lax
from jax.experimental import pallas as pl
from jax.experimental.pallas import tpu as pltpu
from jax.sharding import PartitionSpec as P

LAGS = 128
GROUPS = 8
SPAN = 6
SIDES = 2
LEVELS = 4
TEAM = SIDES * LEVELS

epsilon = 1e-05

HIGHEST = lax.Precision.HIGHEST


def lag_table(freq_bins, lag_count):
    frequency = jnp.arange(freq_bins, dtype=jnp.int32)[:, None]
    lag_shift = jnp.arange(lag_count, dtype=jnp.int32)[None, :] - lag_count // 2
    phase_turns = jnp.mod(frequency * lag_shift, 2 * freq_bins).astype(jnp.float32)
    phase_angle = jnp.pi * phase_turns / freq_bins
    normaliser = 1.0 / math.sqrt(freq_bins)
    lag_rows = jnp.concatenate(
        [jnp.cos(phase_angle) * normaliser, -jnp.sin(phase_angle) * normaliser], axis=0
    )
    return lag_rows.astype(jnp.bfloat16)


def phases(offsets, freq_bins):
    frequency = jnp.arange(freq_bins, dtype=jnp.int32)[None, :]
    phase_turns = jnp.mod(offsets[:, None] * frequency, 2 * freq_bins).astype(jnp.float32)
    phase_angle = jnp.pi * phase_turns / freq_bins
    return jnp.stack([jnp.cos(phase_angle), jnp.sin(phase_angle)])


def member_rows(group_row):
    channels = group_row.shape[1]
    groups = lax.broadcasted_iota(jnp.int32, (GROUPS, channels), 0)
    return (group_row == groups).astype(jnp.float32)


def power_kernel(spectra_ref, group_ref, power_ref, rows_ref):
    windows, rows, _ = spectra_ref.shape
    member = member_rows(group_ref[...])
    lane = lax.broadcasted_iota(jnp.int32, power_ref.shape, 1)
    power = jnp.zeros(power_ref.shape, jnp.float32)
    for window in range(windows):
        value = spectra_ref[window].astype(jnp.float32)
        rows_ref[window] = value * value
        squares = rows_ref[window, pl.ds(0, rows // 2, stride=2), :] + rows_ref[window, pl.ds(1, rows // 2, stride=2), :]
        grouped = jnp.dot(member, squares, precision=HIGHEST, preferred_element_type=jnp.float32)
        power = jnp.where(lane == window, jnp.sum(grouped, axis=1, keepdims=True), power)
    power_ref[...] = power


def align_kernel(scale_of_energy, spectra_ref, group_ref, own_ref, other_ref, phase_ref, *rest):
    pieces, (rows_ref, scale_ref) = rest[:LEVELS], rest[LEVELS:]
    windows, rows, _ = spectra_ref.shape
    part = rows // 2 // LEVELS
    level = lax.rem(lax.axis_index("tm"), TEAM) // SIDES
    energy = (own_ref[...] + other_ref[...]) * scale_of_energy
    scale_ref[...] = lax.dot_general(
        member_rows(group_ref[...]), lax.rsqrt(energy + epsilon), (((0,), (0,)), ((), ())),
        precision=HIGHEST, preferred_element_type=jnp.float32,
    )
    for window in range(windows):
        rows_ref[window] = spectra_ref[window].astype(jnp.float32)
    for step in range(LEVELS):
        first = pl.multiple_of((level ^ step) * part, part)
        weights = scale_ref[pl.ds(first, part), :]
        for window in range(windows):
            cosine = phase_ref[0, window : window + 1, :]
            sine = phase_ref[1, window : window + 1, :]
            real = rows_ref[window, pl.ds(2 * first, part, stride=2), :]
            imag = rows_ref[window, pl.ds(2 * first + 1, part, stride=2), :]
            weight = weights[:, window : window + 1]
            pieces[step][window, 0] = (weight * (real * cosine + imag * sine)).astype(jnp.bfloat16)
            pieces[step][window, 1] = (weight * (imag * cosine - real * sine)).astype(jnp.bfloat16)


def stack_kernel(blocks_before, count, *refs):
    table_ref = refs[0]
    pieces = refs[1 : 1 + count]
    outs = refs[1 + count : 1 + count + LEVELS]
    held, sems = refs[1 + count + LEVELS :]
    windows, _, part, _ = pieces[0].shape
    member = lax.rem(lax.axis_index("tm"), TEAM)
    side, level = lax.rem(member, SIDES), member // SIDES
    core = lax.axis_index("chan")
    halves = held.shape[2] // part
    copies = []
    for index, piece in enumerate(pieces):
        slot, half = index // halves, index % halves
        round_, slot = slot // TEAM, slot % TEAM
        hop, step = slot // LEVELS, slot % LEVELS
        block = (level ^ step) * SIDES + (side ^ hop)
        place = (block + (blocks_before if round_ == 0 else 0)) * windows
        copies.append(pltpu.make_async_copy(
            piece, held.at[pl.ds(place, windows), :, pl.ds(half * part, part), :], sems.at[index]))
    for copy in copies:
        copy.start()
    if count == TEAM * halves:
        held[pl.ds(0, blocks_before * windows)] = jnp.zeros((blocks_before * windows,) + held.shape[1:], held.dtype)
    for copy in copies:
        copy.wait()
    table = table_ref[...]
    batch = windows
    channels, freq = held.shape[2], held.shape[3]
    band = outs[0].shape[1]
    keep = outs[0].shape[0]
    for step in range(LEVELS):
        out = outs[step]
        block = (level ^ step) * SIDES + side + blocks_before
        for inner in range(keep):
            window = block * windows + core * keep + inner
            lowest = jnp.maximum(0, (band - window) // batch)
            if count == TEAM * halves:
                lowest = jnp.maximum(0, (band + (blocks_before * windows) - window) // batch)

            def clear(index, carry):
                out[inner, pl.ds(pl.multiple_of(index * batch, batch), batch), :] = jnp.zeros((batch, out.shape[2]), out.dtype)
                return carry

            def one(index, carry):
                start = window - band + index * batch
                left_real = held[window, 0][None]
                left_imag = held[window, 1][None]
                right_real = held[pl.ds(start, batch), 0]
                right_imag = held[pl.ds(start, batch), 1]
                real = left_real * right_real + left_imag * right_imag
                imag = left_imag * right_real - left_real * right_imag
                cross = jnp.concatenate(
                    [real.reshape(batch * channels, freq), imag.reshape(batch * channels, freq)], axis=1)
                lagged = jnp.dot(cross, table, preferred_element_type=jnp.float32)
                total = jnp.sum((lagged * lagged).reshape(batch, channels, table.shape[1]), axis=1)
                out[inner, pl.ds(pl.multiple_of(index * batch, batch), batch), :] = total.astype(out.dtype)
                return carry

            lax.fori_loop(0, lowest, clear, 0)
            lax.fori_loop(lowest, band // batch, one, 0)


def vmem():
    return pl.BlockSpec(memory_space=pltpu.VMEM)


def flip(value, axis, size, bits):
    return lax.ppermute(value, axis, [(source, source ^ bits) for source in range(size)])


def shards(spectra, offsets, channel_group):
    windows, local_chans, _, freq = spectra.shape
    chan_count = lax.axis_size("chan")
    tm_count = lax.axis_size("tm")
    channels = local_chans * chan_count
    part = local_chans // LEVELS
    band = SPAN * windows
    keep = windows // chan_count
    params = pltpu.CompilerParams(vmem_limit_bytes=48 * 1024 * 1024)

    rows = spectra.reshape(windows, 2 * local_chans, freq)
    group_row = channel_group.reshape(1, local_chans)
    power = pl.pallas_call(
        power_kernel,
        out_shape=jax.ShapeDtypeStruct((GROUPS, 128), jnp.float32),
        in_specs=[vmem(), vmem()],
        out_specs=vmem(),
        scratch_shapes=[pltpu.VMEM((windows, 2 * local_chans, freq), jnp.float32)],
        compiler_params=params,
        name="power",
    )(rows, group_row)
    other_power = flip(power, "chan", chan_count, 1)
    piece_shape = jax.ShapeDtypeStruct((windows, 2, part, freq), jnp.bfloat16)
    own = pl.pallas_call(
        functools.partial(align_kernel, GROUPS / (freq * channels)),
        out_shape=[piece_shape] * LEVELS,
        in_specs=[vmem()] * 5,
        out_specs=[vmem()] * LEVELS,
        scratch_shapes=[
            pltpu.VMEM((windows, 2 * local_chans, freq), jnp.float32),
            pltpu.VMEM((local_chans, 128), jnp.float32),
        ],
        compiler_params=params,
        name="align",
    )(rows, group_row, power, other_power, phases(offsets, freq))

    near = [own[0]] + [None] * (LEVELS - 1)
    far = [None] * LEVELS
    order = (2, 1, 3)
    near[2] = flip(own[2], "tm", tm_count, 2 * SIDES)
    far[0] = flip(own[0], "tm", tm_count, 1)
    near[1] = flip(own[1], "tm", tm_count, 1 * SIDES)
    near[3] = flip(own[3], "tm", tm_count, 3 * SIDES)
    for step in order:
        far[step] = flip(near[step], "tm", tm_count, 1)
    held = []
    for piece in near + far:
        held += [piece, flip(piece, "chan", chan_count, 1)]
    before = 1
    if tm_count > TEAM:
        pairs = [(source, source + TEAM) for source in range(tm_count - TEAM)]
        held += [lax.ppermute(piece, "tm", pairs) for piece in held]
        before = TEAM
    count = len(held)

    sums = pl.pallas_call(
        functools.partial(stack_kernel, before, count),
        out_shape=[
            jax.ShapeDtypeStruct((keep, band, LAGS), jnp.float32 if step == 0 else jnp.bfloat16) for step in range(LEVELS)
        ],
        in_specs=[vmem()] + [pl.BlockSpec(memory_space=pl.ANY)] * count,
        out_specs=[vmem()] * LEVELS,
        scratch_shapes=[
            pltpu.VMEM(((before + TEAM) * windows, 2, part * chan_count, freq), jnp.bfloat16),
            pltpu.SemaphoreType.DMA((count,)),
        ],
        compiler_params=params,
        name="stack",
    )(lag_table(freq, LAGS), *held)
    total = sums[0]
    for step in range(1, LEVELS):
        total = total + flip(sums[step], "tm", tm_count, step * SIDES).astype(jnp.float32)
    return total * (1.0 / channels)


def solution(mesh):
    placed = (P(("arrays", "tm"), "chan", None, None), P(("arrays", "tm")), P(("arrays", "chan")))
    return jax.shard_map(
        shards,
        mesh=mesh,
        in_specs=placed,
        out_specs=P(("arrays", "tm", "chan"), None, None),
        check_vma=False,
    )
```

time: 235 us -> 56.3 us (0.24)
  the two profiles are of different devices: /device:TPU:0 before, /device:TPU:6 now
where the time goes in v1:
time: 56.3 us; the launch traced here: 56.2 us
  waiting for transfers between devices  21 us (37%)
  Pallas kernels  19 us (34%)
  starting transfers between devices  13.3 us (24%)
  local copies, waits for them, and re-layouts  1.72 us (3%)
  other arithmetic  1.09 us (2%)
    ppermute x19, waiting for transfers between devices, flip(): lax.ppermute(value, axis, [(source, source ^ bits) for source in range(si...  21 us
    pallas_call x1, Pallas kernels, shards(): pl.pallas_call(functools.partial(stack_kernel, before, count), out_shape=...  17.8 us
    ppermute x19, starting transfers between devices, flip(): lax.ppermute(value, axis, [(source, source ^ bits) for source in range(si...  13.3 us
    unnamed x6, local copies, waits for them, and re-layouts  1.72 us
  transfers between devices with their start and end apart: 19, of which 9 were waited for; matrix products, arithmetic and copies ran while one was open for 1% of the time, Pallas kernels for 0%

profile of v1, /device:TPU:6, one launch (start us, length us, event | category | flops | bytes accessed | tf_op | source)
XLA Modules:
  0.0 56.2 jit_solution(14768325664401500373)
XLA Ops:
  0.0 0.7 %copy-done.1 = s32[128]{0:T(128)S(1)} copy-done((s32[128]{0:T(128)S(1)}, s32[128]{0:T(128)}, u32[]{:S(2)}) %copy-start.1) | copy-done | bytes 536
  0.7 1.0 %copy-done = bf16[8,128,2,128]{3,2,1,0:T(2,128)(2,1)S(1)} copy-done((bf16[8,128,2,128]{3,2,1,0:T(2,128)(2,1)S(1)}, bf16[8,128,2,128]{3,2,1,0:T(2,128)(2,1)}, u32[]{:S(2)}) %copy-start) | copy-done | bytes 524312
  1.7 0.6 %power.1.own_ref = f32[8,128]{1,0:T(8,128)S(1)} custom-call(bf16[8,256,128]{2,1,0:T(8,128)(2,1)S(1)} %bitcast.2, s32[1,128]{1,0:T(1,128)S(1)} %bitcast.4), custom_call_target="tpu_custom_call" | custom-call | tf_op jit(solution)/shard_map/power/pallas_call | solution.py:169
  2.5 1.0 %collective-permute-done.other_ref = f32[8,128]{1,0:T(8,128)S(1)} collective-permute-done((f32[8,128]{1,0:T(8,128)S(1)}, f32[8,128]{1,0:T(8,128)S(1)}, u32[]{:S(2)}, u32[]{:S(2)}) %collective-permute-start) | collective-permute-done | bytes 4128 | tf_op jit(solution)/shard_map/ppermute | solution.py:154
  3.5 0.6 align.1
  4.1 1.6 %collective-permute-start.2 = (bf16[8,2,32,128]{3,2,1,0:T(8,128)(2,1)S(1)}, bf16[8,2,32,128]{3,2,1,0:T(8,128)(2,1)S(1)}, u32[]{:S(2)}, u32[]{:S(2)}) collective-permute-start(bf16[8,2,32,128]{3,2,1,0:T(8,128)(2,1)S(1)} %get-tuple-element.14), channel_id=1, source_target_pairs={{0,4},{2,6},{4,0},{6,2},{8,12},{10,14},{12,8},{14,10},{1,5},{3,7},... | collective-permute-start | bytes 393224 | tf_op jit(solution)/shard_map/ppermute | solution.py:154
  5.7 2.6 %collective-permute-start.4 = (bf16[8,2,32,128]{3,2,1,0:T(8,128)(2,1)S(1)}, bf16[8,2,32,128]{3,2,1,0:T(8,128)(2,1)S(1)}, u32[]{:S(2)}, u32[]{:S(2)}) collective-permute-start(bf16[8,2,32,128]{3,2,1,0:T(8,128)(2,1)S(1)} %get-tuple-element.15), channel_id=1, source_target_pairs={{0,8},{2,10},{4,12},{6,14},{8,0},{10,2},{12,4},{14,6},{1,9},{3,11}... | collective-permute-start | bytes 393224 | tf_op jit(solution)/shard_map/ppermute | solution.py:154
  8.5 0.5 collective-permute-start.8
  9.0 2.6 %collective-permute-done.2.refs_3_ = bf16[8,2,32,128]{3,2,1,0:T(8,128)(2,1)S(1)} collective-permute-done((bf16[8,2,32,128]{3,2,1,0:T(8,128)(2,1)S(1)}, bf16[8,2,32,128]{3,2,1,0:T(8,128)(2,1)S(1)}, u32[]{:S(2)}, u32[]{:S(2)}) %collective-permute-start.2) | collective-permute-done | bytes 131104 | tf_op jit(solution)/shard_map/ppermute | solution.py:154
  11.7 0.5 collective-permute-start.10
  12.2 6.4 %collective-permute-done.4.refs_5_ = bf16[8,2,32,128]{3,2,1,0:T(8,128)(2,1)S(1)} collective-permute-done((bf16[8,2,32,128]{3,2,1,0:T(8,128)(2,1)S(1)}, bf16[8,2,32,128]{3,2,1,0:T(8,128)(2,1)S(1)}, u32[]{:S(2)}, u32[]{:S(2)}) %collective-permute-start.4) | collective-permute-done | bytes 131104 | tf_op jit(solution)/shard_map/ppermute | solution.py:154
  18.6 0.5 collective-permute-start.12
  19.4 1.5 %collective-permute-start.14 = (bf16[8,2,32,128]{3,2,1,0:T(8,128)(2,1)S(1)}, bf16[8,2,32,128]{3,2,1,0:T(8,128)(2,1)S(1)}, u32[]{:S(2)}, u32[]{:S(2)}) collective-permute-start(bf16[8,2,32,128]{3,2,1,0:T(8,128)(2,1)S(1)} %collective-permute-done.6.refs_7_), channel_id=1, source_target_pairs={{0,2},{2,0},{4,6},{6,4},{8,10},{10,8},{12,14},{14,12},{1,3},{3,1},... | collective-permute-start | bytes 393224 | tf_op jit(solution)/shard_map/ppermute | solution.py:154
  21.4 3.5 %collective-permute-done.12.refs_13_ = bf16[8,2,32,128]{3,2,1,0:T(8,128)(2,1)S(1)} collective-permute-done((bf16[8,2,32,128]{3,2,1,0:T(8,128)(2,1)S(1)}, bf16[8,2,32,128]{3,2,1,0:T(8,128)(2,1)S(1)}, u32[]{:S(2)}, u32[]{:S(2)}) %collective-permute-start.12) | collective-permute-done | bytes 131104 | tf_op jit(solution)/shard_map/ppermute | solution.py:154
  24.9 0.5 collective-permute-start.13
  25.4 1.9 %collective-permute-done.14.refs_15_ = bf16[8,2,32,128]{3,2,1,0:T(8,128)(2,1)S(1)} collective-permute-done((bf16[8,2,32,128]{3,2,1,0:T(8,128)(2,1)S(1)}, bf16[8,2,32,128]{3,2,1,0:T(8,128)(2,1)S(1)}, u32[]{:S(2)}, u32[]{:S(2)}) %collective-permute-start.14) | collective-permute-done | bytes 131104 | tf_op jit(solution)/shard_map/ppermute | solution.py:154
  27.7 1.0 %collective-permute-done.15.refs_16_ = bf16[8,2,32,128]{3,2,1,0:T(8,128)(2,1)S(1)} collective-permute-done((bf16[8,2,32,128]{3,2,1,0:T(8,128)(2,1)S(1)}, bf16[8,2,32,128]{3,2,1,0:T(8,128)(2,1)S(1)}, u32[]{:S(2)}, u32[]{:S(2)}) %collective-permute-start.15) | collective-permute-done | bytes 131104 | tf_op jit(solution)/shard_map/ppermute | solution.py:154
  28.7 17.8 %stack.7 = (f32[4,48,128]{2,1,0:T(8,128)S(1)}, bf16[4,48,128]{2,1,0:T(8,128)(2,1)S(1)}, bf16[4,48,128]{2,1,0:T(8,128)(2,1)S(1)}, bf16[4,48,128]{2,1,0:T(8,128)(2,1)S(1)}) custom-call(bf16[256,128]{1,0:T(8,128)(2,1)S(1)} %pad_maximum_fusion.refs_0_, bf16[8,2,32,128]{3,2,1,0:T(8,128)(2,1)S(1)} %get-tuple-element.13.refs_1_, ...), custom_call_target="tpu_custom_call" | custom-call | tf_op jit(solution)/shard_map/stack/pallas_call | solution.py:212
  46.5 1.4 %collective-permute-start.16 = (bf16[4,48,128]{2,1,0:T(8,128)(2,1)S(1)}, bf16[4,48,128]{2,1,0:T(8,128)(2,1)S(1)}, u32[]{:S(2)}, u32[]{:S(2)}) collective-permute-start(bf16[4,48,128]{2,1,0:T(8,128)(2,1)S(1)} %get-tuple-element.18), channel_id=1, source_target_pairs={{0,4},{2,6},{4,0},{6,2},{8,12},{10,14},{12,8},{14,10},{1,5},{3,7},... | collective-permute-start | bytes 147464 | tf_op jit(solution)/shard_map/ppermute | solution.py:154
  47.9 1.6 %collective-permute-start.17 = (bf16[4,48,128]{2,1,0:T(8,128)(2,1)S(1)}, bf16[4,48,128]{2,1,0:T(8,128)(2,1)S(1)}, u32[]{:S(2)}, u32[]{:S(2)}) collective-permute-start(bf16[4,48,128]{2,1,0:T(8,128)(2,1)S(1)} %get-tuple-element.19), channel_id=1, source_target_pairs={{0,8},{2,10},{4,12},{6,14},{8,0},{10,2},{12,4},{14,6},{1,9},{3,11}... | collective-permute-start | bytes 147464 | tf_op jit(solution)/shard_map/ppermute | solution.py:154
  49.6 1.4 %collective-permute-start.18 = (bf16[4,48,128]{2,1,0:T(8,128)(2,1)S(1)}, bf16[4,48,128]{2,1,0:T(8,128)(2,1)S(1)}, u32[]{:S(2)}, u32[]{:S(2)}) collective-permute-start(bf16[4,48,128]{2,1,0:T(8,128)(2,1)S(1)} %get-tuple-element.20), channel_id=1, source_target_pairs={{0,12},{2,14},{4,8},{6,10},{8,4},{10,6},{12,0},{14,2},{1,13},{3,15... | collective-permute-start | bytes 147464 | tf_op jit(solution)/shard_map/ppermute | solution.py:154
  51.1 3.1 %collective-permute-done.17 = bf16[4,48,128]{2,1,0:T(8,128)(2,1)S(1)} collective-permute-done((bf16[4,48,128]{2,1,0:T(8,128)(2,1)S(1)}, bf16[4,48,128]{2,1,0:T(8,128)(2,1)S(1)}, u32[]{:S(2)}, u32[]{:S(2)}) %collective-permute-start.17) | collective-permute-done | bytes 49184 | tf_op jit(solution)/shard_map/ppermute | solution.py:154
  54.2 1.3 %collective-permute-done.18 = bf16[4,48,128]{2,1,0:T(8,128)(2,1)S(1)} collective-permute-done((bf16[4,48,128]{2,1,0:T(8,128)(2,1)S(1)}, bf16[4,48,128]{2,1,0:T(8,128)(2,1)S(1)}, u32[]{:S(2)}, u32[]{:S(2)}) %collective-permute-start.18) | collective-permute-done | bytes 49184 | tf_op jit(solution)/shard_map/ppermute | solution.py:154
  55.5 0.7 %add_multiply_fusion = f32[4,48,128]{2,1,0:T(8,128)} fusion(bf16[4,48,128]{2,1,0:T(8,128)(2,1)S(1)} %collective-permute-done.18, bf16[4,48,128]{2,1,0:T(8,128)(2,1)S(1)} %collective-permute-done.17, f32[4,48,128]{2,1,0:T(8,128)S(1)} %get-tuple-element.17, bf16[4,48,128]{2,1,0:T(8,128)(2,1)S(1)} %collective-permute-done.16), kind=kLoop, calls=%fused_computation | loop fusion | flops 172032 | bytes 344064 | tf_op jit(solution)/shard_map/mul | solution.py:229
  (29 shorter events, 1.6 us)
Async XLA Ops:
  0.0 0.7 %copy-start.1 = (s32[128]{0:T(128)S(1)}, s32[128]{0:T(128)}, u32[]{:S(2)}) copy-start(s32[128]{0:T(128)} %param.5) | copy-start | bytes 1540
  0.7 1.0 %copy-start = (bf16[8,128,2,128]{3,2,1,0:T(2,128)(2,1)S(1)}, bf16[8,128,2,128]{3,2,1,0:T(2,128)(2,1)}, u32[]{:S(2)}) copy-start(bf16[8,128,2,128]{3,2,1,0:T(2,128)(2,1)} %param.3) | copy-start | bytes 1572868
  1.7 0.7 %copy-start.2 = (s32[8]{0:T(128)S(1)}, s32[8]{0:T(128)}, u32[]{:S(2)}) copy-start(s32[8]{0:T(128)} %param.4) | copy-start | bytes 100
  2.3 1.2 %collective-permute-start = (f32[8,128]{1,0:T(8,128)S(1)}, f32[8,128]{1,0:T(8,128)S(1)}, u32[]{:S(2)}, u32[]{:S(2)}) collective-permute-start(f32[8,128]{1,0:T(8,128)S(1)} %power.1.own_ref), channel_id=1, source_target_pairs={{0,1},{1,0},{2,3},{3,2},{4,5},{5,4},{6,7},{7,6},{8,9},{9,8},{10,11... | collective-permute-start | bytes 12296 | tf_op jit(solution)/shard_map/ppermute | solution.py:154
  4.1 7.6 %collective-permute-start.2 = (bf16[8,2,32,128]{3,2,1,0:T(8,128)(2,1)S(1)}, bf16[8,2,32,128]{3,2,1,0:T(8,128)(2,1)S(1)}, u32[]{:S(2)}, u32[]{:S(2)}) collective-permute-start(bf16[8,2,32,128]{3,2,1,0:T(8,128)(2,1)S(1)} %get-tuple-element.14), channel_id=1, source_target_pairs={{0,4},{2,6},{4,0},{6,2},{8,12},{10,14},{12,8},{14,10},{1,5},{3,7},... | collective-permute-start | bytes 393224 | tf_op jit(solution)/shard_map/ppermute | solution.py:154
  5.7 12.9 %collective-permute-start.4 = (bf16[8,2,32,128]{3,2,1,0:T(8,128)(2,1)S(1)}, bf16[8,2,32,128]{3,2,1,0:T(8,128)(2,1)S(1)}, u32[]{:S(2)}, u32[]{:S(2)}) collective-permute-start(bf16[8,2,32,128]{3,2,1,0:T(8,128)(2,1)S(1)} %get-tuple-element.15), channel_id=1, source_target_pairs={{0,8},{2,10},{4,12},{6,14},{8,0},{10,2},{12,4},{14,6},{1,9},{3,11}... | collective-permute-start | bytes 393224 | tf_op jit(solution)/shard_map/ppermute | solution.py:154
  8.3 10.3 %collective-permute-start.6 = (bf16[8,2,32,128]{3,2,1,0:T(8,128)(2,1)S(1)}, bf16[8,2,32,128]{3,2,1,0:T(8,128)(2,1)S(1)}, u32[]{:S(2)}, u32[]{:S(2)}) collective-permute-start(bf16[8,2,32,128]{3,2,1,0:T(8,128)(2,1)S(1)} %get-tuple-element.16), channel_id=1, source_target_pairs={{0,12},{2,14},{4,8},{6,10},{8,4},{10,6},{12,0},{14,2},{1,13},{3,15... | collective-permute-start | bytes 393224 | tf_op jit(solution)/shard_map/ppermute | solution.py:154
  8.5 10.6 %collective-permute-start.8 = (bf16[8,2,32,128]{3,2,1,0:T(8,128)(2,1)S(1)}, bf16[8,2,32,128]{3,2,1,0:T(8,128)(2,1)S(1)}, u32[]{:S(2)}, u32[]{:S(2)}) collective-permute-start(bf16[8,2,32,128]{3,2,1,0:T(8,128)(2,1)S(1)} %get-tuple-element.13.refs_1_), channel_id=1, source_target_pairs={{0,2},{2,0},{4,6},{6,4},{8,10},{10,8},{12,14},{14,12},{1,3},{3,1},... | collective-permute-start | bytes 393224 | tf_op jit(solution)/shard_map/ppermute | solution.py:154
  9.0 10.3 %collective-permute-start.1 = (bf16[8,2,32,128]{3,2,1,0:T(8,128)(2,1)S(1)}, bf16[8,2,32,128]{3,2,1,0:T(8,128)(2,1)S(1)}, u32[]{:S(2)}, u32[]{:S(2)}) collective-permute-start(bf16[8,2,32,128]{3,2,1,0:T(8,128)(2,1)S(1)} %get-tuple-element.13.refs_1_), channel_id=1, source_target_pairs={{0,1},{1,0},{2,3},{3,2},{4,5},{5,4},{6,7},{7,6},{8,9},{9,8},{10,11... | collective-permute-start | bytes 393224 | tf_op jit(solution)/shard_map/ppermute | solution.py:154
  11.7 9.2 %collective-permute-start.10 = (bf16[8,2,32,128]{3,2,1,0:T(8,128)(2,1)S(1)}, bf16[8,2,32,128]{3,2,1,0:T(8,128)(2,1)S(1)}, u32[]{:S(2)}, u32[]{:S(2)}) collective-permute-start(bf16[8,2,32,128]{3,2,1,0:T(8,128)(2,1)S(1)} %collective-permute-done.2.refs_3_), channel_id=1, source_target_pairs={{0,2},{2,0},{4,6},{6,4},{8,10},{10,8},{12,14},{14,12},{1,3},{3,1},... | collective-permute-start | bytes 393224 | tf_op jit(solution)/shard_map/ppermute | solution.py:154
  18.6 2.3 %collective-permute-start.3 = (bf16[8,2,32,128]{3,2,1,0:T(8,128)(2,1)S(1)}, bf16[8,2,32,128]{3,2,1,0:T(8,128)(2,1)S(1)}, u32[]{:S(2)}, u32[]{:S(2)}) collective-permute-start(bf16[8,2,32,128]{3,2,1,0:T(8,128)(2,1)S(1)} %collective-permute-done.2.refs_3_), channel_id=1, source_target_pairs={{0,1},{1,0},{2,3},{3,2},{4,5},{5,4},{6,7},{7,6},{8,9},{9,8},{10,11... | collective-permute-start | bytes 393224 | tf_op jit(solution)/shard_map/ppermute | solution.py:154
  18.6 6.3 %collective-permute-start.12 = (bf16[8,2,32,128]{3,2,1,0:T(8,128)(2,1)S(1)}, bf16[8,2,32,128]{3,2,1,0:T(8,128)(2,1)S(1)}, u32[]{:S(2)}, u32[]{:S(2)}) collective-permute-start(bf16[8,2,32,128]{3,2,1,0:T(8,128)(2,1)S(1)} %collective-permute-done.4.refs_5_), channel_id=1, source_target_pairs={{0,2},{2,0},{4,6},{6,4},{8,10},{10,8},{12,14},{14,12},{1,3},{3,1},... | collective-permute-start | bytes 393224 | tf_op jit(solution)/shard_map/ppermute | solution.py:154
  19.1 5.8 %collective-permute-start.5 = (bf16[8,2,32,128]{3,2,1,0:T(8,128)(2,1)S(1)}, bf16[8,2,32,128]{3,2,1,0:T(8,128)(2,1)S(1)}, u32[]{:S(2)}, u32[]{:S(2)}) collective-permute-start(bf16[8,2,32,128]{3,2,1,0:T(8,128)(2,1)S(1)} %collective-permute-done.4.refs_5_), channel_id=1, source_target_pairs={{0,1},{1,0},{2,3},{3,2},{4,5},{5,4},{6,7},{7,6},{8,9},{9,8},{10,11... | collective-permute-start | bytes 393224 | tf_op jit(solution)/shard_map/ppermute | solution.py:154
  19.4 7.9 %collective-permute-start.14 = (bf16[8,2,32,128]{3,2,1,0:T(8,128)(2,1)S(1)}, bf16[8,2,32,128]{3,2,1,0:T(8,128)(2,1)S(1)}, u32[]{:S(2)}, u32[]{:S(2)}) collective-permute-start(bf16[8,2,32,128]{3,2,1,0:T(8,128)(2,1)S(1)} %collective-permute-done.6.refs_7_), channel_id=1, source_target_pairs={{0,2},{2,0},{4,6},{6,4},{8,10},{10,8},{12,14},{14,12},{1,3},{3,1},... | collective-permute-start | bytes 393224 | tf_op jit(solution)/shard_map/ppermute | solution.py:154
  20.9 6.8 %collective-permute-start.7 = (bf16[8,2,32,128]{3,2,1,0:T(8,128)(2,1)S(1)}, bf16[8,2,32,128]{3,2,1,0:T(8,128)(2,1)S(1)}, u32[]{:S(2)}, u32[]{:S(2)}) collective-permute-start(bf16[8,2,32,128]{3,2,1,0:T(8,128)(2,1)S(1)} %collective-permute-done.6.refs_7_), channel_id=1, source_target_pairs={{0,1},{1,0},{2,3},{3,2},{4,5},{5,4},{6,7},{7,6},{8,9},{9,8},{10,11... | collective-permute-start | bytes 393224 | tf_op jit(solution)/shard_map/ppermute | solution.py:154
  20.9 6.8 %collective-permute-start.9 = (bf16[8,2,32,128]{3,2,1,0:T(8,128)(2,1)S(1)}, bf16[8,2,32,128]{3,2,1,0:T(8,128)(2,1)S(1)}, u32[]{:S(2)}, u32[]{:S(2)}) collective-permute-start(bf16[8,2,32,128]{3,2,1,0:T(8,128)(2,1)S(1)} %collective-permute-done.8.refs_9_), channel_id=1, source_target_pairs={{0,1},{1,0},{2,3},{3,2},{4,5},{5,4},{6,7},{7,6},{8,9},{9,8},{10,11... | collective-permute-start | bytes 393224 | tf_op jit(solution)/shard_map/ppermute | solution.py:154
  24.9 2.8 %collective-permute-start.11 = (bf16[8,2,32,128]{3,2,1,0:T(8,128)(2,1)S(1)}, bf16[8,2,32,128]{3,2,1,0:T(8,128)(2,1)S(1)}, u32[]{:S(2)}, u32[]{:S(2)}) collective-permute-start(bf16[8,2,32,128]{3,2,1,0:T(8,128)(2,1)S(1)} %collective-permute-done.10.refs_11_), channel_id=1, source_target_pairs={{0,1},{1,0},{2,3},{3,2},{4,5},{5,4},{6,7},{7,6},{8,9},{9,8},{10,11... | collective-permute-start | bytes 393224 | tf_op jit(solution)/shard_map/ppermute | solution.py:154
  24.9 2.8 %collective-permute-start.13 = (bf16[8,2,32,128]{3,2,1,0:T(8,128)(2,1)S(1)}, bf16[8,2,32,128]{3,2,1,0:T(8,128)(2,1)S(1)}, u32[]{:S(2)}, u32[]{:S(2)}) collective-permute-start(bf16[8,2,32,128]{3,2,1,0:T(8,128)(2,1)S(1)} %collective-permute-done.12.refs_13_), channel_id=1, source_target_pairs={{0,1},{1,0},{2,3},{3,2},{4,5},{5,4},{6,7},{7,6},{8,9},{9,8},{10,11... | collective-permute-start | bytes 393224 | tf_op jit(solution)/shard_map/ppermute | solution.py:154
  27.3 1.3 %collective-permute-start.15 = (bf16[8,2,32,128]{3,2,1,0:T(8,128)(2,1)S(1)}, bf16[8,2,32,128]{3,2,1,0:T(8,128)(2,1)S(1)}, u32[]{:S(2)}, u32[]{:S(2)}) collective-permute-start(bf16[8,2,32,128]{3,2,1,0:T(8,128)(2,1)S(1)} %collective-permute-done.14.refs_15_), channel_id=1, source_target_pairs={{0,1},{1,0},{2,3},{3,2},{4,5},{5,4},{6,7},{7,6},{8,9},{9,8},{10,11... | collective-permute-start | bytes 393224 | tf_op jit(solution)/shard_map/ppermute | solution.py:154
  46.5 4.6 %collective-permute-start.16 = (bf16[4,48,128]{2,1,0:T(8,128)(2,1)S(1)}, bf16[4,48,128]{2,1,0:T(8,128)(2,1)S(1)}, u32[]{:S(2)}, u32[]{:S(2)}) collective-permute-start(bf16[4,48,128]{2,1,0:T(8,128)(2,1)S(1)} %get-tuple-element.18), channel_id=1, source_target_pairs={{0,4},{2,6},{4,0},{6,2},{8,12},{10,14},{12,8},{14,10},{1,5},{3,7},... | collective-permute-start | bytes 147464 | tf_op jit(solution)/shard_map/ppermute | solution.py:154
  47.9 6.3 %collective-permute-start.17 = (bf16[4,48,128]{2,1,0:T(8,128)(2,1)S(1)}, bf16[4,48,128]{2,1,0:T(8,128)(2,1)S(1)}, u32[]{:S(2)}, u32[]{:S(2)}) collective-permute-start(bf16[4,48,128]{2,1,0:T(8,128)(2,1)S(1)} %get-tuple-element.19), channel_id=1, source_target_pairs={{0,8},{2,10},{4,12},{6,14},{8,0},{10,2},{12,4},{14,6},{1,9},{3,11}... | collective-permute-start | bytes 147464 | tf_op jit(solution)/shard_map/ppermute | solution.py:154
  49.6 5.9 %collective-permute-start.18 = (bf16[4,48,128]{2,1,0:T(8,128)(2,1)S(1)}, bf16[4,48,128]{2,1,0:T(8,128)(2,1)S(1)}, u32[]{:S(2)}, u32[]{:S(2)}) collective-permute-start(bf16[4,48,128]{2,1,0:T(8,128)(2,1)S(1)} %get-tuple-element.20), channel_id=1, source_target_pairs={{0,12},{2,14},{4,8},{6,10},{8,4},{10,6},{12,0},{14,2},{1,13},{3,15... | collective-permute-start | bytes 147464 | tf_op jit(solution)/shard_map/ppermute | solution.py:154

commit v2 on v1

v2 whole, which is shorter than its diff:
```python
import functools
import math

import jax
import jax.numpy as jnp
from jax import lax
from jax.experimental import pallas as pl
from jax.experimental.pallas import tpu as pltpu
from jax.sharding import PartitionSpec as P

LAGS = 128
GROUPS = 8
SPAN = 6
SIDES = 2
LEVELS = 4
TEAM = SIDES * LEVELS
EARLY = (("near", 2), ("far", 0), ("near", 3), ("near", 1), ("far", 1))
LATE = (2, 3)
OUT_ORDER = (2, 3, 1)

epsilon = 1e-05

HIGHEST = lax.Precision.HIGHEST


def lag_table(freq_bins, lag_count):
    frequency = jnp.arange(freq_bins, dtype=jnp.int32)[:, None]
    lag_shift = jnp.arange(lag_count, dtype=jnp.int32)[None, :] - lag_count // 2
    phase_turns = jnp.mod(frequency * lag_shift, 2 * freq_bins).astype(jnp.float32)
    phase_angle = jnp.pi * phase_turns / freq_bins
    normaliser = 1.0 / math.sqrt(freq_bins)
    lag_rows = jnp.concatenate(
        [jnp.cos(phase_angle) * normaliser, -jnp.sin(phase_angle) * normaliser], axis=0
    )
    return lag_rows.astype(jnp.bfloat16)


def phases(offsets, freq_bins):
    frequency = jnp.arange(freq_bins, dtype=jnp.int32)[None, :]
    phase_turns = jnp.mod(offsets[:, None] * frequency, 2 * freq_bins).astype(jnp.float32)
    phase_angle = jnp.pi * phase_turns / freq_bins
    return jnp.stack([jnp.cos(phase_angle), jnp.sin(phase_angle)])


def power_kernel(spectra_ref, member_ref, power_ref, rows_ref):
    windows, rows, _ = spectra_ref.shape
    half = rows // 2
    lane = lax.broadcasted_iota(jnp.int32, power_ref.shape, 1)
    power = jnp.zeros(power_ref.shape, jnp.float32)
    for window in range(windows):
        value = spectra_ref[window].astype(jnp.float32)
        rows_ref[window] = value * value
        squares = rows_ref[window, pl.ds(0, half, stride=2), :] + rows_ref[window, pl.ds(1, half, stride=2), :]
        grouped = jnp.dot(member_ref[...], squares, precision=HIGHEST, preferred_element_type=jnp.float32)
        power = jnp.where(lane == window, jnp.sum(grouped, axis=1, keepdims=True), power)
    power_ref[...] = power


def align_kernel(scale_of_energy, spectra_ref, member_ref, own_ref, other_ref, phase_ref, *rest):
    pieces, (rows_ref, scale_ref) = rest[:LEVELS], rest[LEVELS:]
    windows, rows, _ = spectra_ref.shape
    part = rows // 2 // LEVELS
    level = lax.rem(lax.axis_index("tm"), TEAM) // SIDES
    energy = (own_ref[...] + other_ref[...]) * scale_of_energy
    scale_ref[...] = lax.dot_general(
        member_ref[...], lax.rsqrt(energy + epsilon), (((0,), (0,)), ((), ())),
        precision=HIGHEST, preferred_element_type=jnp.float32,
    )
    for window in range(windows):
        rows_ref[window] = spectra_ref[window].astype(jnp.float32)
    for step in range(LEVELS):
        first = pl.multiple_of((level ^ step) * part, part)
        weights = scale_ref[pl.ds(first, part), :]
        for window in range(windows):
            cosine = phase_ref[0, window : window + 1, :]
            sine = phase_ref[1, window : window + 1, :]
            real = rows_ref[window, pl.ds(2 * first, part, stride=2), :]
            imag = rows_ref[window, pl.ds(2 * first + 1, part, stride=2), :]
            weight = weights[:, window : window + 1]
            pieces[step][window, 0] = (weight * (real * cosine + imag * sine)).astype(jnp.bfloat16)
            pieces[step][window, 1] = (weight * (imag * cosine - real * sine)).astype(jnp.bfloat16)


def gather(pieces, held, before):
    windows = pieces[0].shape[0]
    level = lax.rem(lax.axis_index("tm"), TEAM) // SIDES
    for index, piece in enumerate(pieces):
        block = (level ^ (index % LEVELS)) + (before if index < LEVELS else 0)
        held[pl.ds(block * windows, windows)] = piece[...]


def band_sums(left_real, left_imag, right_real, right_imag, table):
    real = left_real[None] * right_real + left_imag[None] * right_imag
    imag = left_imag[None] * right_real - left_real[None] * right_imag
    count, part, freq = real.shape
    cross = jnp.concatenate([real.reshape(count * part, freq), imag.reshape(count * part, freq)], axis=1)
    lagged = jnp.dot(cross, table, preferred_element_type=jnp.float32)
    return jnp.sum((lagged * lagged).reshape(count, part, table.shape[1]), axis=1)


def block_sums(left, left_at, right, right_at, windows, table, store):
    right_real, right_imag = right[pl.ds(right_at, windows), 0], right[pl.ds(right_at, windows), 1]
    for window in range(windows):
        store(window, band_sums(left[left_at + window, 0], left[left_at + window, 1], right_real, right_imag, table))


def level_of(pair, firsts):
    level = jnp.int32(0)
    for first in firsts[1:]:
        level += (pair >= first).astype(jnp.int32)
    start = jnp.int32(0)
    for index, first in enumerate(firsts):
        start = jnp.where(level == index, first, start)
    return level, pair - start


def sweep(counts, unroll, visit):
    firsts = [sum(counts[:index]) for index in range(len(counts))]
    pairs = sum(counts)
    assert pairs % unroll == 0

    def turn(index, carry):
        for inner in range(unroll):
            visit(*level_of(index * unroll + inner, firsts))
        return carry

    lax.fori_loop(0, pairs // unroll, turn, 0)


def near_kernel(teams, count, *refs):
    table_ref, pieces, (sums_ref, held) = refs[0], refs[1 : 1 + count], refs[1 + count :]
    windows = pieces[0].shape[0]
    before = LEVELS if teams else 0
    gather(pieces, held, before)
    table = table_ref[...]
    counts = [LEVELS if teams else level + 1 for level in range(LEVELS)]
    for level in range(LEVELS):
        skipped = (LEVELS - counts[level]) * windows
        if skipped:
            sums_ref[level, :, :skipped, :] = jnp.zeros((windows, skipped, sums_ref.shape[3]), jnp.float32)

    def visit(level, back):
        place = pl.multiple_of((LEVELS - 1 - back) * windows, windows)

        def store(window, sums):
            sums_ref[level, window, pl.ds(place, windows), :] = sums

        block_sums(held, (before + level) * windows, held, (before + level - back) * windows, windows, table, store)

    sweep(counts, 2, visit)


def far_kernel(teams, count, *refs):
    table_ref, near_ref, pieces = refs[0], refs[1], refs[2 : 2 + 2 * count]
    mine_ref, other_ref, held, across, grid = refs[2 + 2 * count :]
    windows = pieces[0].shape[0]
    side = lax.rem(lax.axis_index("tm"), SIDES)
    core = lax.axis_index("chan")
    before = LEVELS if teams else 0
    margin = LEVELS if teams else 1
    gather(pieces[:count], held, before)
    gather(pieces[count:], across, margin)
    if not teams:
        across[pl.ds(0, windows)] = jnp.zeros((windows,) + across.shape[1:], across.dtype)
    table = table_ref[...]
    band = mine_ref.shape[2]
    keep = mine_ref.shape[1]
    reach = LEVELS - 1
    counts = [reach if teams else min(reach, level + 1) for level in range(LEVELS)]
    for level in range(LEVELS):
        for block in range(reach - counts[level]):
            grid[level, :, (2 * block + 1) * windows : (2 * block + 2) * windows, :] = jnp.zeros(
                (windows, windows, grid.shape[3]), jnp.float32
            )

    def visit(level, back):
        place = pl.multiple_of((2 * (reach - 1 - back) + 1) * windows, windows)

        def store(window, sums):
            grid[level, window, pl.ds(place, windows), :] = sums

        right = (margin + level + side - 1 - back) * windows
        block_sums(held, (before + level) * windows, across, right, windows, table, store)

    sweep(counts, 3, visit)

    def finish(level, carry):
        for block in range(LEVELS):
            grid[level, :, 2 * block * windows : (2 * block + 1) * windows, :] = near_ref[
                level, :, block * windows : (block + 1) * windows, :
            ]
        for inner in range(keep):
            window = core * keep + inner
            mine_ref[level, inner] = grid[level, window, pl.ds(window, band), :]
            window = (1 - core) * keep + inner
            other_ref[level, inner] = grid[level, window, pl.ds(window, band), :].astype(other_ref.dtype)
        return carry

    lax.fori_loop(0, LEVELS, finish, 0)


def merge_kernel(mine_ref, other_ref, *outs):
    level = lax.rem(lax.axis_index("tm"), TEAM) // SIDES
    for step, out in enumerate(outs):
        at = level ^ step
        out[...] = (mine_ref[at] + other_ref[at].astype(jnp.float32)).astype(out.dtype)


def vmem():
    return pl.BlockSpec(memory_space=pltpu.VMEM)


def flip(value, axis, size, bits):
    return lax.ppermute(value, axis, [(source, source ^ bits) for source in range(size)])


def shards(spectra, offsets, channel_group):
    windows, local_chans, _, freq = spectra.shape
    chan_count = lax.axis_size("chan")
    tm_count = lax.axis_size("tm")
    channels = local_chans * chan_count
    part = local_chans // LEVELS
    band = SPAN * windows
    keep = windows // chan_count
    params = pltpu.CompilerParams(vmem_limit_bytes=40 * 1024 * 1024)

    rows = spectra.reshape(windows, 2 * local_chans, freq)
    member = (channel_group[None, :] == jnp.arange(GROUPS, dtype=jnp.int32)[:, None]).astype(jnp.float32)
    power = pl.pallas_call(
        power_kernel,
        out_shape=jax.ShapeDtypeStruct((GROUPS, 128), jnp.float32),
        in_specs=[vmem()] * 2,
        out_specs=vmem(),
        scratch_shapes=[pltpu.VMEM((windows, 2 * local_chans, freq), jnp.float32)],
        compiler_params=params,
        name="power",
    )(rows, member)
    other_power = flip(power, "chan", chan_count, 1)
    piece_shape = jax.ShapeDtypeStruct((windows, 2, part, freq), jnp.bfloat16)
    own = pl.pallas_call(
        functools.partial(align_kernel, GROUPS / (freq * channels)),
        out_shape=[piece_shape] * LEVELS,
        in_specs=[vmem()] * 5,
        out_specs=[vmem()] * LEVELS,
        scratch_shapes=[
            pltpu.VMEM((windows, 2 * local_chans, freq), jnp.float32),
            pltpu.VMEM((local_chans, 128), jnp.float32),
        ],
        compiler_params=params,
        name="align",
    )(rows, member, power, other_power, phases(offsets, freq))

    near = [own[0]] + [None] * (LEVELS - 1)
    far = [None] * LEVELS
    for kind, step in EARLY:
        if kind == "near":
            near[step] = flip(own[step], "tm", tm_count, step * SIDES)
        else:
            far[step] = flip(own[step], "tm", tm_count, step * SIDES + 1)
    for step in LATE:
        far[step] = flip(near[step], "tm", tm_count, 1)
    teams = tm_count > TEAM
    if teams:
        pairs = [(source, source + TEAM) for source in range(tm_count - TEAM)]
        near += [lax.ppermute(piece, "tm", pairs) for piece in near]
        far += [lax.ppermute(piece, "tm", pairs) for piece in far]
    count = len(near)
    held_blocks = count
    across_blocks = count if teams else count + 1
    table = lag_table(freq, LAGS)

    near_sums = pl.pallas_call(
        functools.partial(near_kernel, teams, count),
        out_shape=jax.ShapeDtypeStruct((LEVELS, windows, LEVELS * windows, LAGS), jnp.float32),
        in_specs=[vmem()] * (1 + count),
        out_specs=vmem(),
        scratch_shapes=[
            pltpu.VMEM((held_blocks * windows, 2, part, freq), jnp.bfloat16),
        ],
        compiler_params=params,
        cost_estimate=pl.CostEstimate(flops=2000000000, bytes_accessed=2000000, transcendentals=0),
        name="near",
    )(table, *near)
    sums_shape = (LEVELS, keep, band, LAGS)
    mine, other = pl.pallas_call(
        functools.partial(far_kernel, teams, count),
        out_shape=[
            jax.ShapeDtypeStruct(sums_shape, jnp.float32), jax.ShapeDtypeStruct(sums_shape, jnp.bfloat16)
        ],
        in_specs=[vmem()] * (2 + 2 * count),
        out_specs=[vmem()] * 2,
        scratch_shapes=[
            pltpu.VMEM((held_blocks * windows, 2, part, freq), jnp.bfloat16),
            pltpu.VMEM((across_blocks * windows, 2, part, freq), jnp.bfloat16),
            pltpu.VMEM((LEVELS, windows, (SPAN + 1) * windows, LAGS), jnp.float32),
        ],
        compiler_params=params,
        name="far",
    )(table, near_sums, *near, *far)
    sums = pl.pallas_call(
        merge_kernel,
        out_shape=[
            jax.ShapeDtypeStruct(sums_shape[1:], jnp.float32 if step == 0 else jnp.bfloat16) for step in range(LEVELS)
        ],
        in_specs=[vmem()] * 2,
        out_specs=[vmem()] * LEVELS,
        compiler_params=params,
        name="merge",
    )(mine, flip(other, "chan", chan_count, 1))
    total = sums[0]
    for step in OUT_ORDER:
        total = total + flip(sums[step], "tm", tm_count, step * SIDES).astype(jnp.float32)
    return total * (1.0 / channels)


def solution(mesh):
    placed = (P(("arrays", "tm"), "chan", None, None), P(("arrays", "tm")), P(("arrays", "chan")))
    return jax.shard_map(
        shards,
        mesh=mesh,
        in_specs=placed,
        out_specs=P(("arrays", "tm", "chan"), None, None),
        check_vma=False,
    )
```

time: 56.3 us -> 42.5 us (0.75)
  the two profiles are of different devices: /device:TPU:6 before, /device:TPU:0 now
where the time goes in v2:
time: 42.5 us; the launch traced here: 42.4 us
  starting transfers between devices  15.8 us (37%)
  waiting for transfers between devices  13.8 us (32%)
  Pallas kernels  9.93 us (23%)
  other arithmetic  1.75 us (4%)
  local copies, waits for them, and re-layouts  1.04 us (2%)
    ppermute x12, starting transfers between devices, flip(): lax.ppermute(value, axis, [(source, source ^ bits) for source in range(si...  15.8 us
    ppermute x12, waiting for transfers between devices, flip(): lax.ppermute(value, axis, [(source, source ^ bits) for source in range(si...  13.8 us
    pallas_call x1, Pallas kernels, shards(): pl.pallas_call(functools.partial(near_kernel, teams, count), out_shape=ja...  4.61 us
    pallas_call x1, Pallas kernels, shards(): pl.pallas_call(functools.partial(far_kernel, teams, count), out_shape=[ja...  4.12 us
    unnamed x4, local copies, waits for them, and re-layouts  1.04 us
  transfers between devices with their start and end apart: 12, of which 8 were waited for; matrix products, arithmetic and copies ran while one was open for 1% of the time, Pallas kernels for 11%

profile of v2, /device:TPU:0, one launch (start us, length us, event | category | flops | bytes accessed | tf_op | source)
XLA Modules:
  0.0 42.4 jit_solution(6591347340613704161)
XLA Ops:
  0.0 0.7 %fusion.12.member_ref = f32[8,128]{1,0:T(8,128)S(1)} fusion(s32[128]{0:T(128)} %param.5), kind=kLoop, calls=%fused_computation.24 | loop fusion | flops 2048 | bytes 4608 | tf_op jit(solution)/shard_map/convert_element_type | solution.py:228
  0.7 1.0 %copy-done = bf16[8,128,2,128]{3,2,1,0:T(2,128)(2,1)S(1)} copy-done((bf16[8,128,2,128]{3,2,1,0:T(2,128)(2,1)S(1)}, bf16[8,128,2,128]{3,2,1,0:T(2,128)(2,1)}, u32[]{:S(2)}) %copy-start) | copy-done | bytes 524312
  1.7 0.6 %power.1.own_ref = f32[8,128]{1,0:T(8,128)S(1)} custom-call(bf16[8,256,128]{2,1,0:T(8,128)(2,1)S(1)} %bitcast.1, f32[8,128]{1,0:T(8,128)S(1)} %fusion.12.member_ref), custom_call_target="tpu_custom_call" | custom-call | tf_op jit(solution)/shard_map/power/pallas_call | solution.py:229
  2.3 0.5 %collective-permute-start = (f32[8,128]{1,0:T(8,128)S(1)}, f32[8,128]{1,0:T(8,128)S(1)}, u32[]{:S(2)}, u32[]{:S(2)}) collective-permute-start(f32[8,128]{1,0:T(8,128)S(1)} %power.1.own_ref), channel_id=1, source_target_pairs={{0,1},{1,0},{2,3},{3,2},{4,5},{5,4},{6,7},{7,6},{8,9},{9,8},{10,11... | collective-permute-start | bytes 12296 | tf_op jit(solution)/shard_map/ppermute | solution.py:214
  2.9 0.7 %collective-permute-done.other_ref = f32[8,128]{1,0:T(8,128)S(1)} collective-permute-done((f32[8,128]{1,0:T(8,128)S(1)}, f32[8,128]{1,0:T(8,128)S(1)}, u32[]{:S(2)}, u32[]{:S(2)}) %collective-permute-start) | collective-permute-done | bytes 4128 | tf_op jit(solution)/shard_map/ppermute | solution.py:214
  3.6 0.5 %align.1 = (bf16[8,2,32,128]{3,2,1,0:T(8,128)(2,1)S(1)}, bf16[8,2,32,128]{3,2,1,0:T(8,128)(2,1)S(1)}, bf16[8,2,32,128]{3,2,1,0:T(8,128)(2,1)S(1)}, bf16[8,2,32,128]{3,2,1,0:T(8,128)(2,1)S(1)}) custom-call(bf16[8,256,128]{2,1,0:T(8,128)(2,1)S(1)} %bitcast.2, f32[8,128]{1,0:T(8,128)S(1)} %fusion.12.member_ref, f32[8,128]{1,0:T(8,128)S(1)} %power.1.own_ref, ...), custom_call_target="tpu_custom_call" | custom-call | tf_op jit(solution)/shard_map/align/pallas_call | solution.py:240
  4.2 4.0 %collective-permute-start.2 = (bf16[8,2,32,128]{3,2,1,0:T(8,128)(2,1)S(1)}, bf16[8,2,32,128]{3,2,1,0:T(8,128)(2,1)S(1)}, u32[]{:S(2)}, u32[]{:S(2)}) collective-permute-start(bf16[8,2,32,128]{3,2,1,0:T(8,128)(2,1)S(1)} %get-tuple-element.17), channel_id=1, source_target_pairs={{0,8},{2,10},{4,12},{6,14},{8,0},{10,2},{12,4},{14,6},{1,9},{3,11}... | collective-permute-start | bytes 393224 | tf_op jit(solution)/shard_map/ppermute | solution.py:214
  8.2 1.3 %collective-permute-start.3 = (bf16[8,2,32,128]{3,2,1,0:T(8,128)(2,1)S(1)}, bf16[8,2,32,128]{3,2,1,0:T(8,128)(2,1)S(1)}, u32[]{:S(2)}, u32[]{:S(2)}) collective-permute-start(bf16[8,2,32,128]{3,2,1,0:T(8,128)(2,1)S(1)} %get-tuple-element.18), channel_id=1, source_target_pairs={{0,12},{2,14},{4,8},{6,10},{8,4},{10,6},{12,0},{14,2},{1,13},{3,15... | collective-permute-start | bytes 393224 | tf_op jit(solution)/shard_map/ppermute | solution.py:214
  10.0 2.8 %collective-permute-start.5 = (bf16[8,2,32,128]{3,2,1,0:T(8,128)(2,1)S(1)}, bf16[8,2,32,128]{3,2,1,0:T(8,128)(2,1)S(1)}, u32[]{:S(2)}, u32[]{:S(2)}) collective-permute-start(bf16[8,2,32,128]{3,2,1,0:T(8,128)(2,1)S(1)} %get-tuple-element.16), channel_id=1, source_target_pairs={{0,6},{2,4},{4,2},{6,0},{8,14},{10,12},{12,10},{14,8},{1,7},{3,5},... | collective-permute-start | bytes 393224 | tf_op jit(solution)/shard_map/ppermute | solution.py:214
  12.8 0.5 %collective-permute-start.4 = (bf16[8,2,32,128]{3,2,1,0:T(8,128)(2,1)S(1)}, bf16[8,2,32,128]{3,2,1,0:T(8,128)(2,1)S(1)}, u32[]{:S(2)}, u32[]{:S(2)}) collective-permute-start(bf16[8,2,32,128]{3,2,1,0:T(8,128)(2,1)S(1)} %get-tuple-element.15.refs_1_.refs_2_), channel_id=1, source_target_pairs={{0,2},{2,0},{4,6},{6,4},{8,10},{10,8},{12,14},{14,12},{1,3},{3,1},... | collective-permute-start | bytes 393224 | tf_op jit(solution)/shard_map/ppermute | solution.py:214
  13.4 4.7 %collective-permute-done.2.refs_3_.refs_4_ = bf16[8,2,32,128]{3,2,1,0:T(8,128)(2,1)S(1)} collective-permute-done((bf16[8,2,32,128]{3,2,1,0:T(8,128)(2,1)S(1)}, bf16[8,2,32,128]{3,2,1,0:T(8,128)(2,1)S(1)}, u32[]{:S(2)}, u32[]{:S(2)}) %collective-permute-start.2) | collective-permute-done | bytes 131104 | tf_op jit(solution)/shard_map/ppermute | solution.py:214
  18.1 1.9 %collective-permute-start.6 = (bf16[8,2,32,128]{3,2,1,0:T(8,128)(2,1)S(1)}, bf16[8,2,32,128]{3,2,1,0:T(8,128)(2,1)S(1)}, u32[]{:S(2)}, u32[]{:S(2)}) collective-permute-start(bf16[8,2,32,128]{3,2,1,0:T(8,128)(2,1)S(1)} %collective-permute-done.2.refs_3_.refs_4_), channel_id=1, source_target_pairs={{0,2},{2,0},{4,6},{6,4},{8,10},{10,8},{12,14},{14,12},{1,3},{3,1},... | collective-permute-start | bytes 393224 | tf_op jit(solution)/shard_map/ppermute | solution.py:214
  20.1 4.6 %near.1.refs_1_ = f32[4,8,32,128]{3,2,1,0:T(8,128)S(1)} custom-call(bf16[256,128]{1,0:T(8,128)(2,1)S(1)} %pad_maximum_fusion.refs_0_, bf16[8,2,32,128]{3,2,1,0:T(8,128)(2,1)S(1)} %get-tuple-element.15.refs_1_.refs_2_, bf16[8,2,32,128]{3,2,1,0:T(8,128)(2,1)S(1)} %collective-permute-done.1.refs_2_.refs_3_, ...), custom_call_target="tpu_custom_call" | custom-call | flops 2000000000 | bytes 2000000 | tf_op jit(solution)/shard_map/near/pallas_call | solution.py:272
  24.8 1.0 %collective-permute-done.6.refs_8_ = bf16[8,2,32,128]{3,2,1,0:T(8,128)(2,1)S(1)} collective-permute-done((bf16[8,2,32,128]{3,2,1,0:T(8,128)(2,1)S(1)}, bf16[8,2,32,128]{3,2,1,0:T(8,128)(2,1)S(1)}, u32[]{:S(2)}, u32[]{:S(2)}) %collective-permute-start.6) | collective-permute-done | bytes 131104 | tf_op jit(solution)/shard_map/ppermute | solution.py:214
  25.8 2.1 %collective-permute-done.7.refs_9_ = bf16[8,2,32,128]{3,2,1,0:T(8,128)(2,1)S(1)} collective-permute-done((bf16[8,2,32,128]{3,2,1,0:T(8,128)(2,1)S(1)}, bf16[8,2,32,128]{3,2,1,0:T(8,128)(2,1)S(1)}, u32[]{:S(2)}, u32[]{:S(2)}) %collective-permute-start.7) | collective-permute-done | bytes 131104 | tf_op jit(solution)/shard_map/ppermute | solution.py:214
  27.8 4.1 %far.1 = (f32[4,4,48,128]{3,2,1,0:T(8,128)S(1)}, bf16[4,4,48,128]{3,2,1,0:T(8,128)(2,1)S(1)}) custom-call(bf16[256,128]{1,0:T(8,128)(2,1)S(1)} %pad_maximum_fusion.refs_0_, f32[4,8,32,128]{3,2,1,0:T(8,128)S(1)} %near.1.refs_1_, bf16[8,2,32,128]{3,2,1,0:T(8,128)(2,1)S(1)} %get-tuple-element.15.refs_1_.refs_2_, ...), custom_call_target="tpu_custom_call" | custom-call | tf_op jit(solution)/shard_map/far/pallas_call | solution.py:285
  32.0 1.4 %collective-permute-done.8.other_ref = bf16[4,4,48,128]{3,2,1,0:T(8,128)(2,1)S(1)} collective-permute-done((bf16[4,4,48,128]{3,2,1,0:T(8,128)(2,1)S(1)}, bf16[4,4,48,128]{3,2,1,0:T(8,128)(2,1)S(1)}, u32[]{:S(2)}, u32[]{:S(2)}) %collective-permute-start.8) | collective-permute-done | bytes 196640 | tf_op jit(solution)/shard_map/ppermute | solution.py:214
  33.5 1.5 %collective-permute-start.9 = (bf16[4,48,128]{2,1,0:T(8,128)(2,1)S(1)}, bf16[4,48,128]{2,1,0:T(8,128)(2,1)S(1)}, u32[]{:S(2)}, u32[]{:S(2)}) collective-permute-start(bf16[4,48,128]{2,1,0:T(8,128)(2,1)S(1)} %get-tuple-element.22), channel_id=1, source_target_pairs={{0,8},{2,10},{4,12},{6,14},{8,0},{10,2},{12,4},{14,6},{1,9},{3,11}... | collective-permute-start | bytes 147464 | tf_op jit(solution)/shard_map/ppermute | solution.py:214
  35.0 2.3 %collective-permute-start.10 = (bf16[4,48,128]{2,1,0:T(8,128)(2,1)S(1)}, bf16[4,48,128]{2,1,0:T(8,128)(2,1)S(1)}, u32[]{:S(2)}, u32[]{:S(2)}) collective-permute-start(bf16[4,48,128]{2,1,0:T(8,128)(2,1)S(1)} %get-tuple-element.23), channel_id=1, source_target_pairs={{0,12},{2,14},{4,8},{6,10},{8,4},{10,6},{12,0},{14,2},{1,13},{3,15... | collective-permute-start | bytes 147464 | tf_op jit(solution)/shard_map/ppermute | solution.py:214
  37.3 0.5 %collective-permute-start.11 = (bf16[4,48,128]{2,1,0:T(8,128)(2,1)S(1)}, bf16[4,48,128]{2,1,0:T(8,128)(2,1)S(1)}, u32[]{:S(2)}, u32[]{:S(2)}) collective-permute-start(bf16[4,48,128]{2,1,0:T(8,128)(2,1)S(1)} %get-tuple-element.24), channel_id=1, source_target_pairs={{0,4},{2,6},{4,0},{6,2},{8,12},{10,14},{12,8},{14,10},{1,5},{3,7},... | collective-permute-start | bytes 147464 | tf_op jit(solution)/shard_map/ppermute | solution.py:214
  37.8 2.4 %collective-permute-done.9 = bf16[4,48,128]{2,1,0:T(8,128)(2,1)S(1)} collective-permute-done((bf16[4,48,128]{2,1,0:T(8,128)(2,1)S(1)}, bf16[4,48,128]{2,1,0:T(8,128)(2,1)S(1)}, u32[]{:S(2)}, u32[]{:S(2)}) %collective-permute-start.9) | collective-permute-done | bytes 49184 | tf_op jit(solution)/shard_map/ppermute | solution.py:214
  40.2 0.7 %collective-permute-done.10 = bf16[4,48,128]{2,1,0:T(8,128)(2,1)S(1)} collective-permute-done((bf16[4,48,128]{2,1,0:T(8,128)(2,1)S(1)}, bf16[4,48,128]{2,1,0:T(8,128)(2,1)S(1)}, u32[]{:S(2)}, u32[]{:S(2)}) %collective-permute-start.10) | collective-permute-done | bytes 49184 | tf_op jit(solution)/shard_map/ppermute | solution.py:214
  40.9 0.8 %collective-permute-done.11 = bf16[4,48,128]{2,1,0:T(8,128)(2,1)S(1)} collective-permute-done((bf16[4,48,128]{2,1,0:T(8,128)(2,1)S(1)}, bf16[4,48,128]{2,1,0:T(8,128)(2,1)S(1)}, u32[]{:S(2)}, u32[]{:S(2)}) %collective-permute-start.11) | collective-permute-done | bytes 49184 | tf_op jit(solution)/shard_map/ppermute | solution.py:214
  41.7 0.7 %add_multiply_fusion = f32[4,48,128]{2,1,0:T(8,128)} fusion(bf16[4,48,128]{2,1,0:T(8,128)(2,1)S(1)} %collective-permute-done.11, bf16[4,48,128]{2,1,0:T(8,128)(2,1)S(1)} %collective-permute-done.10, f32[4,48,128]{2,1,0:T(8,128)S(1)} %get-tuple-element.21, bf16[4,48,128]{2,1,0:T(8,128)(2,1)S(1)} %collective-permute-done.9), kind=kLoop, calls=%fused_computation | loop fusion | flops 172032 | bytes 344064 | tf_op jit(solution)/shard_map/mul | solution.py:313
  (16 shorter events, 0.9 us)
Async XLA Ops:
  0.7 1.0 %copy-start = (bf16[8,128,2,128]{3,2,1,0:T(2,128)(2,1)S(1)}, bf16[8,128,2,128]{3,2,1,0:T(2,128)(2,1)}, u32[]{:S(2)}) copy-start(bf16[8,128,2,128]{3,2,1,0:T(2,128)(2,1)} %param.3) | copy-start | bytes 1572868
  1.7 1.1 %copy-start.1 = (s32[8]{0:T(128)S(1)}, s32[8]{0:T(128)}, u32[]{:S(2)}) copy-start(s32[8]{0:T(128)} %param.4) | copy-start | bytes 100
  2.3 1.3 %collective-permute-start = (f32[8,128]{1,0:T(8,128)S(1)}, f32[8,128]{1,0:T(8,128)S(1)}, u32[]{:S(2)}, u32[]{:S(2)}) collective-permute-start(f32[8,128]{1,0:T(8,128)S(1)} %power.1.own_ref), channel_id=1, source_target_pairs={{0,1},{1,0},{2,3},{3,2},{4,5},{5,4},{6,7},{7,6},{8,9},{9,8},{10,11... | collective-permute-start | bytes 12296 | tf_op jit(solution)/shard_map/ppermute | solution.py:214
  4.2 13.9 %collective-permute-start.2 = (bf16[8,2,32,128]{3,2,1,0:T(8,128)(2,1)S(1)}, bf16[8,2,32,128]{3,2,1,0:T(8,128)(2,1)S(1)}, u32[]{:S(2)}, u32[]{:S(2)}) collective-permute-start(bf16[8,2,32,128]{3,2,1,0:T(8,128)(2,1)S(1)} %get-tuple-element.17), channel_id=1, source_target_pairs={{0,8},{2,10},{4,12},{6,14},{8,0},{10,2},{12,4},{14,6},{1,9},{3,11}... | collective-permute-start | bytes 393224 | tf_op jit(solution)/shard_map/ppermute | solution.py:214
  8.2 11.8 %collective-permute-start.3 = (bf16[8,2,32,128]{3,2,1,0:T(8,128)(2,1)S(1)}, bf16[8,2,32,128]{3,2,1,0:T(8,128)(2,1)S(1)}, u32[]{:S(2)}, u32[]{:S(2)}) collective-permute-start(bf16[8,2,32,128]{3,2,1,0:T(8,128)(2,1)S(1)} %get-tuple-element.18), channel_id=1, source_target_pairs={{0,12},{2,14},{4,8},{6,10},{8,4},{10,6},{12,0},{14,2},{1,13},{3,15... | collective-permute-start | bytes 393224 | tf_op jit(solution)/shard_map/ppermute | solution.py:214
  9.5 10.6 %collective-permute-start.1 = (bf16[8,2,32,128]{3,2,1,0:T(8,128)(2,1)S(1)}, bf16[8,2,32,128]{3,2,1,0:T(8,128)(2,1)S(1)}, u32[]{:S(2)}, u32[]{:S(2)}) collective-permute-start(bf16[8,2,32,128]{3,2,1,0:T(8,128)(2,1)S(1)} %get-tuple-element.16), channel_id=1, source_target_pairs={{0,4},{2,6},{4,0},{6,2},{8,12},{10,14},{12,8},{14,10},{1,5},{3,7},... | collective-permute-start | bytes 393224 | tf_op jit(solution)/shard_map/ppermute | solution.py:214
  10.0 14.7 %collective-permute-start.5 = (bf16[8,2,32,128]{3,2,1,0:T(8,128)(2,1)S(1)}, bf16[8,2,32,128]{3,2,1,0:T(8,128)(2,1)S(1)}, u32[]{:S(2)}, u32[]{:S(2)}) collective-permute-start(bf16[8,2,32,128]{3,2,1,0:T(8,128)(2,1)S(1)} %get-tuple-element.16), channel_id=1, source_target_pairs={{0,6},{2,4},{4,2},{6,0},{8,14},{10,12},{12,10},{14,8},{1,7},{3,5},... | collective-permute-start | bytes 393224 | tf_op jit(solution)/shard_map/ppermute | solution.py:214
  12.8 11.9 %collective-permute-start.4 = (bf16[8,2,32,128]{3,2,1,0:T(8,128)(2,1)S(1)}, bf16[8,2,32,128]{3,2,1,0:T(8,128)(2,1)S(1)}, u32[]{:S(2)}, u32[]{:S(2)}) collective-permute-start(bf16[8,2,32,128]{3,2,1,0:T(8,128)(2,1)S(1)} %get-tuple-element.15.refs_1_.refs_2_), channel_id=1, source_target_pairs={{0,2},{2,0},{4,6},{6,4},{8,10},{10,8},{12,14},{14,12},{1,3},{3,1},... | collective-permute-start | bytes 393224 | tf_op jit(solution)/shard_map/ppermute | solution.py:214
  18.1 7.7 %collective-permute-start.6 = (bf16[8,2,32,128]{3,2,1,0:T(8,128)(2,1)S(1)}, bf16[8,2,32,128]{3,2,1,0:T(8,128)(2,1)S(1)}, u32[]{:S(2)}, u32[]{:S(2)}) collective-permute-start(bf16[8,2,32,128]{3,2,1,0:T(8,128)(2,1)S(1)} %collective-permute-done.2.refs_3_.refs_4_), channel_id=1, source_target_pairs={{0,2},{2,0},{4,6},{6,4},{8,10},{10,8},{12,14},{14,12},{1,3},{3,1},... | collective-permute-start | bytes 393224 | tf_op jit(solution)/shard_map/ppermute | solution.py:214
  20.0 7.8 %collective-permute-start.7 = (bf16[8,2,32,128]{3,2,1,0:T(8,128)(2,1)S(1)}, bf16[8,2,32,128]{3,2,1,0:T(8,128)(2,1)S(1)}, u32[]{:S(2)}, u32[]{:S(2)}) collective-permute-start(bf16[8,2,32,128]{3,2,1,0:T(8,128)(2,1)S(1)} %collective-permute-done.3.refs_4_.refs_5_), channel_id=1, source_target_pairs={{0,2},{2,0},{4,6},{6,4},{8,10},{10,8},{12,14},{14,12},{1,3},{3,1},... | collective-permute-start | bytes 393224 | tf_op jit(solution)/shard_map/ppermute | solution.py:214
  31.9 1.5 %collective-permute-start.8 = (bf16[4,4,48,128]{3,2,1,0:T(8,128)(2,1)S(1)}, bf16[4,4,48,128]{3,2,1,0:T(8,128)(2,1)S(1)}, u32[]{:S(2)}, u32[]{:S(2)}) collective-permute-start(bf16[4,4,48,128]{3,2,1,0:T(8,128)(2,1)S(1)} %get-tuple-element.20), channel_id=1, source_target_pairs={{0,1},{1,0},{2,3},{3,2},{4,5},{5,4},{6,7},{7,6},{8,9},{9,8},{10,11... | collective-permute-start | bytes 589832 | tf_op jit(solution)/shard_map/ppermute | solution.py:214
  33.5 6.7 %collective-permute-start.9 = (bf16[4,48,128]{2,1,0:T(8,128)(2,1)S(1)}, bf16[4,48,128]{2,1,0:T(8,128)(2,1)S(1)}, u32[]{:S(2)}, u32[]{:S(2)}) collective-permute-start(bf16[4,48,128]{2,1,0:T(8,128)(2,1)S(1)} %get-tuple-element.22), channel_id=1, source_target_pairs={{0,8},{2,10},{4,12},{6,14},{8,0},{10,2},{12,4},{14,6},{1,9},{3,11}... | collective-permute-start | bytes 147464 | tf_op jit(solution)/shard_map/ppermute | solution.py:214
  35.0 5.9 %collective-permute-start.10 = (bf16[4,48,128]{2,1,0:T(8,128)(2,1)S(1)}, bf16[4,48,128]{2,1,0:T(8,128)(2,1)S(1)}, u32[]{:S(2)}, u32[]{:S(2)}) collective-permute-start(bf16[4,48,128]{2,1,0:T(8,128)(2,1)S(1)} %get-tuple-element.23), channel_id=1, source_target_pairs={{0,12},{2,14},{4,8},{6,10},{8,4},{10,6},{12,0},{14,2},{1,13},{3,15... | collective-permute-start | bytes 147464 | tf_op jit(solution)/shard_map/ppermute | solution.py:214
  37.3 4.4 %collective-permute-start.11 = (bf16[4,48,128]{2,1,0:T(8,128)(2,1)S(1)}, bf16[4,48,128]{2,1,0:T(8,128)(2,1)S(1)}, u32[]{:S(2)}, u32[]{:S(2)}) collective-permute-start(bf16[4,48,128]{2,1,0:T(8,128)(2,1)S(1)} %get-tuple-element.24), channel_id=1, source_target_pairs={{0,4},{2,6},{4,0},{6,2},{8,12},{10,14},{12,8},{14,10},{1,5},{3,7},... | collective-permute-start | bytes 147464 | tf_op jit(solution)/shard_map/ppermute | solution.py:214

commit v3 on v2

--- a/solution.py
+++ b/solution.py
@@ -14,6 +14,8 @@
 SIDES = 2
 LEVELS = 4
 TEAM = SIDES * LEVELS
+FIRST_LATE = 2
+UNROLL = 3
 EARLY = (("near", 2), ("far", 0), ("near", 3), ("near", 1), ("far", 1))
 LATE = (2, 3)
 OUT_ORDER = (2, 3, 1)
@@ -81,11 +83,11 @@
             pieces[step][window, 1] = (weight * (imag * cosine - real * sine)).astype(jnp.bfloat16)
 
 
-def gather(pieces, held, before):
+def gather(pieces, held, before, skip=0):
     windows = pieces[0].shape[0]
     level = lax.rem(lax.axis_index("tm"), TEAM) // SIDES
     for index, piece in enumerate(pieces):
-        block = (level ^ (index % LEVELS)) + (before if index < LEVELS else 0)
+        block = (level ^ ((index + skip) % LEVELS)) + (before if index + skip < LEVELS else 0)
         held[pl.ds(block * windows, windows)] = piece[...]
 
 
@@ -104,99 +106,106 @@
         store(window, band_sums(left[left_at + window, 0], left[left_at + window, 1], right_real, right_imag, table))
 
 
-def level_of(pair, firsts):
-    level = jnp.int32(0)
-    for first in firsts[1:]:
-        level += (pair >= first).astype(jnp.int32)
-    start = jnp.int32(0)
-    for index, first in enumerate(firsts):
-        start = jnp.where(level == index, first, start)
-    return level, pair - start
-
-
-def sweep(counts, unroll, visit):
-    firsts = [sum(counts[:index]) for index in range(len(counts))]
-    pairs = sum(counts)
-    assert pairs % unroll == 0
-
-    def turn(index, carry):
-        for inner in range(unroll):
-            visit(*level_of(index * unroll + inner, firsts))
-        return carry
-
-    lax.fori_loop(0, pairs // unroll, turn, 0)
-
-
 def near_kernel(teams, count, *refs):
-    table_ref, pieces, (sums_ref, held) = refs[0], refs[1 : 1 + count], refs[1 + count :]
+    table_ref, pieces, (grid, held) = refs[0], refs[1 : 1 + count], refs[1 + count :]
     windows = pieces[0].shape[0]
     before = LEVELS if teams else 0
     gather(pieces, held, before)
+    grid[...] = jnp.zeros(grid.shape, grid.dtype)
     table = table_ref[...]
-    counts = [LEVELS if teams else level + 1 for level in range(LEVELS)]
+    furthest = LEVELS - 1
+
+    def block(level, kind):
+        return held[pl.ds((before + level) * windows, windows), kind]
+
     for level in range(LEVELS):
-        skipped = (LEVELS - counts[level]) * windows
-        if skipped:
-            sums_ref[level, :, :skipped, :] = jnp.zeros((windows, skipped, sums_ref.shape[3]), jnp.float32)
-
-    def visit(level, back):
-        place = pl.multiple_of((LEVELS - 1 - back) * windows, windows)
-
-        def store(window, sums):
-            sums_ref[level, window, pl.ds(place, windows), :] = sums
-
-        block_sums(held, (before + level) * windows, held, (before + level - back) * windows, windows, table, store)
-
-    sweep(counts, 2, visit)
-
-
-def far_kernel(teams, count, *refs):
-    table_ref, near_ref, pieces = refs[0], refs[1], refs[2 : 2 + 2 * count]
-    mine_ref, other_ref, held, across, grid = refs[2 + 2 * count :]
-    windows = pieces[0].shape[0]
-    side = lax.rem(lax.axis_index("tm"), SIDES)
-    core = lax.axis_index("chan")
-    before = LEVELS if teams else 0
-    margin = LEVELS if teams else 1
-    gather(pieces[:count], held, before)
-    gather(pieces[count:], across, margin)
-    if not teams:
-        across[pl.ds(0, windows)] = jnp.zeros((windows,) + across.shape[1:], across.dtype)
+        lefts = (before + level) * windows
+        own_real, own_imag = block(level, 0), block(level, 1)
+        ring = teams or level == furthest
+        for back in range(furthest + 1):
+            place = 2 * (furthest - back) * windows
+            if 0 < back < furthest and (teams or back <= level):
+                right_real, right_imag = block(level - back, 0), block(level - back, 1)
+                for window in range(windows):
+                    grid[level, window, place : place + windows, :] = band_sums(
+                        held[lefts + window, 0], held[lefts + window, 1], right_real, right_imag, table
+                    )
+        last = 2 * furthest * windows
+        if ring:
+            old_real, old_imag = block(level - furthest, 0), block(level - furthest, 1)
+        for window in range(windows):
+            rows = windows if ring else window
+            if rows:
+                if ring and window:
+                    right_real = jnp.concatenate([own_real[:window], old_real[window:]], axis=0)
+                    right_imag = jnp.concatenate([own_imag[:window], old_imag[window:]], axis=0)
+                elif ring:
+                    right_real, right_imag = old_real, old_imag
+                else:
+                    right_real, right_imag = own_real[:window], own_imag[:window]
+                sums = band_sums(held[lefts + window, 0], held[lefts + window, 1], right_real, right_imag, table)
+                grid[level, window, last : last + rows, :] = sums
+                if ring:
+                    grid[level, window, :windows, :] = sums
+
+
+def list_units(kernel, teams, windows, units_ref):
+    member = lax.rem(lax.axis_index("tm"), TEAM)
+    side, here = lax.rem(member, SIDES), member // SIDES
+    halo = LEVELS if teams else 0
+    found = jnp.int32(0)
+    reach = LEVELS - 1
+    for left in range(LEVELS):
+        for back in range(reach):
+            right = left - 1 - back + side
+            late = (right < 0) | ((lax.rem(right + LEVELS, LEVELS) ^ here) >= FIRST_LATE)
+            wanted = (right >= -halo) & (late == (kernel == 1))
+            values = (left, (left + halo) * windows, (right + halo) * windows, (2 * (reach - 1 - back) + 1) * windows)
+            for index, value in enumerate(values):
+                units_ref[4 * found + index] = jnp.int32(value)
+            found = jnp.where(wanted, found + 1, found)
+    last = jnp.maximum(found - 1, 0)
+    for extra in range(UNROLL - 1):
+        for index in range(4):
+            units_ref[4 * (found + extra) + index] = units_ref[4 * last + index]
+    return (found + UNROLL - 1) // UNROLL
+
+
+def far_kernel(kernel, teams, count, *refs):
+    table_ref, _, near, pieces = refs[0], refs[1], refs[2], refs[3 : 3 + count]
+    grid, (far, units_ref) = refs[3 + count], refs[-2:]
+    windows = grid.shape[1]
+    turns = list_units(kernel, teams, windows, units_ref)
+    gather(pieces, far, LEVELS if teams else 0, 0 if teams or kernel == 0 else FIRST_LATE)
     table = table_ref[...]
-    band = mine_ref.shape[2]
-    keep = mine_ref.shape[1]
-    reach = LEVELS - 1
-    counts = [reach if teams else min(reach, level + 1) for level in range(LEVELS)]
-    for level in range(LEVELS):
-        for block in range(reach - counts[level]):
-            grid[level, :, (2 * block + 1) * windows : (2 * block + 2) * windows, :] = jnp.zeros(
-                (windows, windows, grid.shape[3]), jnp.float32
-            )
-
-    def visit(level, back):
-        place = pl.multiple_of((2 * (reach - 1 - back) + 1) * windows, windows)
-
-        def store(window, sums):
-            grid[level, window, pl.ds(place, windows), :] = sums
-
-        right = (margin + level + side - 1 - back) * windows
-        block_sums(held, (before + level) * windows, across, right, windows, table, store)
-
-    sweep(counts, 3, visit)
-
-    def finish(level, carry):
-        for block in range(LEVELS):
-            grid[level, :, 2 * block * windows : (2 * block + 1) * windows, :] = near_ref[
-                level, :, block * windows : (block + 1) * windows, :
-            ]
-        for inner in range(keep):
-            window = core * keep + inner
-            mine_ref[level, inner] = grid[level, window, pl.ds(window, band), :]
-            window = (1 - core) * keep + inner
-            other_ref[level, inner] = grid[level, window, pl.ds(window, band), :].astype(other_ref.dtype)
+
+    def turn(index, carry):
+        for inner in range(UNROLL):
+            at = 4 * (index * UNROLL + inner)
+            level = units_ref[at]
+            row = pl.multiple_of(units_ref[at + 3], windows)
+
+            def store(window, sums):
+                grid[level, window, pl.ds(row, windows), :] = sums
+
+            block_sums(near, units_ref[at + 1], far, units_ref[at + 2], windows, table, store)
         return carry
 
-    lax.fori_loop(0, LEVELS, finish, 0)
+    lax.fori_loop(0, turns, turn, 0)
+    if kernel == 1:
+        mine_ref, other_ref = refs[4 + count : 6 + count]
+        core = lax.axis_index("chan")
+        keep, band = mine_ref.shape[1:3]
+
+        def finish(level, carry):
+            for inner in range(keep):
+                window = core * keep + inner
+                mine_ref[level, inner] = grid[level, window, pl.ds(window, band), :]
+                window = (1 - core) * keep + inner
+                other_ref[level, inner] = grid[level, window, pl.ds(window, band), :].astype(other_ref.dtype)
+            return carry
+
+        lax.fori_loop(0, LEVELS, finish, 0)
 
 
 def merge_kernel(mine_ref, other_ref, *outs):
@@ -265,38 +274,37 @@
         near += [lax.ppermute(piece, "tm", pairs) for piece in near]
         far += [lax.ppermute(piece, "tm", pairs) for piece in far]
     count = len(near)
-    held_blocks = count
-    across_blocks = count if teams else count + 1
     table = lag_table(freq, LAGS)
-
-    near_sums = pl.pallas_call(
+    held = (count * windows, 2, part, freq)
+    grid_shape = jax.ShapeDtypeStruct((LEVELS, windows, (SPAN + 1) * windows, LAGS), jnp.float32)
+    sums_shape = (LEVELS, keep, band, LAGS)
+    grid, near_held = pl.pallas_call(
         functools.partial(near_kernel, teams, count),
-        out_shape=jax.ShapeDtypeStruct((LEVELS, windows, LEVELS * windows, LAGS), jnp.float32),
+        out_shape=[grid_shape, jax.ShapeDtypeStruct(held, jnp.bfloat16)],
         in_specs=[vmem()] * (1 + count),
-        out_specs=vmem(),
-        scratch_shapes=[
-            pltpu.VMEM((held_blocks * windows, 2, part, freq), jnp.bfloat16),
-        ],
+        out_specs=[vmem()] * 2,
         compiler_params=params,
         cost_estimate=pl.CostEstimate(flops=2000000000, bytes_accessed=2000000, transcendentals=0),
         name="near",
     )(table, *near)
-    sums_shape = (LEVELS, keep, band, LAGS)
-    mine, other = pl.pallas_call(
-        functools.partial(far_kernel, teams, count),
-        out_shape=[
+    for kernel, pieces in enumerate((far[:FIRST_LATE], far if teams else far[FIRST_LATE:])):
+        results = [
             jax.ShapeDtypeStruct(sums_shape, jnp.float32), jax.ShapeDtypeStruct(sums_shape, jnp.bfloat16)
-        ],
-        in_specs=[vmem()] * (2 + 2 * count),
-        out_specs=[vmem()] * 2,
-        scratch_shapes=[
-            pltpu.VMEM((held_blocks * windows, 2, part, freq), jnp.bfloat16),
-            pltpu.VMEM((across_blocks * windows, 2, part, freq), jnp.bfloat16),
-            pltpu.VMEM((LEVELS, windows, (SPAN + 1) * windows, LAGS), jnp.float32),
-        ],
-        compiler_params=params,
-        name="far",
-    )(table, near_sums, *near, *far)
+        ] * kernel
+        grid, *sums = pl.pallas_call(
+            functools.partial(far_kernel, kernel, teams, len(pieces)),
+            out_shape=[grid_shape] + results,
+            in_specs=[vmem()] * (3 + len(pieces)),
+            out_specs=[vmem()] * (1 + len(results)),
+            scratch_shapes=[
+                pltpu.VMEM(held, jnp.bfloat16), pltpu.SMEM((4 * (LEVELS * (LEVELS - 1) + UNROLL),), jnp.int32)
+            ],
+            input_output_aliases={1: 0},
+            compiler_params=params,
+            cost_estimate=pl.CostEstimate(flops=1000000000, bytes_accessed=1000000, transcendentals=0),
+            name=("far", "late")[kernel],
+        )(table, grid, near_held, *pieces)
+    mine, other = sums
     sums = pl.pallas_call(
         merge_kernel,
         out_shape=[

time: 42.5 us -> 40.9 us (0.962)
  waiting for transfers between devices: 13.8 us -> 12.2 us
  Pallas kernels: 9.93 us -> 8.53 us
  starting transfers between devices: 15.8 us -> 17.1 us
    ppermute x12, waiting for transfers between devices: 13.8 us -> 12.2 us  [flip(): lax.ppermute(value, axis, [(source, source ^ bits) for source in range(si...]
    pallas_call x2 -> x3, Pallas kernels: 8.73 us -> 7.32 us  [the longest x2 4.17 us: shards(): pl.pallas_call(functools.partial(far_kernel, kernel, teams, len(pieces)),...]
    ppermute x12, starting transfers between devices: 15.8 us -> 17.1 us  [flip(): lax.ppermute(value, axis, [(source, source ^ bits) for source in range(si...]
  transfers between devices with their start and end apart: 12 -> 12, of which waited for: 8 -> 6; matrix products, arithmetic and copies ran while one was open for 1% -> 1% of each run, Pallas kernels for 11% -> 14%
where the time goes in v3:
time: 40.9 us; the launch traced here: 40.8 us
  starting transfers between devices  17.1 us (42%)
  waiting for transfers between devices  12.2 us (30%)
  Pallas kernels  8.53 us (21%)
  other arithmetic  1.75 us (4%)
  local copies, waits for them, and re-layouts  1.04 us (3%)
    ppermute x12, starting transfers between devices, flip(): lax.ppermute(value, axis, [(source, source ^ bits) for source in range(si...  17.1 us
    ppermute x12, waiting for transfers between devices, flip(): lax.ppermute(value, axis, [(source, source ^ bits) for source in range(si...  12.2 us
    pallas_call x2, Pallas kernels, shards(): pl.pallas_call(functools.partial(far_kernel, kernel, teams, len(pieces)),...  4.17 us
    pallas_call x1, Pallas kernels, shards(): pl.pallas_call(functools.partial(near_kernel, teams, count), out_shape=[g...  3.15 us
    unnamed x4, local copies, waits for them, and re-layouts  1.04 us
  transfers between devices with their start and end apart: 12, of which 6 were waited for; matrix products, arithmetic and copies ran while one was open for 1% of the time, Pallas kernels for 14%

profile of v3, /device:TPU:0, one launch (start us, length us, event | category | flops | bytes accessed | tf_op | source)
XLA Modules:
  0.0 40.8 jit_solution(6779967858753817143)
XLA Ops:
  0.0 0.7 %fusion.12.member_ref = f32[8,128]{1,0:T(8,128)S(1)} fusion(s32[128]{0:T(128)} %param.5), kind=kLoop, calls=%fused_computation.24 | loop fusion | flops 2048 | bytes 4608 | tf_op jit(solution)/shard_map/convert_element_type | solution.py:237
  0.7 1.0 %copy-done = bf16[8,128,2,128]{3,2,1,0:T(2,128)(2,1)S(1)} copy-done((bf16[8,128,2,128]{3,2,1,0:T(2,128)(2,1)S(1)}, bf16[8,128,2,128]{3,2,1,0:T(2,128)(2,1)}, u32[]{:S(2)}) %copy-start) | copy-done | bytes 524312
  1.7 0.6 %power.1.own_ref = f32[8,128]{1,0:T(8,128)S(1)} custom-call(bf16[8,256,128]{2,1,0:T(8,128)(2,1)S(1)} %bitcast.1, f32[8,128]{1,0:T(8,128)S(1)} %fusion.12.member_ref), custom_call_target="tpu_custom_call" | custom-call | tf_op jit(solution)/shard_map/power/pallas_call | solution.py:238
  2.3 0.5 %collective-permute-start = (f32[8,128]{1,0:T(8,128)S(1)}, f32[8,128]{1,0:T(8,128)S(1)}, u32[]{:S(2)}, u32[]{:S(2)}) collective-permute-start(f32[8,128]{1,0:T(8,128)S(1)} %power.1.own_ref), channel_id=1, source_target_pairs={{0,1},{1,0},{2,3},{3,2},{4,5},{5,4},{6,7},{7,6},{8,9},{9,8},{10,11... | collective-permute-start | bytes 12296 | tf_op jit(solution)/shard_map/ppermute | solution.py:223
  2.9 0.7 %collective-permute-done.other_ref = f32[8,128]{1,0:T(8,128)S(1)} collective-permute-done((f32[8,128]{1,0:T(8,128)S(1)}, f32[8,128]{1,0:T(8,128)S(1)}, u32[]{:S(2)}, u32[]{:S(2)}) %collective-permute-start) | collective-permute-done | bytes 4128 | tf_op jit(solution)/shard_map/ppermute | solution.py:223
  3.6 0.5 %align.1 = (bf16[8,2,32,128]{3,2,1,0:T(8,128)(2,1)S(1)}, bf16[8,2,32,128]{3,2,1,0:T(8,128)(2,1)S(1)}, bf16[8,2,32,128]{3,2,1,0:T(8,128)(2,1)S(1)}, bf16[8,2,32,128]{3,2,1,0:T(8,128)(2,1)S(1)}) custom-call(bf16[8,256,128]{2,1,0:T(8,128)(2,1)S(1)} %bitcast.2, f32[8,128]{1,0:T(8,128)S(1)} %fusion.12.member_ref, f32[8,128]{1,0:T(8,128)S(1)} %power.1.own_ref, ...), custom_call_target="tpu_custom_call" | custom-call | tf_op jit(solution)/shard_map/align/pallas_call | solution.py:249
  4.2 4.0 %collective-permute-start.2 = (bf16[8,2,32,128]{3,2,1,0:T(8,128)(2,1)S(1)}, bf16[8,2,32,128]{3,2,1,0:T(8,128)(2,1)S(1)}, u32[]{:S(2)}, u32[]{:S(2)}) collective-permute-start(bf16[8,2,32,128]{3,2,1,0:T(8,128)(2,1)S(1)} %get-tuple-element.19), channel_id=1, source_target_pairs={{0,8},{2,10},{4,12},{6,14},{8,0},{10,2},{12,4},{14,6},{1,9},{3,11}... | collective-permute-start | bytes 393224 | tf_op jit(solution)/shard_map/ppermute | solution.py:223
  8.2 1.3 %collective-permute-start.3 = (bf16[8,2,32,128]{3,2,1,0:T(8,128)(2,1)S(1)}, bf16[8,2,32,128]{3,2,1,0:T(8,128)(2,1)S(1)}, u32[]{:S(2)}, u32[]{:S(2)}) collective-permute-start(bf16[8,2,32,128]{3,2,1,0:T(8,128)(2,1)S(1)} %get-tuple-element.20), channel_id=1, source_target_pairs={{0,12},{2,14},{4,8},{6,10},{8,4},{10,6},{12,0},{14,2},{1,13},{3,15... | collective-permute-start | bytes 393224 | tf_op jit(solution)/shard_map/ppermute | solution.py:223
  9.7 0.3 multiply_convert_fusion.1
  10.0 2.8 %collective-permute-start.5 = (bf16[8,2,32,128]{3,2,1,0:T(8,128)(2,1)S(1)}, bf16[8,2,32,128]{3,2,1,0:T(8,128)(2,1)S(1)}, u32[]{:S(2)}, u32[]{:S(2)}) collective-permute-start(bf16[8,2,32,128]{3,2,1,0:T(8,128)(2,1)S(1)} %get-tuple-element.18), channel_id=1, source_target_pairs={{0,6},{2,4},{4,2},{6,0},{8,14},{10,12},{12,10},{14,8},{1,7},{3,5},... | collective-permute-start | bytes 393224 | tf_op jit(solution)/shard_map/ppermute | solution.py:223
  12.8 0.5 %collective-permute-start.4 = (bf16[8,2,32,128]{3,2,1,0:T(8,128)(2,1)S(1)}, bf16[8,2,32,128]{3,2,1,0:T(8,128)(2,1)S(1)}, u32[]{:S(2)}, u32[]{:S(2)}) collective-permute-start(bf16[8,2,32,128]{3,2,1,0:T(8,128)(2,1)S(1)} %get-tuple-element.17.refs_1_), channel_id=1, source_target_pairs={{0,2},{2,0},{4,6},{6,4},{8,10},{10,8},{12,14},{14,12},{1,3},{3,1},... | collective-permute-start | bytes 393224 | tf_op jit(solution)/shard_map/ppermute | solution.py:223
  13.4 4.7 %collective-permute-done.2.refs_3_ = bf16[8,2,32,128]{3,2,1,0:T(8,128)(2,1)S(1)} collective-permute-done((bf16[8,2,32,128]{3,2,1,0:T(8,128)(2,1)S(1)}, bf16[8,2,32,128]{3,2,1,0:T(8,128)(2,1)S(1)}, u32[]{:S(2)}, u32[]{:S(2)}) %collective-permute-start.2) | collective-permute-done | bytes 131104 | tf_op jit(solution)/shard_map/ppermute | solution.py:223
  18.1 1.9 %collective-permute-start.6 = (bf16[8,2,32,128]{3,2,1,0:T(8,128)(2,1)S(1)}, bf16[8,2,32,128]{3,2,1,0:T(8,128)(2,1)S(1)}, u32[]{:S(2)}, u32[]{:S(2)}) collective-permute-start(bf16[8,2,32,128]{3,2,1,0:T(8,128)(2,1)S(1)} %collective-permute-done.2.refs_3_), channel_id=1, source_target_pairs={{0,2},{2,0},{4,6},{6,4},{8,10},{10,8},{12,14},{14,12},{1,3},{3,1},... | collective-permute-start | bytes 393224 | tf_op jit(solution)/shard_map/ppermute | solution.py:223
  20.1 3.2 %near.1 = (f32[4,8,56,128]{3,2,1,0:T(8,128)S(1)}, bf16[32,2,32,128]{3,2,1,0:T(8,128)(2,1)S(1)}) custom-call(bf16[256,128]{1,0:T(8,128)(2,1)S(1)} %pad_maximum_fusion.refs_0_, bf16[8,2,32,128]{3,2,1,0:T(8,128)(2,1)S(1)} %get-tuple-element.17.refs_1_, bf16[8,2,32,128]{3,2,1,0:T(8,128)(2,1)S(1)} %collective-permute-done.1.refs_2_, ...), custom_call_target="tpu_custom_call" | custom-call | flops 2000000000 | bytes 2000000 | tf_op jit(solution)/shard_map/near/pallas_call | solution.py:281
  23.3 2.7 %far.1.refs_1_ = f32[4,8,56,128]{3,2,1,0:T(8,128)S(1)} custom-call(bf16[256,128]{1,0:T(8,128)(2,1)S(1)} %pad_maximum_fusion.refs_0_, f32[4,8,56,128]{3,2,1,0:T(8,128)S(1)} %get-tuple-element.21.refs_1_, bf16[32,2,32,128]{3,2,1,0:T(8,128)(2,1)S(1)} %get-tuple-element.22.refs_2_, ...), custom_call_target="tpu_custom_call", output_to_operand_aliasing={{}: (1, {})} | custom-call | flops 1000000000 | bytes 1000000 | tf_op jit(solution)/shard_map/far/pallas_call | solution.py:294
  26.0 1.8 %collective-permute-done.7.refs_4_ = bf16[8,2,32,128]{3,2,1,0:T(8,128)(2,1)S(1)} collective-permute-done((bf16[8,2,32,128]{3,2,1,0:T(8,128)(2,1)S(1)}, bf16[8,2,32,128]{3,2,1,0:T(8,128)(2,1)S(1)}, u32[]{:S(2)}, u32[]{:S(2)}) %collective-permute-start.7) | collective-permute-done | bytes 131104 | tf_op jit(solution)/shard_map/ppermute | solution.py:223
  27.8 1.5 %late.1 = (f32[4,8,56,128]{3,2,1,0:T(8,128)S(1)}, f32[4,4,48,128]{3,2,1,0:T(8,128)S(1)}, bf16[4,4,48,128]{3,2,1,0:T(8,128)(2,1)S(1)}) custom-call(bf16[256,128]{1,0:T(8,128)(2,1)S(1)} %pad_maximum_fusion.refs_0_, f32[4,8,56,128]{3,2,1,0:T(8,128)S(1)} %far.1.refs_1_, ...), custom_call_target="tpu_custom_call", output_to_operand_aliasing={{0}: (1, {})} | custom-call | flops 1000000000 | bytes 1000000 | tf_op jit(solution)/shard_map/late/pallas_call | solution.py:294
  29.3 1.4 %collective-permute-done.8.other_ref = bf16[4,4,48,128]{3,2,1,0:T(8,128)(2,1)S(1)} collective-permute-done((bf16[4,4,48,128]{3,2,1,0:T(8,128)(2,1)S(1)}, bf16[4,4,48,128]{3,2,1,0:T(8,128)(2,1)S(1)}, u32[]{:S(2)}, u32[]{:S(2)}) %collective-permute-start.8) | collective-permute-done | bytes 196640 | tf_op jit(solution)/shard_map/ppermute | solution.py:223
  30.8 2.8 %collective-permute-start.9 = (bf16[4,48,128]{2,1,0:T(8,128)(2,1)S(1)}, bf16[4,48,128]{2,1,0:T(8,128)(2,1)S(1)}, u32[]{:S(2)}, u32[]{:S(2)}) collective-permute-start(bf16[4,48,128]{2,1,0:T(8,128)(2,1)S(1)} %get-tuple-element.26), channel_id=1, source_target_pairs={{0,8},{2,10},{4,12},{6,14},{8,0},{10,2},{12,4},{14,6},{1,9},{3,11}... | collective-permute-start | bytes 147464 | tf_op jit(solution)/shard_map/ppermute | solution.py:223
  33.6 2.4 %collective-permute-start.10 = (bf16[4,48,128]{2,1,0:T(8,128)(2,1)S(1)}, bf16[4,48,128]{2,1,0:T(8,128)(2,1)S(1)}, u32[]{:S(2)}, u32[]{:S(2)}) collective-permute-start(bf16[4,48,128]{2,1,0:T(8,128)(2,1)S(1)} %get-tuple-element.27), channel_id=1, source_target_pairs={{0,12},{2,14},{4,8},{6,10},{8,4},{10,6},{12,0},{14,2},{1,13},{3,15... | collective-permute-start | bytes 147464 | tf_op jit(solution)/shard_map/ppermute | solution.py:223
  36.0 0.5 %collective-permute-start.11 = (bf16[4,48,128]{2,1,0:T(8,128)(2,1)S(1)}, bf16[4,48,128]{2,1,0:T(8,128)(2,1)S(1)}, u32[]{:S(2)}, u32[]{:S(2)}) collective-permute-start(bf16[4,48,128]{2,1,0:T(8,128)(2,1)S(1)} %get-tuple-element.28), channel_id=1, source_target_pairs={{0,4},{2,6},{4,0},{6,2},{8,12},{10,14},{12,8},{14,10},{1,5},{3,7},... | collective-permute-start | bytes 147464 | tf_op jit(solution)/shard_map/ppermute | solution.py:223
  36.5 3.1 %collective-permute-done.10 = bf16[4,48,128]{2,1,0:T(8,128)(2,1)S(1)} collective-permute-done((bf16[4,48,128]{2,1,0:T(8,128)(2,1)S(1)}, bf16[4,48,128]{2,1,0:T(8,128)(2,1)S(1)}, u32[]{:S(2)}, u32[]{:S(2)}) %collective-permute-start.10) | collective-permute-done | bytes 49184 | tf_op jit(solution)/shard_map/ppermute | solution.py:223
  39.6 0.5 %collective-permute-done.11 = bf16[4,48,128]{2,1,0:T(8,128)(2,1)S(1)} collective-permute-done((bf16[4,48,128]{2,1,0:T(8,128)(2,1)S(1)}, bf16[4,48,128]{2,1,0:T(8,128)(2,1)S(1)}, u32[]{:S(2)}, u32[]{:S(2)}) %collective-permute-start.11) | collective-permute-done | bytes 49184 | tf_op jit(solution)/shard_map/ppermute | solution.py:223
  40.1 0.7 %add_multiply_fusion = f32[4,48,128]{2,1,0:T(8,128)} fusion(bf16[4,48,128]{2,1,0:T(8,128)(2,1)S(1)} %collective-permute-done.11, bf16[4,48,128]{2,1,0:T(8,128)(2,1)S(1)} %collective-permute-done.10, f32[4,48,128]{2,1,0:T(8,128)S(1)} %get-tuple-element.25, bf16[4,48,128]{2,1,0:T(8,128)(2,1)S(1)} %collective-permute-done.9), kind=kLoop, calls=%fused_computation | loop fusion | flops 172032 | bytes 344064 | tf_op jit(solution)/shard_map/mul | solution.py:321
  (17 shorter events, 0.7 us)
Async XLA Ops:
  0.7 1.0 %copy-start = (bf16[8,128,2,128]{3,2,1,0:T(2,128)(2,1)S(1)}, bf16[8,128,2,128]{3,2,1,0:T(2,128)(2,1)}, u32[]{:S(2)}) copy-start(bf16[8,128,2,128]{3,2,1,0:T(2,128)(2,1)} %param.3) | copy-start | bytes 1572868
  1.7 1.1 %copy-start.1 = (s32[8]{0:T(128)S(1)}, s32[8]{0:T(128)}, u32[]{:S(2)}) copy-start(s32[8]{0:T(128)} %param.4) | copy-start | bytes 100
  2.3 1.3 %collective-permute-start = (f32[8,128]{1,0:T(8,128)S(1)}, f32[8,128]{1,0:T(8,128)S(1)}, u32[]{:S(2)}, u32[]{:S(2)}) collective-permute-start(f32[8,128]{1,0:T(8,128)S(1)} %power.1.own_ref), channel_id=1, source_target_pairs={{0,1},{1,0},{2,3},{3,2},{4,5},{5,4},{6,7},{7,6},{8,9},{9,8},{10,11... | collective-permute-start | bytes 12296 | tf_op jit(solution)/shard_map/ppermute | solution.py:223
  4.2 13.9 %collective-permute-start.2 = (bf16[8,2,32,128]{3,2,1,0:T(8,128)(2,1)S(1)}, bf16[8,2,32,128]{3,2,1,0:T(8,128)(2,1)S(1)}, u32[]{:S(2)}, u32[]{:S(2)}) collective-permute-start(bf16[8,2,32,128]{3,2,1,0:T(8,128)(2,1)S(1)} %get-tuple-element.19), channel_id=1, source_target_pairs={{0,8},{2,10},{4,12},{6,14},{8,0},{10,2},{12,4},{14,6},{1,9},{3,11}... | collective-permute-start | bytes 393224 | tf_op jit(solution)/shard_map/ppermute | solution.py:223
  8.2 11.8 %collective-permute-start.3 = (bf16[8,2,32,128]{3,2,1,0:T(8,128)(2,1)S(1)}, bf16[8,2,32,128]{3,2,1,0:T(8,128)(2,1)S(1)}, u32[]{:S(2)}, u32[]{:S(2)}) collective-permute-start(bf16[8,2,32,128]{3,2,1,0:T(8,128)(2,1)S(1)} %get-tuple-element.20), channel_id=1, source_target_pairs={{0,12},{2,14},{4,8},{6,10},{8,4},{10,6},{12,0},{14,2},{1,13},{3,15... | collective-permute-start | bytes 393224 | tf_op jit(solution)/shard_map/ppermute | solution.py:223
  9.5 10.6 %collective-permute-start.1 = (bf16[8,2,32,128]{3,2,1,0:T(8,128)(2,1)S(1)}, bf16[8,2,32,128]{3,2,1,0:T(8,128)(2,1)S(1)}, u32[]{:S(2)}, u32[]{:S(2)}) collective-permute-start(bf16[8,2,32,128]{3,2,1,0:T(8,128)(2,1)S(1)} %get-tuple-element.18), channel_id=1, source_target_pairs={{0,4},{2,6},{4,0},{6,2},{8,12},{10,14},{12,8},{14,10},{1,5},{3,7},... | collective-permute-start | bytes 393224 | tf_op jit(solution)/shard_map/ppermute | solution.py:223
  10.0 13.3 %collective-permute-start.5 = (bf16[8,2,32,128]{3,2,1,0:T(8,128)(2,1)S(1)}, bf16[8,2,32,128]{3,2,1,0:T(8,128)(2,1)S(1)}, u32[]{:S(2)}, u32[]{:S(2)}) collective-permute-start(bf16[8,2,32,128]{3,2,1,0:T(8,128)(2,1)S(1)} %get-tuple-element.18), channel_id=1, source_target_pairs={{0,6},{2,4},{4,2},{6,0},{8,14},{10,12},{12,10},{14,8},{1,7},{3,5},... | collective-permute-start | bytes 393224 | tf_op jit(solution)/shard_map/ppermute | solution.py:223
  12.8 10.5 %collective-permute-start.4 = (bf16[8,2,32,128]{3,2,1,0:T(8,128)(2,1)S(1)}, bf16[8,2,32,128]{3,2,1,0:T(8,128)(2,1)S(1)}, u32[]{:S(2)}, u32[]{:S(2)}) collective-permute-start(bf16[8,2,32,128]{3,2,1,0:T(8,128)(2,1)S(1)} %get-tuple-element.17.refs_1_), channel_id=1, source_target_pairs={{0,2},{2,0},{4,6},{6,4},{8,10},{10,8},{12,14},{14,12},{1,3},{3,1},... | collective-permute-start | bytes 393224 | tf_op jit(solution)/shard_map/ppermute | solution.py:223
  18.1 7.9 %collective-permute-start.6 = (bf16[8,2,32,128]{3,2,1,0:T(8,128)(2,1)S(1)}, bf16[8,2,32,128]{3,2,1,0:T(8,128)(2,1)S(1)}, u32[]{:S(2)}, u32[]{:S(2)}) collective-permute-start(bf16[8,2,32,128]{3,2,1,0:T(8,128)(2,1)S(1)} %collective-permute-done.2.refs_3_), channel_id=1, source_target_pairs={{0,2},{2,0},{4,6},{6,4},{8,10},{10,8},{12,14},{14,12},{1,3},{3,1},... | collective-permute-start | bytes 393224 | tf_op jit(solution)/shard_map/ppermute | solution.py:223
  20.0 7.8 %collective-permute-start.7 = (bf16[8,2,32,128]{3,2,1,0:T(8,128)(2,1)S(1)}, bf16[8,2,32,128]{3,2,1,0:T(8,128)(2,1)S(1)}, u32[]{:S(2)}, u32[]{:S(2)}) collective-permute-start(bf16[8,2,32,128]{3,2,1,0:T(8,128)(2,1)S(1)} %collective-permute-done.3.refs_4_), channel_id=1, source_target_pairs={{0,2},{2,0},{4,6},{6,4},{8,10},{10,8},{12,14},{14,12},{1,3},{3,1},... | collective-permute-start | bytes 393224 | tf_op jit(solution)/shard_map/ppermute | solution.py:223
  29.3 1.5 %collective-permute-start.8 = (bf16[4,4,48,128]{3,2,1,0:T(8,128)(2,1)S(1)}, bf16[4,4,48,128]{3,2,1,0:T(8,128)(2,1)S(1)}, u32[]{:S(2)}, u32[]{:S(2)}) collective-permute-start(bf16[4,4,48,128]{3,2,1,0:T(8,128)(2,1)S(1)} %get-tuple-element.24), channel_id=1, source_target_pairs={{0,1},{1,0},{2,3},{3,2},{4,5},{5,4},{6,7},{7,6},{8,9},{9,8},{10,11... | collective-permute-start | bytes 589832 | tf_op jit(solution)/shard_map/ppermute | solution.py:223
  30.8 5.7 %collective-permute-start.9 = (bf16[4,48,128]{2,1,0:T(8,128)(2,1)S(1)}, bf16[4,48,128]{2,1,0:T(8,128)(2,1)S(1)}, u32[]{:S(2)}, u32[]{:S(2)}) collective-permute-start(bf16[4,48,128]{2,1,0:T(8,128)(2,1)S(1)} %get-tuple-element.26), channel_id=1, source_target_pairs={{0,8},{2,10},{4,12},{6,14},{8,0},{10,2},{12,4},{14,6},{1,9},{3,11}... | collective-permute-start | bytes 147464 | tf_op jit(solution)/shard_map/ppermute | solution.py:223
  33.6 6.0 %collective-permute-start.10 = (bf16[4,48,128]{2,1,0:T(8,128)(2,1)S(1)}, bf16[4,48,128]{2,1,0:T(8,128)(2,1)S(1)}, u32[]{:S(2)}, u32[]{:S(2)}) collective-permute-start(bf16[4,48,128]{2,1,0:T(8,128)(2,1)S(1)} %get-tuple-element.27), channel_id=1, source_target_pairs={{0,12},{2,14},{4,8},{6,10},{8,4},{10,6},{12,0},{14,2},{1,13},{3,15... | collective-permute-start | bytes 147464 | tf_op jit(solution)/shard_map/ppermute | solution.py:223
  36.0 4.1 %collective-permute-start.11 = (bf16[4,48,128]{2,1,0:T(8,128)(2,1)S(1)}, bf16[4,48,128]{2,1,0:T(8,128)(2,1)S(1)}, u32[]{:S(2)}, u32[]{:S(2)}) collective-permute-start(bf16[4,48,128]{2,1,0:T(8,128)(2,1)S(1)} %get-tuple-element.28), channel_id=1, source_target_pairs={{0,4},{2,6},{4,0},{6,2},{8,12},{10,14},{12,8},{14,10},{1,5},{3,7},... | collective-permute-start | bytes 147464 | tf_op jit(solution)/shard_map/ppermute | solution.py:223

commit v4 on v3

--- a/solution.py
+++ b/solution.py
@@ -14,10 +14,13 @@
 SIDES = 2
 LEVELS = 4
 TEAM = SIDES * LEVELS
-FIRST_LATE = 2
+FAR_STEPS = ((0, 2), (1, 3))
+UNROLL = 3
+RAW = (2,)
+LATE = 2
 UNROLL = 3
 EARLY = (("near", 2), ("far", 0), ("near", 3), ("near", 1), ("far", 1))
-LATE = (2, 3)
+LATE = (2, 1, 3)
 OUT_ORDER = (2, 3, 1)
 
 epsilon = 1e-05
@@ -44,7 +47,8 @@
     return jnp.stack([jnp.cos(phase_angle), jnp.sin(phase_angle)])
 
 
-def power_kernel(spectra_ref, member_ref, power_ref, rows_ref):
+def power_kernel(spectra_ref, member_ref, *rest):
+    power_ref, rows_ref = rest[-2:]
     windows, rows, _ = spectra_ref.shape
     half = rows // 2
     lane = lax.broadcasted_iota(jnp.int32, power_ref.shape, 1)
@@ -58,36 +62,76 @@
     power_ref[...] = power
 
 
-def align_kernel(scale_of_energy, spectra_ref, member_ref, own_ref, other_ref, phase_ref, *rest):
-    pieces, (rows_ref, scale_ref) = rest[:LEVELS], rest[LEVELS:]
+def split_kernel(spectra_ref, *rest):
+    pieces, rows_ref = rest[:-1], rest[-1]
+    windows, part = pieces[0].shape[0], pieces[0].shape[2]
+    level = lax.rem(lax.axis_index("tm"), TEAM) // SIDES
+    for index, (step, piece) in enumerate(zip(RAW, pieces)):
+        first = pl.multiple_of((level ^ step) * 2 * part, 2 * part)
+        for window in range(windows):
+            rows_ref[index, window] = spectra_ref[window, pl.ds(first, 2 * part), :].astype(jnp.float32)
+            for kind in range(2):
+                piece[window, kind] = rows_ref[index, window, pl.ds(kind, part, stride=2), :].astype(jnp.bfloat16)
+
+
+def rotate(real, imag, weight, cosine, sine):
+    return (
+        (weight * (real * cosine + imag * sine)).astype(jnp.bfloat16),
+        (weight * (imag * cosine - real * sine)).astype(jnp.bfloat16),
+    )
+
+
+def spread(member, scales):
+    return lax.dot_general(
+        member, scales, (((0,), (0,)), ((), ())), precision=HIGHEST, preferred_element_type=jnp.float32
+    )
+
+
+def align_kernel(scale_of_energy, steps, spectra_ref, member_ref, own_ref, other_ref, phase_ref, offset_ref, *rest):
+    pieces, (facts_ref, rows_ref, scale_ref) = rest[-3 - len(steps) : -3], rest[-3:]
     windows, rows, _ = spectra_ref.shape
     part = rows // 2 // LEVELS
     level = lax.rem(lax.axis_index("tm"), TEAM) // SIDES
     energy = (own_ref[...] + other_ref[...]) * scale_of_energy
-    scale_ref[...] = lax.dot_general(
-        member_ref[...], lax.rsqrt(energy + epsilon), (((0,), (0,)), ((), ())),
-        precision=HIGHEST, preferred_element_type=jnp.float32,
-    )
+    scales = lax.rsqrt(energy + epsilon)
+    lane = lax.broadcasted_iota(jnp.int32, scales.shape, 1)
+    facts_ref[...] = jnp.where(lane < windows, scales, offset_ref[...])
+    scale_ref[...] = spread(member_ref[...], scales)
     for window in range(windows):
         rows_ref[window] = spectra_ref[window].astype(jnp.float32)
-    for step in range(LEVELS):
+    for step, piece in zip(steps, pieces):
         first = pl.multiple_of((level ^ step) * part, part)
         weights = scale_ref[pl.ds(first, part), :]
         for window in range(windows):
-            cosine = phase_ref[0, window : window + 1, :]
-            sine = phase_ref[1, window : window + 1, :]
-            real = rows_ref[window, pl.ds(2 * first, part, stride=2), :]
-            imag = rows_ref[window, pl.ds(2 * first + 1, part, stride=2), :]
-            weight = weights[:, window : window + 1]
-            pieces[step][window, 0] = (weight * (real * cosine + imag * sine)).astype(jnp.bfloat16)
-            pieces[step][window, 1] = (weight * (imag * cosine - real * sine)).astype(jnp.bfloat16)
-
-
-def gather(pieces, held, before, skip=0):
+            piece[window, 0], piece[window, 1] = rotate(
+                rows_ref[window, pl.ds(2 * first, part, stride=2), :],
+                rows_ref[window, pl.ds(2 * first + 1, part, stride=2), :],
+                weights[:, window : window + 1],
+                phase_ref[0, window : window + 1, :],
+                phase_ref[1, window : window + 1, :],
+            )
+
+
+def align_raw_kernel(raw_ref, member_ref, facts_ref, phase_ref, piece_ref, scale_ref):
+    windows, _, part, _ = raw_ref.shape
+    level = lax.rem(lax.axis_index("tm"), TEAM) // SIDES
+    scale_ref[...] = spread(member_ref[...], facts_ref[...])
+    weights = scale_ref[pl.ds(pl.multiple_of(level * part, part), part), :]
+    for window in range(windows):
+        piece_ref[window, 0], piece_ref[window, 1] = rotate(
+            raw_ref[window, 0].astype(jnp.float32),
+            raw_ref[window, 1].astype(jnp.float32),
+            weights[:, window : window + 1],
+            phase_ref[0, window : window + 1, :],
+            phase_ref[1, window : window + 1, :],
+        )
+
+
+def gather(pieces, held, before, steps=tuple(range(LEVELS))):
     windows = pieces[0].shape[0]
     level = lax.rem(lax.axis_index("tm"), TEAM) // SIDES
     for index, piece in enumerate(pieces):
-        block = (level ^ ((index + skip) % LEVELS)) + (before if index + skip < LEVELS else 0)
+        block = (level ^ steps[index % len(steps)]) + (before if index < len(steps) else 0)
         held[pl.ds(block * windows, windows)] = piece[...]
 
 
@@ -158,7 +202,7 @@
     for left in range(LEVELS):
         for back in range(reach):
             right = left - 1 - back + side
-            late = (right < 0) | ((lax.rem(right + LEVELS, LEVELS) ^ here) >= FIRST_LATE)
+            late = (right < 0) | (((lax.rem(right + LEVELS, LEVELS) ^ here) & 1) == 1)
             wanted = (right >= -halo) & (late == (kernel == 1))
             values = (left, (left + halo) * windows, (right + halo) * windows, (2 * (reach - 1 - back) + 1) * windows)
             for index, value in enumerate(values):
@@ -176,7 +220,10 @@
     grid, (far, units_ref) = refs[3 + count], refs[-2:]
     windows = grid.shape[1]
     turns = list_units(kernel, teams, windows, units_ref)
-    gather(pieces, far, LEVELS if teams else 0, 0 if teams or kernel == 0 else FIRST_LATE)
+    if teams and kernel == 1:
+        gather(pieces, far, LEVELS)
+    else:
+        gather(pieces, far, LEVELS if teams else 0, FAR_STEPS[kernel])
     table = table_ref[...]
 
     def turn(index, carry):
@@ -234,38 +281,67 @@
     params = pltpu.CompilerParams(vmem_limit_bytes=40 * 1024 * 1024)
 
     rows = spectra.reshape(windows, 2 * local_chans, freq)
+    piece_shape = jax.ShapeDtypeStruct((windows, 2, part, freq), jnp.bfloat16)
+    raw_own = pl.pallas_call(
+        split_kernel,
+        out_shape=[piece_shape] * len(RAW),
+        in_specs=[vmem()],
+        out_specs=[vmem()] * len(RAW),
+        scratch_shapes=[pltpu.VMEM((len(RAW), windows, 2 * part, freq), jnp.float32)],
+        compiler_params=params,
+        name="split",
+    )(rows)
+    raw = [flip(piece, "tm", tm_count, step * SIDES) for step, piece in zip(RAW, raw_own)]
     member = (channel_group[None, :] == jnp.arange(GROUPS, dtype=jnp.int32)[:, None]).astype(jnp.float32)
     power = pl.pallas_call(
         power_kernel,
         out_shape=jax.ShapeDtypeStruct((GROUPS, 128), jnp.float32),
-        in_specs=[vmem()] * 2,
+        in_specs=[vmem()] * (2 + len(RAW)),
         out_specs=vmem(),
         scratch_shapes=[pltpu.VMEM((windows, 2 * local_chans, freq), jnp.float32)],
         compiler_params=params,
         name="power",
-    )(rows, member)
+    )(rows, member, *raw_own)
     other_power = flip(power, "chan", chan_count, 1)
-    piece_shape = jax.ShapeDtypeStruct((windows, 2, part, freq), jnp.bfloat16)
-    own = pl.pallas_call(
-        functools.partial(align_kernel, GROUPS / (freq * channels)),
-        out_shape=[piece_shape] * LEVELS,
-        in_specs=[vmem()] * 5,
-        out_specs=[vmem()] * LEVELS,
-        scratch_shapes=[
-            pltpu.VMEM((windows, 2 * local_chans, freq), jnp.float32),
-            pltpu.VMEM((local_chans, 128), jnp.float32),
-        ],
-        compiler_params=params,
-        name="align",
-    )(rows, member, power, other_power, phases(offsets, freq))
+    lanes = power.shape[1]
+    lane = jnp.arange(lanes, dtype=jnp.int32)[:, None] - windows
+    offset_row = jnp.sum(jnp.where(lane == jnp.arange(windows, dtype=jnp.int32)[None, :], offsets[None, :], 0), axis=1)
+    offset_tile = jnp.broadcast_to(offset_row.astype(jnp.float32)[None, :], power.shape)
+    turns = phases(offsets, freq)
+
+    def aligned(steps, *after):
+        return pl.pallas_call(
+            functools.partial(align_kernel, GROUPS / (freq * channels), steps),
+            out_shape=[piece_shape] * len(steps) + [jax.ShapeDtypeStruct(power.shape, jnp.float32)],
+            in_specs=[vmem()] * (6 + len(after)),
+            out_specs=[vmem()] * (len(steps) + 1),
+            scratch_shapes=[
+                pltpu.VMEM((windows, 2 * local_chans, freq), jnp.float32),
+                pltpu.VMEM((local_chans, lanes), jnp.float32),
+            ],
+            compiler_params=params,
+            name="align",
+        )(rows, member, power, other_power, turns, offset_tile, *after)
+
+    own = [None] * LEVELS
+    own[3], own[1], own[0], facts = aligned((3, 1, 0))
 
     near = [own[0]] + [None] * (LEVELS - 1)
     far = [None] * LEVELS
-    for kind, step in EARLY:
-        if kind == "near":
-            near[step] = flip(own[step], "tm", tm_count, step * SIDES)
-        else:
-            far[step] = flip(own[step], "tm", tm_count, step * SIDES + 1)
+    near[3] = flip(own[3], "tm", tm_count, 3 * SIDES)
+    near[1] = flip(own[1], "tm", tm_count, SIDES)
+    far[0] = flip(own[0], "tm", tm_count, 1)
+    for step, piece in zip(RAW, raw):
+        their = flip(facts, "tm", tm_count, step * SIDES)
+        near[step] = pl.pallas_call(
+            align_raw_kernel,
+            out_shape=piece_shape,
+            in_specs=[vmem()] * 4,
+            out_specs=vmem(),
+            scratch_shapes=[pltpu.VMEM((local_chans, lanes), jnp.float32)],
+            compiler_params=params,
+            name="align_raw",
+        )(piece, member, their, phases(their[0, windows : 2 * windows].astype(jnp.int32), freq))
     for step in LATE:
         far[step] = flip(near[step], "tm", tm_count, 1)
     teams = tm_count > TEAM
@@ -287,7 +363,7 @@
         cost_estimate=pl.CostEstimate(flops=2000000000, bytes_accessed=2000000, transcendentals=0),
         name="near",
     )(table, *near)
-    for kernel, pieces in enumerate((far[:FIRST_LATE], far if teams else far[FIRST_LATE:])):
+    for kernel, pieces in enumerate(([far[step] for step in FAR_STEPS[0]], far if teams else [far[step] for step in FAR_STEPS[1]])):
         results = [
             jax.ShapeDtypeStruct(sums_shape, jnp.float32), jax.ShapeDtypeStruct(sums_shape, jnp.bfloat16)
         ] * kernel

time: 40.9 us -> 38.5 us (0.941)
  waiting for transfers between devices: 12.2 us -> 7.41 us
  starting transfers between devices: 17.1 us -> 18.8 us
  local copies, waits for them, and re-layouts: 1.04 us -> 1.7 us
    ppermute x12 -> x13, waiting for transfers between devices: 12.2 us -> 7.41 us  [flip(): lax.ppermute(value, axis, [(source, source ^ bits) for source in range(si...]
    ppermute x12 -> x13, starting transfers between devices: 17.1 us -> 18.8 us  [flip(): lax.ppermute(value, axis, [(source, source ^ bits) for source in range(si...]
    convert_element_type x1, other arithmetic: 0.66 us -> 0.01 us  [shards(): (channel_group[None, :] == jnp.arange(GROUPS, dtype=jnp.int32)[:, None])....]
    unnamed x4 -> x6, local copies, waits for them, and re-layouts: 1.04 us -> 1.69 us
    pallas_call x1 -> x3, Pallas kernels: 0.55 us -> 0.93 us  [the longest x1 0.5 us: aligned(): pl.pallas_call(functools.partial(align_kernel, GROUPS / (freq * channels)...]
  transfers between devices with their start and end apart: 12 -> 13, of which waited for: 6 -> 4; matrix products, arithmetic and copies ran while one was open for 1% -> 2% of each run, Pallas kernels for 14% -> 19%
where the time goes in v4:
time: 38.5 us; the launch traced here: 38.3 us
  starting transfers between devices  18.8 us (49%)
  Pallas kernels  8.9 us (23%)
  waiting for transfers between devices  7.41 us (19%)
  local copies, waits for them, and re-layouts  1.7 us (4%)
  other arithmetic  1.38 us (4%)
    ppermute x13, starting transfers between devices, flip(): lax.ppermute(value, axis, [(source, source ^ bits) for source in range(si...  18.8 us
    ppermute x13, waiting for transfers between devices, flip(): lax.ppermute(value, axis, [(source, source ^ bits) for source in range(si...  7.41 us
    pallas_call x2, Pallas kernels, shards(): pl.pallas_call(functools.partial(far_kernel, kernel, teams, len(pieces)),...  4.17 us
    pallas_call x1, Pallas kernels, shards(): pl.pallas_call(functools.partial(near_kernel, teams, count), out_shape=[g...  3.14 us
    unnamed x6, local copies, waits for them, and re-layouts  1.69 us
  transfers between devices with their start and end apart: 13, of which 4 were waited for; matrix products, arithmetic and copies ran while one was open for 2% of the time, Pallas kernels for 19%

profile of v4, /device:TPU:0, one launch (start us, length us, event | category | flops | bytes accessed | tf_op | source)
XLA Modules:
  0.0 38.3 jit_solution(8028644297589921892)
XLA Ops:
  0.0 1.0 %copy-done = bf16[8,128,2,128]{3,2,1,0:T(2,128)(2,1)S(1)} copy-done((bf16[8,128,2,128]{3,2,1,0:T(2,128)(2,1)S(1)}, bf16[8,128,2,128]{3,2,1,0:T(2,128)(2,1)}, u32[]{:S(2)}) %copy-start) | copy-done | bytes 524312
  1.1 4.1 %collective-permute-start.2 = (bf16[8,2,32,128]{3,2,1,0:T(8,128)(2,1)S(1)}, bf16[8,2,32,128]{3,2,1,0:T(8,128)(2,1)S(1)}, u32[]{:S(2)}, u32[]{:S(2)}) collective-permute-start(bf16[8,2,32,128]{3,2,1,0:T(8,128)(2,1)S(1)} %split.1.rest_0_), channel_id=1, source_target_pairs={{0,8},{2,10},{4,12},{6,14},{8,0},{10,2},{12,4},{14,6},{1,9},{3,11}... | collective-permute-start | bytes 393224 | tf_op jit(solution)/shard_map/ppermute | solution.py:270
  5.2 0.6 %power.1.own_ref = f32[8,128]{1,0:T(8,128)S(1)} custom-call(bf16[8,256,128]{2,1,0:T(8,128)(2,1)S(1)} %bitcast.4, f32[8,128]{1,0:T(8,128)S(1)} %fusion.18.member_ref, bf16[8,2,32,128]{3,2,1,0:T(8,128)(2,1)S(1)} %split.1.rest_0_), custom_call_target="tpu_custom_call" | custom-call | tf_op jit(solution)/shard_map/power/pallas_call | solution.py:296
  5.8 0.6 %copy-done.2 = s32[8]{0:T(128)S(1)} copy-done((s32[8]{0:T(128)S(1)}, s32[8]{0:T(128)}, u32[]{:S(2)}) %copy-start.2) | copy-done | bytes 56
  7.0 0.5 %align.1 = (bf16[8,2,32,128]{3,2,1,0:T(8,128)(2,1)S(1)}, bf16[8,2,32,128]{3,2,1,0:T(8,128)(2,1)S(1)}, bf16[8,2,32,128]{3,2,1,0:T(8,128)(2,1)S(1)}, f32[8,128]{1,0:T(8,128)S(1)}) custom-call(bf16[8,256,128]{2,1,0:T(8,128)(2,1)S(1)} %bitcast.5, f32[8,128]{1,0:T(8,128)S(1)} %fusion.18.member_ref, f32[8,128]{1,0:T(8,128)S(1)} %power.1.own_ref, ...), custom_call_target="tpu_custom_call" | custom-call | tf_op jit(solution)/shard_map/align/pallas_call | solution.py:313
  7.5 0.6 %collective-permute-start.3 = (f32[8,128]{1,0:T(8,128)S(1)}, f32[8,128]{1,0:T(8,128)S(1)}, u32[]{:S(2)}, u32[]{:S(2)}) collective-permute-start(f32[8,128]{1,0:T(8,128)S(1)} %get-tuple-element.19), channel_id=1, source_target_pairs={{0,8},{2,10},{4,12},{6,14},{8,0},{10,2},{12,4},{14,6},{1,9},{3,11}... | collective-permute-start | bytes 12296 | tf_op jit(solution)/shard_map/ppermute | solution.py:270
  8.1 1.6 %collective-permute-start.1 = (bf16[8,2,32,128]{3,2,1,0:T(8,128)(2,1)S(1)}, bf16[8,2,32,128]{3,2,1,0:T(8,128)(2,1)S(1)}, u32[]{:S(2)}, u32[]{:S(2)}) collective-permute-start(bf16[8,2,32,128]{3,2,1,0:T(8,128)(2,1)S(1)} %get-tuple-element.18), channel_id=1, source_target_pairs={{0,4},{2,6},{4,0},{6,2},{8,12},{10,14},{12,8},{14,10},{1,5},{3,7},... | collective-permute-start | bytes 393224 | tf_op jit(solution)/shard_map/ppermute | solution.py:270
  9.7 2.3 %collective-permute-start.4 = (bf16[8,2,32,128]{3,2,1,0:T(8,128)(2,1)S(1)}, bf16[8,2,32,128]{3,2,1,0:T(8,128)(2,1)S(1)}, u32[]{:S(2)}, u32[]{:S(2)}) collective-permute-start(bf16[8,2,32,128]{3,2,1,0:T(8,128)(2,1)S(1)} %get-tuple-element.20), channel_id=1, source_target_pairs={{0,12},{2,14},{4,8},{6,10},{8,4},{10,6},{12,0},{14,2},{1,13},{3,15... | collective-permute-start | bytes 393224 | tf_op jit(solution)/shard_map/ppermute | solution.py:270
  12.0 1.5 %collective-permute-start.5 = (bf16[8,2,32,128]{3,2,1,0:T(8,128)(2,1)S(1)}, bf16[8,2,32,128]{3,2,1,0:T(8,128)(2,1)S(1)}, u32[]{:S(2)}, u32[]{:S(2)}) collective-permute-start(bf16[8,2,32,128]{3,2,1,0:T(8,128)(2,1)S(1)} %get-tuple-element.17.refs_1_), channel_id=1, source_target_pairs={{0,2},{2,0},{4,6},{6,4},{8,10},{10,8},{12,14},{14,12},{1,3},{3,1},... | collective-permute-start | bytes 393224 | tf_op jit(solution)/shard_map/ppermute | solution.py:270
  13.7 0.4 %align_raw.1.refs_3_ = bf16[8,2,32,128]{3,2,1,0:T(8,128)(2,1)S(1)} custom-call(bf16[8,2,32,128]{3,2,1,0:T(8,128)(2,1)S(1)} %collective-permute-done.2.raw_ref, f32[8,128]{1,0:T(8,128)S(1)} %fusion.18.member_ref, f32[8,128]{1,0:T(8,128)S(1)} %collective-permute-done.3.facts_ref, f32[2,8,128]{2,1,0:T(8,128)S(1)} %pad_maximum_fusion.2.phase_ref), custom_call_target="tpu_custom_call" | custom-call | tf_op jit(solution)/shard_map/align_raw/pallas_call | solution.py:336
  14.1 0.6 %collective-permute-start.6 = (bf16[8,2,32,128]{3,2,1,0:T(8,128)(2,1)S(1)}, bf16[8,2,32,128]{3,2,1,0:T(8,128)(2,1)S(1)}, u32[]{:S(2)}, u32[]{:S(2)}) collective-permute-start(bf16[8,2,32,128]{3,2,1,0:T(8,128)(2,1)S(1)} %align_raw.1.refs_3_), channel_id=1, source_target_pairs={{0,2},{2,0},{4,6},{6,4},{8,10},{10,8},{12,14},{14,12},{1,3},{3,1},... | collective-permute-start | bytes 393224 | tf_op jit(solution)/shard_map/ppermute | solution.py:270
  14.7 1.5 %collective-permute-start.7 = (bf16[8,2,32,128]{3,2,1,0:T(8,128)(2,1)S(1)}, bf16[8,2,32,128]{3,2,1,0:T(8,128)(2,1)S(1)}, u32[]{:S(2)}, u32[]{:S(2)}) collective-permute-start(bf16[8,2,32,128]{3,2,1,0:T(8,128)(2,1)S(1)} %collective-permute-done.1.refs_2_), channel_id=1, source_target_pairs={{0,2},{2,0},{4,6},{6,4},{8,10},{10,8},{12,14},{14,12},{1,3},{3,1},... | collective-permute-start | bytes 393224 | tf_op jit(solution)/shard_map/ppermute | solution.py:270
  16.2 2.4 %collective-permute-done.4.refs_4_ = bf16[8,2,32,128]{3,2,1,0:T(8,128)(2,1)S(1)} collective-permute-done((bf16[8,2,32,128]{3,2,1,0:T(8,128)(2,1)S(1)}, bf16[8,2,32,128]{3,2,1,0:T(8,128)(2,1)S(1)}, u32[]{:S(2)}, u32[]{:S(2)}) %collective-permute-start.4) | collective-permute-done | bytes 131104 | tf_op jit(solution)/shard_map/ppermute | solution.py:270
  18.5 1.5 %collective-permute-start.8 = (bf16[8,2,32,128]{3,2,1,0:T(8,128)(2,1)S(1)}, bf16[8,2,32,128]{3,2,1,0:T(8,128)(2,1)S(1)}, u32[]{:S(2)}, u32[]{:S(2)}) collective-permute-start(bf16[8,2,32,128]{3,2,1,0:T(8,128)(2,1)S(1)} %collective-permute-done.4.refs_4_), channel_id=1, source_target_pairs={{0,2},{2,0},{4,6},{6,4},{8,10},{10,8},{12,14},{14,12},{1,3},{3,1},... | collective-permute-start | bytes 393224 | tf_op jit(solution)/shard_map/ppermute | solution.py:270
  20.0 3.1 %near.1 = (f32[4,8,56,128]{3,2,1,0:T(8,128)S(1)}, bf16[32,2,32,128]{3,2,1,0:T(8,128)(2,1)S(1)}) custom-call(bf16[256,128]{1,0:T(8,128)(2,1)S(1)} %pad_maximum_fusion.refs_0_, bf16[8,2,32,128]{3,2,1,0:T(8,128)(2,1)S(1)} %get-tuple-element.17.refs_1_, bf16[8,2,32,128]{3,2,1,0:T(8,128)(2,1)S(1)} %collective-permute-done.1.refs_2_, ...), custom_call_target="tpu_custom_call" | custom-call | flops 2000000000 | bytes 2000000 | tf_op jit(solution)/shard_map/near/pallas_call | solution.py:357
  23.2 2.7 %far.1.refs_1_ = f32[4,8,56,128]{3,2,1,0:T(8,128)S(1)} custom-call(bf16[256,128]{1,0:T(8,128)(2,1)S(1)} %pad_maximum_fusion.refs_0_, f32[4,8,56,128]{3,2,1,0:T(8,128)S(1)} %get-tuple-element.21.refs_1_, bf16[32,2,32,128]{3,2,1,0:T(8,128)(2,1)S(1)} %get-tuple-element.22.refs_2_, ...), custom_call_target="tpu_custom_call", output_to_operand_aliasing={{}: (1, {})} | custom-call | flops 1000000000 | bytes 1000000 | tf_op jit(solution)/shard_map/far/pallas_call | solution.py:370
  25.9 1.5 %late.1 = (f32[4,8,56,128]{3,2,1,0:T(8,128)S(1)}, f32[4,4,48,128]{3,2,1,0:T(8,128)S(1)}, bf16[4,4,48,128]{3,2,1,0:T(8,128)(2,1)S(1)}) custom-call(bf16[256,128]{1,0:T(8,128)(2,1)S(1)} %pad_maximum_fusion.refs_0_, f32[4,8,56,128]{3,2,1,0:T(8,128)S(1)} %far.1.refs_1_, ...), custom_call_target="tpu_custom_call", output_to_operand_aliasing={{0}: (1, {})} | custom-call | flops 1000000000 | bytes 1000000 | tf_op jit(solution)/shard_map/late/pallas_call | solution.py:370
  27.5 1.4 %collective-permute-done.9.other_ref = bf16[4,4,48,128]{3,2,1,0:T(8,128)(2,1)S(1)} collective-permute-done((bf16[4,4,48,128]{3,2,1,0:T(8,128)(2,1)S(1)}, bf16[4,4,48,128]{3,2,1,0:T(8,128)(2,1)S(1)}, u32[]{:S(2)}, u32[]{:S(2)}) %collective-permute-start.9) | collective-permute-done | bytes 196640 | tf_op jit(solution)/shard_map/ppermute | solution.py:270
  29.0 1.8 %collective-permute-start.10 = (bf16[4,48,128]{2,1,0:T(8,128)(2,1)S(1)}, bf16[4,48,128]{2,1,0:T(8,128)(2,1)S(1)}, u32[]{:S(2)}, u32[]{:S(2)}) collective-permute-start(bf16[4,48,128]{2,1,0:T(8,128)(2,1)S(1)} %get-tuple-element.26), channel_id=1, source_target_pairs={{0,8},{2,10},{4,12},{6,14},{8,0},{10,2},{12,4},{14,6},{1,9},{3,11}... | collective-permute-start | bytes 147464 | tf_op jit(solution)/shard_map/ppermute | solution.py:270
  30.7 2.8 %collective-permute-start.11 = (bf16[4,48,128]{2,1,0:T(8,128)(2,1)S(1)}, bf16[4,48,128]{2,1,0:T(8,128)(2,1)S(1)}, u32[]{:S(2)}, u32[]{:S(2)}) collective-permute-start(bf16[4,48,128]{2,1,0:T(8,128)(2,1)S(1)} %get-tuple-element.27), channel_id=1, source_target_pairs={{0,12},{2,14},{4,8},{6,10},{8,4},{10,6},{12,0},{14,2},{1,13},{3,15... | collective-permute-start | bytes 147464 | tf_op jit(solution)/shard_map/ppermute | solution.py:270
  33.5 0.5 %collective-permute-start.12 = (bf16[4,48,128]{2,1,0:T(8,128)(2,1)S(1)}, bf16[4,48,128]{2,1,0:T(8,128)(2,1)S(1)}, u32[]{:S(2)}, u32[]{:S(2)}) collective-permute-start(bf16[4,48,128]{2,1,0:T(8,128)(2,1)S(1)} %get-tuple-element.28), channel_id=1, source_target_pairs={{0,4},{2,6},{4,0},{6,2},{8,12},{10,14},{12,8},{14,10},{1,5},{3,7},... | collective-permute-start | bytes 147464 | tf_op jit(solution)/shard_map/ppermute | solution.py:270
  34.0 2.7 %collective-permute-done.11 = bf16[4,48,128]{2,1,0:T(8,128)(2,1)S(1)} collective-permute-done((bf16[4,48,128]{2,1,0:T(8,128)(2,1)S(1)}, bf16[4,48,128]{2,1,0:T(8,128)(2,1)S(1)}, u32[]{:S(2)}, u32[]{:S(2)}) %collective-permute-start.11) | collective-permute-done | bytes 49184 | tf_op jit(solution)/shard_map/ppermute | solution.py:270
  36.7 0.9 %collective-permute-done.12 = bf16[4,48,128]{2,1,0:T(8,128)(2,1)S(1)} collective-permute-done((bf16[4,48,128]{2,1,0:T(8,128)(2,1)S(1)}, bf16[4,48,128]{2,1,0:T(8,128)(2,1)S(1)}, u32[]{:S(2)}, u32[]{:S(2)}) %collective-permute-start.12) | collective-permute-done | bytes 49184 | tf_op jit(solution)/shard_map/ppermute | solution.py:270
  37.6 0.7 %add_multiply_fusion = f32[4,48,128]{2,1,0:T(8,128)} fusion(bf16[4,48,128]{2,1,0:T(8,128)(2,1)S(1)} %collective-permute-done.12, bf16[4,48,128]{2,1,0:T(8,128)(2,1)S(1)} %collective-permute-done.11, f32[4,48,128]{2,1,0:T(8,128)S(1)} %get-tuple-element.25, bf16[4,48,128]{2,1,0:T(8,128)(2,1)S(1)} %collective-permute-done.10), kind=kLoop, calls=%fused_computation | loop fusion | flops 172032 | bytes 344064 | tf_op jit(solution)/shard_map/mul | solution.py:397
  (30 shorter events, 0.9 us)
Async XLA Ops:
  0.0 1.0 %copy-start = (bf16[8,128,2,128]{3,2,1,0:T(2,128)(2,1)S(1)}, bf16[8,128,2,128]{3,2,1,0:T(2,128)(2,1)}, u32[]{:S(2)}) copy-start(bf16[8,128,2,128]{3,2,1,0:T(2,128)(2,1)} %param.3) | copy-start | bytes 1572868
  1.0 4.1 %copy-start.1 = (s32[128]{0:T(128)S(1)}, s32[128]{0:T(128)}, u32[]{:S(2)}) copy-start(s32[128]{0:T(128)} %param.5) | copy-start | bytes 1540
  1.1 12.6 %collective-permute-start.2 = (bf16[8,2,32,128]{3,2,1,0:T(8,128)(2,1)S(1)}, bf16[8,2,32,128]{3,2,1,0:T(8,128)(2,1)S(1)}, u32[]{:S(2)}, u32[]{:S(2)}) collective-permute-start(bf16[8,2,32,128]{3,2,1,0:T(8,128)(2,1)S(1)} %split.1.rest_0_), channel_id=1, source_target_pairs={{0,8},{2,10},{4,12},{6,14},{8,0},{10,2},{12,4},{14,6},{1,9},{3,11}... | collective-permute-start | bytes 393224 | tf_op jit(solution)/shard_map/ppermute | solution.py:270
  5.8 1.2 %collective-permute-start = (f32[8,128]{1,0:T(8,128)S(1)}, f32[8,128]{1,0:T(8,128)S(1)}, u32[]{:S(2)}, u32[]{:S(2)}) collective-permute-start(f32[8,128]{1,0:T(8,128)S(1)} %power.1.own_ref), channel_id=1, source_target_pairs={{0,1},{1,0},{2,3},{3,2},{4,5},{5,4},{6,7},{7,6},{8,9},{9,8},{10,11... | collective-permute-start | bytes 12296 | tf_op jit(solution)/shard_map/ppermute | solution.py:270
  5.8 0.7 %copy-start.2 = (s32[8]{0:T(128)S(1)}, s32[8]{0:T(128)}, u32[]{:S(2)}) copy-start(s32[8]{0:T(128)} %param.4) | copy-start | bytes 100
  7.5 6.0 %collective-permute-start.3 = (f32[8,128]{1,0:T(8,128)S(1)}, f32[8,128]{1,0:T(8,128)S(1)}, u32[]{:S(2)}, u32[]{:S(2)}) collective-permute-start(f32[8,128]{1,0:T(8,128)S(1)} %get-tuple-element.19), channel_id=1, source_target_pairs={{0,8},{2,10},{4,12},{6,14},{8,0},{10,2},{12,4},{14,6},{1,9},{3,11}... | collective-permute-start | bytes 12296 | tf_op jit(solution)/shard_map/ppermute | solution.py:270
  8.1 6.5 %collective-permute-start.1 = (bf16[8,2,32,128]{3,2,1,0:T(8,128)(2,1)S(1)}, bf16[8,2,32,128]{3,2,1,0:T(8,128)(2,1)S(1)}, u32[]{:S(2)}, u32[]{:S(2)}) collective-permute-start(bf16[8,2,32,128]{3,2,1,0:T(8,128)(2,1)S(1)} %get-tuple-element.18), channel_id=1, source_target_pairs={{0,4},{2,6},{4,0},{6,2},{8,12},{10,14},{12,8},{14,10},{1,5},{3,7},... | collective-permute-start | bytes 393224 | tf_op jit(solution)/shard_map/ppermute | solution.py:270
  9.7 8.8 %collective-permute-start.4 = (bf16[8,2,32,128]{3,2,1,0:T(8,128)(2,1)S(1)}, bf16[8,2,32,128]{3,2,1,0:T(8,128)(2,1)S(1)}, u32[]{:S(2)}, u32[]{:S(2)}) collective-permute-start(bf16[8,2,32,128]{3,2,1,0:T(8,128)(2,1)S(1)} %get-tuple-element.20), channel_id=1, source_target_pairs={{0,12},{2,14},{4,8},{6,10},{8,4},{10,6},{12,0},{14,2},{1,13},{3,15... | collective-permute-start | bytes 393224 | tf_op jit(solution)/shard_map/ppermute | solution.py:270
  12.0 11.2 %collective-permute-start.5 = (bf16[8,2,32,128]{3,2,1,0:T(8,128)(2,1)S(1)}, bf16[8,2,32,128]{3,2,1,0:T(8,128)(2,1)S(1)}, u32[]{:S(2)}, u32[]{:S(2)}) collective-permute-start(bf16[8,2,32,128]{3,2,1,0:T(8,128)(2,1)S(1)} %get-tuple-element.17.refs_1_), channel_id=1, source_target_pairs={{0,2},{2,0},{4,6},{6,4},{8,10},{10,8},{12,14},{14,12},{1,3},{3,1},... | collective-permute-start | bytes 393224 | tf_op jit(solution)/shard_map/ppermute | solution.py:270
  14.1 9.1 %collective-permute-start.6 = (bf16[8,2,32,128]{3,2,1,0:T(8,128)(2,1)S(1)}, bf16[8,2,32,128]{3,2,1,0:T(8,128)(2,1)S(1)}, u32[]{:S(2)}, u32[]{:S(2)}) collective-permute-start(bf16[8,2,32,128]{3,2,1,0:T(8,128)(2,1)S(1)} %align_raw.1.refs_3_), channel_id=1, source_target_pairs={{0,2},{2,0},{4,6},{6,4},{8,10},{10,8},{12,14},{14,12},{1,3},{3,1},... | collective-permute-start | bytes 393224 | tf_op jit(solution)/shard_map/ppermute | solution.py:270
  14.7 11.2 %collective-permute-start.7 = (bf16[8,2,32,128]{3,2,1,0:T(8,128)(2,1)S(1)}, bf16[8,2,32,128]{3,2,1,0:T(8,128)(2,1)S(1)}, u32[]{:S(2)}, u32[]{:S(2)}) collective-permute-start(bf16[8,2,32,128]{3,2,1,0:T(8,128)(2,1)S(1)} %collective-permute-done.1.refs_2_), channel_id=1, source_target_pairs={{0,2},{2,0},{4,6},{6,4},{8,10},{10,8},{12,14},{14,12},{1,3},{3,1},... | collective-permute-start | bytes 393224 | tf_op jit(solution)/shard_map/ppermute | solution.py:270
  18.5 7.4 %collective-permute-start.8 = (bf16[8,2,32,128]{3,2,1,0:T(8,128)(2,1)S(1)}, bf16[8,2,32,128]{3,2,1,0:T(8,128)(2,1)S(1)}, u32[]{:S(2)}, u32[]{:S(2)}) collective-permute-start(bf16[8,2,32,128]{3,2,1,0:T(8,128)(2,1)S(1)} %collective-permute-done.4.refs_4_), channel_id=1, source_target_pairs={{0,2},{2,0},{4,6},{6,4},{8,10},{10,8},{12,14},{14,12},{1,3},{3,1},... | collective-permute-start | bytes 393224 | tf_op jit(solution)/shard_map/ppermute | solution.py:270
  27.4 1.5 %collective-permute-start.9 = (bf16[4,4,48,128]{3,2,1,0:T(8,128)(2,1)S(1)}, bf16[4,4,48,128]{3,2,1,0:T(8,128)(2,1)S(1)}, u32[]{:S(2)}, u32[]{:S(2)}) collective-permute-start(bf16[4,4,48,128]{3,2,1,0:T(8,128)(2,1)S(1)} %get-tuple-element.24), channel_id=1, source_target_pairs={{0,1},{1,0},{2,3},{3,2},{4,5},{5,4},{6,7},{7,6},{8,9},{9,8},{10,11... | collective-permute-start | bytes 589832 | tf_op jit(solution)/shard_map/ppermute | solution.py:270
  29.0 5.1 %collective-permute-start.10 = (bf16[4,48,128]{2,1,0:T(8,128)(2,1)S(1)}, bf16[4,48,128]{2,1,0:T(8,128)(2,1)S(1)}, u32[]{:S(2)}, u32[]{:S(2)}) collective-permute-start(bf16[4,48,128]{2,1,0:T(8,128)(2,1)S(1)} %get-tuple-element.26), channel_id=1, source_target_pairs={{0,8},{2,10},{4,12},{6,14},{8,0},{10,2},{12,4},{14,6},{1,9},{3,11}... | collective-permute-start | bytes 147464 | tf_op jit(solution)/shard_map/ppermute | solution.py:270
  30.7 6.0 %collective-permute-start.11 = (bf16[4,48,128]{2,1,0:T(8,128)(2,1)S(1)}, bf16[4,48,128]{2,1,0:T(8,128)(2,1)S(1)}, u32[]{:S(2)}, u32[]{:S(2)}) collective-permute-start(bf16[4,48,128]{2,1,0:T(8,128)(2,1)S(1)} %get-tuple-element.27), channel_id=1, source_target_pairs={{0,12},{2,14},{4,8},{6,10},{8,4},{10,6},{12,0},{14,2},{1,13},{3,15... | collective-permute-start | bytes 147464 | tf_op jit(solution)/shard_map/ppermute | solution.py:270
  33.5 4.1 %collective-permute-start.12 = (bf16[4,48,128]{2,1,0:T(8,128)(2,1)S(1)}, bf16[4,48,128]{2,1,0:T(8,128)(2,1)S(1)}, u32[]{:S(2)}, u32[]{:S(2)}) collective-permute-start(bf16[4,48,128]{2,1,0:T(8,128)(2,1)S(1)} %get-tuple-element.28), channel_id=1, source_target_pairs={{0,4},{2,6},{4,0},{6,2},{8,12},{10,14},{12,8},{14,10},{1,5},{3,7},... | collective-permute-start | bytes 147464 | tf_op jit(solution)/shard_map/ppermute | solution.py:270

commit v5 on v4

--- a/solution.py
+++ b/solution.py
@@ -15,10 +15,10 @@
 LEVELS = 4
 TEAM = SIDES * LEVELS
 FAR_STEPS = ((0, 2), (1, 3))
-UNROLL = 3
+UNROLL = 2
 RAW = (2,)
 LATE = 2
-UNROLL = 3
+UNROLL = 2
 EARLY = (("near", 2), ("far", 0), ("near", 3), ("near", 1), ("far", 1))
 LATE = (2, 1, 3)
 OUT_ORDER = (2, 3, 1)

time: 38.5 us -> 37.6 us (0.977)
  Pallas kernels: 8.9 us -> 7.65 us
    pallas_call x2, Pallas kernels: 4.17 us -> 2.92 us  [shards(): pl.pallas_call(functools.partial(far_kernel, kernel, teams, len(pieces)),...]
  transfers between devices with their start and end apart: 13 -> 13, of which waited for: 4 -> 5; matrix products, arithmetic and copies ran while one was open for 2% -> 2% of each run, Pallas kernels for 19% -> 17%
where the time goes in v5:
time: 37.6 us; the launch traced here: 37.5 us
  starting transfers between devices  18.8 us (50%)
  waiting for transfers between devices  7.78 us (21%)
  Pallas kernels  7.65 us (20%)
  local copies, waits for them, and re-layouts  1.7 us (5%)
  other arithmetic  1.38 us (4%)
    ppermute x13, starting transfers between devices, flip(): lax.ppermute(value, axis, [(source, source ^ bits) for source in range(si...  18.8 us
    ppermute x13, waiting for transfers between devices, flip(): lax.ppermute(value, axis, [(source, source ^ bits) for source in range(si...  7.78 us
    pallas_call x1, Pallas kernels, shards(): pl.pallas_call(functools.partial(near_kernel, teams, count), out_shape=[g...  3.14 us
    pallas_call x2, Pallas kernels, shards(): pl.pallas_call(functools.partial(far_kernel, kernel, teams, len(pieces)),...  2.92 us
    unnamed x6, local copies, waits for them, and re-layouts  1.69 us
  transfers between devices with their start and end apart: 13, of which 5 were waited for; matrix products, arithmetic and copies ran while one was open for 2% of the time, Pallas kernels for 17%

profile of v5, /device:TPU:0, one launch (start us, length us, event | category | flops | bytes accessed | tf_op | source)
XLA Modules:
  0.0 37.5 jit_solution(2481131050159963744)
XLA Ops:
  0.0 1.0 %copy-done = bf16[8,128,2,128]{3,2,1,0:T(2,128)(2,1)S(1)} copy-done((bf16[8,128,2,128]{3,2,1,0:T(2,128)(2,1)S(1)}, bf16[8,128,2,128]{3,2,1,0:T(2,128)(2,1)}, u32[]{:S(2)}) %copy-start) | copy-done | bytes 524312
  1.1 4.1 %collective-permute-start.2 = (bf16[8,2,32,128]{3,2,1,0:T(8,128)(2,1)S(1)}, bf16[8,2,32,128]{3,2,1,0:T(8,128)(2,1)S(1)}, u32[]{:S(2)}, u32[]{:S(2)}) collective-permute-start(bf16[8,2,32,128]{3,2,1,0:T(8,128)(2,1)S(1)} %split.1.rest_0_), channel_id=1, source_target_pairs={{0,8},{2,10},{4,12},{6,14},{8,0},{10,2},{12,4},{14,6},{1,9},{3,11}... | collective-permute-start | bytes 393224 | tf_op jit(solution)/shard_map/ppermute | solution.py:270
  5.2 0.6 %power.1.own_ref = f32[8,128]{1,0:T(8,128)S(1)} custom-call(bf16[8,256,128]{2,1,0:T(8,128)(2,1)S(1)} %bitcast.4, f32[8,128]{1,0:T(8,128)S(1)} %fusion.18.member_ref, bf16[8,2,32,128]{3,2,1,0:T(8,128)(2,1)S(1)} %split.1.rest_0_), custom_call_target="tpu_custom_call" | custom-call | tf_op jit(solution)/shard_map/power/pallas_call | solution.py:296
  5.8 0.6 %copy-done.2 = s32[8]{0:T(128)S(1)} copy-done((s32[8]{0:T(128)S(1)}, s32[8]{0:T(128)}, u32[]{:S(2)}) %copy-start.2) | copy-done | bytes 56
  7.0 0.5 %align.1 = (bf16[8,2,32,128]{3,2,1,0:T(8,128)(2,1)S(1)}, bf16[8,2,32,128]{3,2,1,0:T(8,128)(2,1)S(1)}, bf16[8,2,32,128]{3,2,1,0:T(8,128)(2,1)S(1)}, f32[8,128]{1,0:T(8,128)S(1)}) custom-call(bf16[8,256,128]{2,1,0:T(8,128)(2,1)S(1)} %bitcast.5, f32[8,128]{1,0:T(8,128)S(1)} %fusion.18.member_ref, f32[8,128]{1,0:T(8,128)S(1)} %power.1.own_ref, ...), custom_call_target="tpu_custom_call" | custom-call | tf_op jit(solution)/shard_map/align/pallas_call | solution.py:313
  7.5 0.6 %collective-permute-start.3 = (f32[8,128]{1,0:T(8,128)S(1)}, f32[8,128]{1,0:T(8,128)S(1)}, u32[]{:S(2)}, u32[]{:S(2)}) collective-permute-start(f32[8,128]{1,0:T(8,128)S(1)} %get-tuple-element.19), channel_id=1, source_target_pairs={{0,8},{2,10},{4,12},{6,14},{8,0},{10,2},{12,4},{14,6},{1,9},{3,11}... | collective-permute-start | bytes 12296 | tf_op jit(solution)/shard_map/ppermute | solution.py:270
  8.1 1.6 %collective-permute-start.1 = (bf16[8,2,32,128]{3,2,1,0:T(8,128)(2,1)S(1)}, bf16[8,2,32,128]{3,2,1,0:T(8,128)(2,1)S(1)}, u32[]{:S(2)}, u32[]{:S(2)}) collective-permute-start(bf16[8,2,32,128]{3,2,1,0:T(8,128)(2,1)S(1)} %get-tuple-element.18), channel_id=1, source_target_pairs={{0,4},{2,6},{4,0},{6,2},{8,12},{10,14},{12,8},{14,10},{1,5},{3,7},... | collective-permute-start | bytes 393224 | tf_op jit(solution)/shard_map/ppermute | solution.py:270
  9.7 2.3 %collective-permute-start.4 = (bf16[8,2,32,128]{3,2,1,0:T(8,128)(2,1)S(1)}, bf16[8,2,32,128]{3,2,1,0:T(8,128)(2,1)S(1)}, u32[]{:S(2)}, u32[]{:S(2)}) collective-permute-start(bf16[8,2,32,128]{3,2,1,0:T(8,128)(2,1)S(1)} %get-tuple-element.20), channel_id=1, source_target_pairs={{0,12},{2,14},{4,8},{6,10},{8,4},{10,6},{12,0},{14,2},{1,13},{3,15... | collective-permute-start | bytes 393224 | tf_op jit(solution)/shard_map/ppermute | solution.py:270
  12.0 1.5 %collective-permute-start.5 = (bf16[8,2,32,128]{3,2,1,0:T(8,128)(2,1)S(1)}, bf16[8,2,32,128]{3,2,1,0:T(8,128)(2,1)S(1)}, u32[]{:S(2)}, u32[]{:S(2)}) collective-permute-start(bf16[8,2,32,128]{3,2,1,0:T(8,128)(2,1)S(1)} %get-tuple-element.17.refs_1_), channel_id=1, source_target_pairs={{0,2},{2,0},{4,6},{6,4},{8,10},{10,8},{12,14},{14,12},{1,3},{3,1},... | collective-permute-start | bytes 393224 | tf_op jit(solution)/shard_map/ppermute | solution.py:270
  13.7 0.4 %align_raw.1.refs_3_ = bf16[8,2,32,128]{3,2,1,0:T(8,128)(2,1)S(1)} custom-call(bf16[8,2,32,128]{3,2,1,0:T(8,128)(2,1)S(1)} %collective-permute-done.2.raw_ref, f32[8,128]{1,0:T(8,128)S(1)} %fusion.18.member_ref, f32[8,128]{1,0:T(8,128)S(1)} %collective-permute-done.3.facts_ref, f32[2,8,128]{2,1,0:T(8,128)S(1)} %pad_maximum_fusion.2.phase_ref), custom_call_target="tpu_custom_call" | custom-call | tf_op jit(solution)/shard_map/align_raw/pallas_call | solution.py:336
  14.1 0.6 %collective-permute-start.6 = (bf16[8,2,32,128]{3,2,1,0:T(8,128)(2,1)S(1)}, bf16[8,2,32,128]{3,2,1,0:T(8,128)(2,1)S(1)}, u32[]{:S(2)}, u32[]{:S(2)}) collective-permute-start(bf16[8,2,32,128]{3,2,1,0:T(8,128)(2,1)S(1)} %align_raw.1.refs_3_), channel_id=1, source_target_pairs={{0,2},{2,0},{4,6},{6,4},{8,10},{10,8},{12,14},{14,12},{1,3},{3,1},... | collective-permute-start | bytes 393224 | tf_op jit(solution)/shard_map/ppermute | solution.py:270
  14.7 1.5 %collective-permute-start.7 = (bf16[8,2,32,128]{3,2,1,0:T(8,128)(2,1)S(1)}, bf16[8,2,32,128]{3,2,1,0:T(8,128)(2,1)S(1)}, u32[]{:S(2)}, u32[]{:S(2)}) collective-permute-start(bf16[8,2,32,128]{3,2,1,0:T(8,128)(2,1)S(1)} %collective-permute-done.1.refs_2_), channel_id=1, source_target_pairs={{0,2},{2,0},{4,6},{6,4},{8,10},{10,8},{12,14},{14,12},{1,3},{3,1},... | collective-permute-start | bytes 393224 | tf_op jit(solution)/shard_map/ppermute | solution.py:270
  16.2 2.4 %collective-permute-done.4.refs_4_ = bf16[8,2,32,128]{3,2,1,0:T(8,128)(2,1)S(1)} collective-permute-done((bf16[8,2,32,128]{3,2,1,0:T(8,128)(2,1)S(1)}, bf16[8,2,32,128]{3,2,1,0:T(8,128)(2,1)S(1)}, u32[]{:S(2)}, u32[]{:S(2)}) %collective-permute-start.4) | collective-permute-done | bytes 131104 | tf_op jit(solution)/shard_map/ppermute | solution.py:270
  18.5 1.5 %collective-permute-start.8 = (bf16[8,2,32,128]{3,2,1,0:T(8,128)(2,1)S(1)}, bf16[8,2,32,128]{3,2,1,0:T(8,128)(2,1)S(1)}, u32[]{:S(2)}, u32[]{:S(2)}) collective-permute-start(bf16[8,2,32,128]{3,2,1,0:T(8,128)(2,1)S(1)} %collective-permute-done.4.refs_4_), channel_id=1, source_target_pairs={{0,2},{2,0},{4,6},{6,4},{8,10},{10,8},{12,14},{14,12},{1,3},{3,1},... | collective-permute-start | bytes 393224 | tf_op jit(solution)/shard_map/ppermute | solution.py:270
  20.0 3.1 %near.1 = (f32[4,8,56,128]{3,2,1,0:T(8,128)S(1)}, bf16[32,2,32,128]{3,2,1,0:T(8,128)(2,1)S(1)}) custom-call(bf16[256,128]{1,0:T(8,128)(2,1)S(1)} %pad_maximum_fusion.refs_0_, bf16[8,2,32,128]{3,2,1,0:T(8,128)(2,1)S(1)} %get-tuple-element.17.refs_1_, bf16[8,2,32,128]{3,2,1,0:T(8,128)(2,1)S(1)} %collective-permute-done.1.refs_2_, ...), custom_call_target="tpu_custom_call" | custom-call | flops 2000000000 | bytes 2000000 | tf_op jit(solution)/shard_map/near/pallas_call | solution.py:357
  23.2 1.9 %far.1.refs_1_ = f32[4,8,56,128]{3,2,1,0:T(8,128)S(1)} custom-call(bf16[256,128]{1,0:T(8,128)(2,1)S(1)} %pad_maximum_fusion.refs_0_, f32[4,8,56,128]{3,2,1,0:T(8,128)S(1)} %get-tuple-element.21.refs_1_, bf16[32,2,32,128]{3,2,1,0:T(8,128)(2,1)S(1)} %get-tuple-element.22.refs_2_, ...), custom_call_target="tpu_custom_call", output_to_operand_aliasing={{}: (1, {})} | custom-call | flops 1000000000 | bytes 1000000 | tf_op jit(solution)/shard_map/far/pallas_call | solution.py:370
  25.5 1.0 %late.1 = (f32[4,8,56,128]{3,2,1,0:T(8,128)S(1)}, f32[4,4,48,128]{3,2,1,0:T(8,128)S(1)}, bf16[4,4,48,128]{3,2,1,0:T(8,128)(2,1)S(1)}) custom-call(bf16[256,128]{1,0:T(8,128)(2,1)S(1)} %pad_maximum_fusion.refs_0_, f32[4,8,56,128]{3,2,1,0:T(8,128)S(1)} %far.1.refs_1_, ...), custom_call_target="tpu_custom_call", output_to_operand_aliasing={{0}: (1, {})} | custom-call | flops 1000000000 | bytes 1000000 | tf_op jit(solution)/shard_map/late/pallas_call | solution.py:370
  26.6 1.4 %collective-permute-done.9.other_ref = bf16[4,4,48,128]{3,2,1,0:T(8,128)(2,1)S(1)} collective-permute-done((bf16[4,4,48,128]{3,2,1,0:T(8,128)(2,1)S(1)}, bf16[4,4,48,128]{3,2,1,0:T(8,128)(2,1)S(1)}, u32[]{:S(2)}, u32[]{:S(2)}) %collective-permute-start.9) | collective-permute-done | bytes 196640 | tf_op jit(solution)/shard_map/ppermute | solution.py:270
  28.1 1.6 %collective-permute-start.10 = (bf16[4,48,128]{2,1,0:T(8,128)(2,1)S(1)}, bf16[4,48,128]{2,1,0:T(8,128)(2,1)S(1)}, u32[]{:S(2)}, u32[]{:S(2)}) collective-permute-start(bf16[4,48,128]{2,1,0:T(8,128)(2,1)S(1)} %get-tuple-element.26), channel_id=1, source_target_pairs={{0,8},{2,10},{4,12},{6,14},{8,0},{10,2},{12,4},{14,6},{1,9},{3,11}... | collective-permute-start | bytes 147464 | tf_op jit(solution)/shard_map/ppermute | solution.py:270
  29.7 3.0 %collective-permute-start.11 = (bf16[4,48,128]{2,1,0:T(8,128)(2,1)S(1)}, bf16[4,48,128]{2,1,0:T(8,128)(2,1)S(1)}, u32[]{:S(2)}, u32[]{:S(2)}) collective-permute-start(bf16[4,48,128]{2,1,0:T(8,128)(2,1)S(1)} %get-tuple-element.27), channel_id=1, source_target_pairs={{0,12},{2,14},{4,8},{6,10},{8,4},{10,6},{12,0},{14,2},{1,13},{3,15... | collective-permute-start | bytes 147464 | tf_op jit(solution)/shard_map/ppermute | solution.py:270
  32.7 0.5 %collective-permute-start.12 = (bf16[4,48,128]{2,1,0:T(8,128)(2,1)S(1)}, bf16[4,48,128]{2,1,0:T(8,128)(2,1)S(1)}, u32[]{:S(2)}, u32[]{:S(2)}) collective-permute-start(bf16[4,48,128]{2,1,0:T(8,128)(2,1)S(1)} %get-tuple-element.28), channel_id=1, source_target_pairs={{0,4},{2,6},{4,0},{6,2},{8,12},{10,14},{12,8},{14,10},{1,5},{3,7},... | collective-permute-start | bytes 147464 | tf_op jit(solution)/shard_map/ppermute | solution.py:270
  33.2 2.6 %collective-permute-done.11 = bf16[4,48,128]{2,1,0:T(8,128)(2,1)S(1)} collective-permute-done((bf16[4,48,128]{2,1,0:T(8,128)(2,1)S(1)}, bf16[4,48,128]{2,1,0:T(8,128)(2,1)S(1)}, u32[]{:S(2)}, u32[]{:S(2)}) %collective-permute-start.11) | collective-permute-done | bytes 49184 | tf_op jit(solution)/shard_map/ppermute | solution.py:270
  35.8 1.0 %collective-permute-done.12 = bf16[4,48,128]{2,1,0:T(8,128)(2,1)S(1)} collective-permute-done((bf16[4,48,128]{2,1,0:T(8,128)(2,1)S(1)}, bf16[4,48,128]{2,1,0:T(8,128)(2,1)S(1)}, u32[]{:S(2)}, u32[]{:S(2)}) %collective-permute-start.12) | collective-permute-done | bytes 49184 | tf_op jit(solution)/shard_map/ppermute | solution.py:270
  36.8 0.7 %add_multiply_fusion = f32[4,48,128]{2,1,0:T(8,128)} fusion(bf16[4,48,128]{2,1,0:T(8,128)(2,1)S(1)} %collective-permute-done.12, bf16[4,48,128]{2,1,0:T(8,128)(2,1)S(1)} %collective-permute-done.11, f32[4,48,128]{2,1,0:T(8,128)S(1)} %get-tuple-element.25, bf16[4,48,128]{2,1,0:T(8,128)(2,1)S(1)} %collective-permute-done.10), kind=kLoop, calls=%fused_computation | loop fusion | flops 172032 | bytes 344064 | tf_op jit(solution)/shard_map/mul | solution.py:397
  (30 shorter events, 1.3 us)
Async XLA Ops:
  0.0 1.0 %copy-start = (bf16[8,128,2,128]{3,2,1,0:T(2,128)(2,1)S(1)}, bf16[8,128,2,128]{3,2,1,0:T(2,128)(2,1)}, u32[]{:S(2)}) copy-start(bf16[8,128,2,128]{3,2,1,0:T(2,128)(2,1)} %param.3) | copy-start | bytes 1572868
  1.0 4.1 %copy-start.1 = (s32[128]{0:T(128)S(1)}, s32[128]{0:T(128)}, u32[]{:S(2)}) copy-start(s32[128]{0:T(128)} %param.5) | copy-start | bytes 1540
  1.1 12.6 %collective-permute-start.2 = (bf16[8,2,32,128]{3,2,1,0:T(8,128)(2,1)S(1)}, bf16[8,2,32,128]{3,2,1,0:T(8,128)(2,1)S(1)}, u32[]{:S(2)}, u32[]{:S(2)}) collective-permute-start(bf16[8,2,32,128]{3,2,1,0:T(8,128)(2,1)S(1)} %split.1.rest_0_), channel_id=1, source_target_pairs={{0,8},{2,10},{4,12},{6,14},{8,0},{10,2},{12,4},{14,6},{1,9},{3,11}... | collective-permute-start | bytes 393224 | tf_op jit(solution)/shard_map/ppermute | solution.py:270
  5.8 1.2 %collective-permute-start = (f32[8,128]{1,0:T(8,128)S(1)}, f32[8,128]{1,0:T(8,128)S(1)}, u32[]{:S(2)}, u32[]{:S(2)}) collective-permute-start(f32[8,128]{1,0:T(8,128)S(1)} %power.1.own_ref), channel_id=1, source_target_pairs={{0,1},{1,0},{2,3},{3,2},{4,5},{5,4},{6,7},{7,6},{8,9},{9,8},{10,11... | collective-permute-start | bytes 12296 | tf_op jit(solution)/shard_map/ppermute | solution.py:270
  5.8 0.7 %copy-start.2 = (s32[8]{0:T(128)S(1)}, s32[8]{0:T(128)}, u32[]{:S(2)}) copy-start(s32[8]{0:T(128)} %param.4) | copy-start | bytes 100
  7.5 6.0 %collective-permute-start.3 = (f32[8,128]{1,0:T(8,128)S(1)}, f32[8,128]{1,0:T(8,128)S(1)}, u32[]{:S(2)}, u32[]{:S(2)}) collective-permute-start(f32[8,128]{1,0:T(8,128)S(1)} %get-tuple-element.19), channel_id=1, source_target_pairs={{0,8},{2,10},{4,12},{6,14},{8,0},{10,2},{12,4},{14,6},{1,9},{3,11}... | collective-permute-start | bytes 12296 | tf_op jit(solution)/shard_map/ppermute | solution.py:270
  8.1 6.5 %collective-permute-start.1 = (bf16[8,2,32,128]{3,2,1,0:T(8,128)(2,1)S(1)}, bf16[8,2,32,128]{3,2,1,0:T(8,128)(2,1)S(1)}, u32[]{:S(2)}, u32[]{:S(2)}) collective-permute-start(bf16[8,2,32,128]{3,2,1,0:T(8,128)(2,1)S(1)} %get-tuple-element.18), channel_id=1, source_target_pairs={{0,4},{2,6},{4,0},{6,2},{8,12},{10,14},{12,8},{14,10},{1,5},{3,7},... | collective-permute-start | bytes 393224 | tf_op jit(solution)/shard_map/ppermute | solution.py:270
  9.7 8.8 %collective-permute-start.4 = (bf16[8,2,32,128]{3,2,1,0:T(8,128)(2,1)S(1)}, bf16[8,2,32,128]{3,2,1,0:T(8,128)(2,1)S(1)}, u32[]{:S(2)}, u32[]{:S(2)}) collective-permute-start(bf16[8,2,32,128]{3,2,1,0:T(8,128)(2,1)S(1)} %get-tuple-element.20), channel_id=1, source_target_pairs={{0,12},{2,14},{4,8},{6,10},{8,4},{10,6},{12,0},{14,2},{1,13},{3,15... | collective-permute-start | bytes 393224 | tf_op jit(solution)/shard_map/ppermute | solution.py:270
  12.0 11.2 %collective-permute-start.5 = (bf16[8,2,32,128]{3,2,1,0:T(8,128)(2,1)S(1)}, bf16[8,2,32,128]{3,2,1,0:T(8,128)(2,1)S(1)}, u32[]{:S(2)}, u32[]{:S(2)}) collective-permute-start(bf16[8,2,32,128]{3,2,1,0:T(8,128)(2,1)S(1)} %get-tuple-element.17.refs_1_), channel_id=1, source_target_pairs={{0,2},{2,0},{4,6},{6,4},{8,10},{10,8},{12,14},{14,12},{1,3},{3,1},... | collective-permute-start | bytes 393224 | tf_op jit(solution)/shard_map/ppermute | solution.py:270
  14.1 9.1 %collective-permute-start.6 = (bf16[8,2,32,128]{3,2,1,0:T(8,128)(2,1)S(1)}, bf16[8,2,32,128]{3,2,1,0:T(8,128)(2,1)S(1)}, u32[]{:S(2)}, u32[]{:S(2)}) collective-permute-start(bf16[8,2,32,128]{3,2,1,0:T(8,128)(2,1)S(1)} %align_raw.1.refs_3_), channel_id=1, source_target_pairs={{0,2},{2,0},{4,6},{6,4},{8,10},{10,8},{12,14},{14,12},{1,3},{3,1},... | collective-permute-start | bytes 393224 | tf_op jit(solution)/shard_map/ppermute | solution.py:270
  14.7 10.4 %collective-permute-start.7 = (bf16[8,2,32,128]{3,2,1,0:T(8,128)(2,1)S(1)}, bf16[8,2,32,128]{3,2,1,0:T(8,128)(2,1)S(1)}, u32[]{:S(2)}, u32[]{:S(2)}) collective-permute-start(bf16[8,2,32,128]{3,2,1,0:T(8,128)(2,1)S(1)} %collective-permute-done.1.refs_2_), channel_id=1, source_target_pairs={{0,2},{2,0},{4,6},{6,4},{8,10},{10,8},{12,14},{14,12},{1,3},{3,1},... | collective-permute-start | bytes 393224 | tf_op jit(solution)/shard_map/ppermute | solution.py:270
  18.5 6.9 %collective-permute-start.8 = (bf16[8,2,32,128]{3,2,1,0:T(8,128)(2,1)S(1)}, bf16[8,2,32,128]{3,2,1,0:T(8,128)(2,1)S(1)}, u32[]{:S(2)}, u32[]{:S(2)}) collective-permute-start(bf16[8,2,32,128]{3,2,1,0:T(8,128)(2,1)S(1)} %collective-permute-done.4.refs_4_), channel_id=1, source_target_pairs={{0,2},{2,0},{4,6},{6,4},{8,10},{10,8},{12,14},{14,12},{1,3},{3,1},... | collective-permute-start | bytes 393224 | tf_op jit(solution)/shard_map/ppermute | solution.py:270
  26.5 1.5 %collective-permute-start.9 = (bf16[4,4,48,128]{3,2,1,0:T(8,128)(2,1)S(1)}, bf16[4,4,48,128]{3,2,1,0:T(8,128)(2,1)S(1)}, u32[]{:S(2)}, u32[]{:S(2)}) collective-permute-start(bf16[4,4,48,128]{3,2,1,0:T(8,128)(2,1)S(1)} %get-tuple-element.24), channel_id=1, source_target_pairs={{0,1},{1,0},{2,3},{3,2},{4,5},{5,4},{6,7},{7,6},{8,9},{9,8},{10,11... | collective-permute-start | bytes 589832 | tf_op jit(solution)/shard_map/ppermute | solution.py:270
  28.1 5.1 %collective-permute-start.10 = (bf16[4,48,128]{2,1,0:T(8,128)(2,1)S(1)}, bf16[4,48,128]{2,1,0:T(8,128)(2,1)S(1)}, u32[]{:S(2)}, u32[]{:S(2)}) collective-permute-start(bf16[4,48,128]{2,1,0:T(8,128)(2,1)S(1)} %get-tuple-element.26), channel_id=1, source_target_pairs={{0,8},{2,10},{4,12},{6,14},{8,0},{10,2},{12,4},{14,6},{1,9},{3,11}... | collective-permute-start | bytes 147464 | tf_op jit(solution)/shard_map/ppermute | solution.py:270
  29.7 6.2 %collective-permute-start.11 = (bf16[4,48,128]{2,1,0:T(8,128)(2,1)S(1)}, bf16[4,48,128]{2,1,0:T(8,128)(2,1)S(1)}, u32[]{:S(2)}, u32[]{:S(2)}) collective-permute-start(bf16[4,48,128]{2,1,0:T(8,128)(2,1)S(1)} %get-tuple-element.27), channel_id=1, source_target_pairs={{0,12},{2,14},{4,8},{6,10},{8,4},{10,6},{12,0},{14,2},{1,13},{3,15... | collective-permute-start | bytes 147464 | tf_op jit(solution)/shard_map/ppermute | solution.py:270
  32.7 4.1 %collective-permute-start.12 = (bf16[4,48,128]{2,1,0:T(8,128)(2,1)S(1)}, bf16[4,48,128]{2,1,0:T(8,128)(2,1)S(1)}, u32[]{:S(2)}, u32[]{:S(2)}) collective-permute-start(bf16[4,48,128]{2,1,0:T(8,128)(2,1)S(1)} %get-tuple-element.28), channel_id=1, source_target_pairs={{0,4},{2,6},{4,0},{6,2},{8,12},{10,14},{12,8},{14,10},{1,5},{3,7},... | collective-permute-start | bytes 147464 | tf_op jit(solution)/shard_map/ppermute | solution.py:270

commit v6 on v5

--- a/solution.py
+++ b/solution.py
@@ -208,37 +208,41 @@
             for index, value in enumerate(values):
                 units_ref[4 * found + index] = jnp.int32(value)
             found = jnp.where(wanted, found + 1, found)
-    last = jnp.maximum(found - 1, 0)
-    for extra in range(UNROLL - 1):
-        for index in range(4):
-            units_ref[4 * (found + extra) + index] = units_ref[4 * last + index]
-    return (found + UNROLL - 1) // UNROLL
+    return found
 
 
 def far_kernel(kernel, teams, count, *refs):
     table_ref, _, near, pieces = refs[0], refs[1], refs[2], refs[3 : 3 + count]
     grid, (far, units_ref) = refs[3 + count], refs[-2:]
     windows = grid.shape[1]
-    turns = list_units(kernel, teams, windows, units_ref)
+    found = list_units(kernel, teams, windows, units_ref)
     if teams and kernel == 1:
         gather(pieces, far, LEVELS)
     else:
         gather(pieces, far, LEVELS if teams else 0, FAR_STEPS[kernel])
     table = table_ref[...]
 
+    def unit(at):
+        level = units_ref[at]
+        row = pl.multiple_of(units_ref[at + 3], windows)
+
+        def store(window, sums):
+            grid[level, window, pl.ds(row, windows), :] = sums
+
+        block_sums(near, units_ref[at + 1], far, units_ref[at + 2], windows, table, store)
+
     def turn(index, carry):
         for inner in range(UNROLL):
-            at = 4 * (index * UNROLL + inner)
-            level = units_ref[at]
-            row = pl.multiple_of(units_ref[at + 3], windows)
-
-            def store(window, sums):
-                grid[level, window, pl.ds(row, windows), :] = sums
-
-            block_sums(near, units_ref[at + 1], far, units_ref[at + 2], windows, table, store)
+            unit(4 * (index * UNROLL + inner))
         return carry
 
+    def single(index, carry):
+        unit(4 * index)
+        return carry
+
+    turns = found // UNROLL
     lax.fori_loop(0, turns, turn, 0)
+    lax.fori_loop(turns * UNROLL, found, single, 0)
     if kernel == 1:
         mine_ref, other_ref = refs[4 + count : 6 + count]
         core = lax.axis_index("chan")

time: 37.6 us -> 37.6 us (level)
  no operation moved by 1% of the time
where the time goes in v6:
time: 37.6 us; the launch traced here: 37.5 us
  starting transfers between devices  18.8 us (50%)
  waiting for transfers between devices  7.78 us (21%)
  Pallas kernels  7.64 us (20%)
  local copies, waits for them, and re-layouts  1.7 us (5%)
  other arithmetic  1.38 us (4%)
    ppermute x13, starting transfers between devices, flip(): lax.ppermute(value, axis, [(source, source ^ bits) for source in range(si...  18.8 us
    ppermute x13, waiting for transfers between devices, flip(): lax.ppermute(value, axis, [(source, source ^ bits) for source in range(si...  7.78 us
    pallas_call x1, Pallas kernels, shards(): pl.pallas_call(functools.partial(near_kernel, teams, count), out_shape=[g...  3.14 us
    pallas_call x2, Pallas kernels, shards(): pl.pallas_call(functools.partial(far_kernel, kernel, teams, len(pieces)),...  2.91 us
    unnamed x6, local copies, waits for them, and re-layouts  1.69 us
  transfers between devices with their start and end apart: 13, of which 5 were waited for; matrix products, arithmetic and copies ran while one was open for 2% of the time, Pallas kernels for 17%

profile of v6, /device:TPU:0, one launch (start us, length us, event | category | flops | bytes accessed | tf_op | source)
XLA Modules:
  0.0 37.5 jit_solution(15732876394984964903)
XLA Ops:
  0.0 1.0 %copy-done = bf16[8,128,2,128]{3,2,1,0:T(2,128)(2,1)S(1)} copy-done((bf16[8,128,2,128]{3,2,1,0:T(2,128)(2,1)S(1)}, bf16[8,128,2,128]{3,2,1,0:T(2,128)(2,1)}, u32[]{:S(2)}) %copy-start) | copy-done | bytes 524312
  1.1 4.1 %collective-permute-start.2 = (bf16[8,2,32,128]{3,2,1,0:T(8,128)(2,1)S(1)}, bf16[8,2,32,128]{3,2,1,0:T(8,128)(2,1)S(1)}, u32[]{:S(2)}, u32[]{:S(2)}) collective-permute-start(bf16[8,2,32,128]{3,2,1,0:T(8,128)(2,1)S(1)} %split.1.rest_0_), channel_id=1, source_target_pairs={{0,8},{2,10},{4,12},{6,14},{8,0},{10,2},{12,4},{14,6},{1,9},{3,11}... | collective-permute-start | bytes 393224 | tf_op jit(solution)/shard_map/ppermute | solution.py:274
  5.2 0.6 %power.1.own_ref = f32[8,128]{1,0:T(8,128)S(1)} custom-call(bf16[8,256,128]{2,1,0:T(8,128)(2,1)S(1)} %bitcast.4, f32[8,128]{1,0:T(8,128)S(1)} %fusion.18.member_ref, bf16[8,2,32,128]{3,2,1,0:T(8,128)(2,1)S(1)} %split.1.rest_0_), custom_call_target="tpu_custom_call" | custom-call | tf_op jit(solution)/shard_map/power/pallas_call | solution.py:300
  5.8 0.6 %copy-done.2 = s32[8]{0:T(128)S(1)} copy-done((s32[8]{0:T(128)S(1)}, s32[8]{0:T(128)}, u32[]{:S(2)}) %copy-start.2) | copy-done | bytes 56
  7.0 0.5 %align.1 = (bf16[8,2,32,128]{3,2,1,0:T(8,128)(2,1)S(1)}, bf16[8,2,32,128]{3,2,1,0:T(8,128)(2,1)S(1)}, bf16[8,2,32,128]{3,2,1,0:T(8,128)(2,1)S(1)}, f32[8,128]{1,0:T(8,128)S(1)}) custom-call(bf16[8,256,128]{2,1,0:T(8,128)(2,1)S(1)} %bitcast.5, f32[8,128]{1,0:T(8,128)S(1)} %fusion.18.member_ref, f32[8,128]{1,0:T(8,128)S(1)} %power.1.own_ref, ...), custom_call_target="tpu_custom_call" | custom-call | tf_op jit(solution)/shard_map/align/pallas_call | solution.py:317
  7.5 0.6 %collective-permute-start.3 = (f32[8,128]{1,0:T(8,128)S(1)}, f32[8,128]{1,0:T(8,128)S(1)}, u32[]{:S(2)}, u32[]{:S(2)}) collective-permute-start(f32[8,128]{1,0:T(8,128)S(1)} %get-tuple-element.19), channel_id=1, source_target_pairs={{0,8},{2,10},{4,12},{6,14},{8,0},{10,2},{12,4},{14,6},{1,9},{3,11}... | collective-permute-start | bytes 12296 | tf_op jit(solution)/shard_map/ppermute | solution.py:274
  8.1 1.6 %collective-permute-start.1 = (bf16[8,2,32,128]{3,2,1,0:T(8,128)(2,1)S(1)}, bf16[8,2,32,128]{3,2,1,0:T(8,128)(2,1)S(1)}, u32[]{:S(2)}, u32[]{:S(2)}) collective-permute-start(bf16[8,2,32,128]{3,2,1,0:T(8,128)(2,1)S(1)} %get-tuple-element.18), channel_id=1, source_target_pairs={{0,4},{2,6},{4,0},{6,2},{8,12},{10,14},{12,8},{14,10},{1,5},{3,7},... | collective-permute-start | bytes 393224 | tf_op jit(solution)/shard_map/ppermute | solution.py:274
  9.7 2.3 %collective-permute-start.4 = (bf16[8,2,32,128]{3,2,1,0:T(8,128)(2,1)S(1)}, bf16[8,2,32,128]{3,2,1,0:T(8,128)(2,1)S(1)}, u32[]{:S(2)}, u32[]{:S(2)}) collective-permute-start(bf16[8,2,32,128]{3,2,1,0:T(8,128)(2,1)S(1)} %get-tuple-element.20), channel_id=1, source_target_pairs={{0,12},{2,14},{4,8},{6,10},{8,4},{10,6},{12,0},{14,2},{1,13},{3,15... | collective-permute-start | bytes 393224 | tf_op jit(solution)/shard_map/ppermute | solution.py:274
  12.0 1.5 %collective-permute-start.5 = (bf16[8,2,32,128]{3,2,1,0:T(8,128)(2,1)S(1)}, bf16[8,2,32,128]{3,2,1,0:T(8,128)(2,1)S(1)}, u32[]{:S(2)}, u32[]{:S(2)}) collective-permute-start(bf16[8,2,32,128]{3,2,1,0:T(8,128)(2,1)S(1)} %get-tuple-element.17.refs_1_), channel_id=1, source_target_pairs={{0,2},{2,0},{4,6},{6,4},{8,10},{10,8},{12,14},{14,12},{1,3},{3,1},... | collective-permute-start | bytes 393224 | tf_op jit(solution)/shard_map/ppermute | solution.py:274
  13.7 0.4 %align_raw.1.refs_3_ = bf16[8,2,32,128]{3,2,1,0:T(8,128)(2,1)S(1)} custom-call(bf16[8,2,32,128]{3,2,1,0:T(8,128)(2,1)S(1)} %collective-permute-done.2.raw_ref, f32[8,128]{1,0:T(8,128)S(1)} %fusion.18.member_ref, f32[8,128]{1,0:T(8,128)S(1)} %collective-permute-done.3.facts_ref, f32[2,8,128]{2,1,0:T(8,128)S(1)} %pad_maximum_fusion.2.phase_ref), custom_call_target="tpu_custom_call" | custom-call | tf_op jit(solution)/shard_map/align_raw/pallas_call | solution.py:340
  14.1 0.6 %collective-permute-start.6 = (bf16[8,2,32,128]{3,2,1,0:T(8,128)(2,1)S(1)}, bf16[8,2,32,128]{3,2,1,0:T(8,128)(2,1)S(1)}, u32[]{:S(2)}, u32[]{:S(2)}) collective-permute-start(bf16[8,2,32,128]{3,2,1,0:T(8,128)(2,1)S(1)} %align_raw.1.refs_3_), channel_id=1, source_target_pairs={{0,2},{2,0},{4,6},{6,4},{8,10},{10,8},{12,14},{14,12},{1,3},{3,1},... | collective-permute-start | bytes 393224 | tf_op jit(solution)/shard_map/ppermute | solution.py:274
  14.7 1.5 %collective-permute-start.7 = (bf16[8,2,32,128]{3,2,1,0:T(8,128)(2,1)S(1)}, bf16[8,2,32,128]{3,2,1,0:T(8,128)(2,1)S(1)}, u32[]{:S(2)}, u32[]{:S(2)}) collective-permute-start(bf16[8,2,32,128]{3,2,1,0:T(8,128)(2,1)S(1)} %collective-permute-done.1.refs_2_), channel_id=1, source_target_pairs={{0,2},{2,0},{4,6},{6,4},{8,10},{10,8},{12,14},{14,12},{1,3},{3,1},... | collective-permute-start | bytes 393224 | tf_op jit(solution)/shard_map/ppermute | solution.py:274
  16.2 2.4 %collective-permute-done.4.refs_4_ = bf16[8,2,32,128]{3,2,1,0:T(8,128)(2,1)S(1)} collective-permute-done((bf16[8,2,32,128]{3,2,1,0:T(8,128)(2,1)S(1)}, bf16[8,2,32,128]{3,2,1,0:T(8,128)(2,1)S(1)}, u32[]{:S(2)}, u32[]{:S(2)}) %collective-permute-start.4) | collective-permute-done | bytes 131104 | tf_op jit(solution)/shard_map/ppermute | solution.py:274
  18.5 1.5 %collective-permute-start.8 = (bf16[8,2,32,128]{3,2,1,0:T(8,128)(2,1)S(1)}, bf16[8,2,32,128]{3,2,1,0:T(8,128)(2,1)S(1)}, u32[]{:S(2)}, u32[]{:S(2)}) collective-permute-start(bf16[8,2,32,128]{3,2,1,0:T(8,128)(2,1)S(1)} %collective-permute-done.4.refs_4_), channel_id=1, source_target_pairs={{0,2},{2,0},{4,6},{6,4},{8,10},{10,8},{12,14},{14,12},{1,3},{3,1},... | collective-permute-start | bytes 393224 | tf_op jit(solution)/shard_map/ppermute | solution.py:274
  20.0 3.1 %near.1 = (f32[4,8,56,128]{3,2,1,0:T(8,128)S(1)}, bf16[32,2,32,128]{3,2,1,0:T(8,128)(2,1)S(1)}) custom-call(bf16[256,128]{1,0:T(8,128)(2,1)S(1)} %pad_maximum_fusion.refs_0_, bf16[8,2,32,128]{3,2,1,0:T(8,128)(2,1)S(1)} %get-tuple-element.17.refs_1_, bf16[8,2,32,128]{3,2,1,0:T(8,128)(2,1)S(1)} %collective-permute-done.1.refs_2_, ...), custom_call_target="tpu_custom_call" | custom-call | flops 2000000000 | bytes 2000000 | tf_op jit(solution)/shard_map/near/pallas_call | solution.py:361
  23.2 1.9 %far.1.refs_1_ = f32[4,8,56,128]{3,2,1,0:T(8,128)S(1)} custom-call(bf16[256,128]{1,0:T(8,128)(2,1)S(1)} %pad_maximum_fusion.refs_0_, f32[4,8,56,128]{3,2,1,0:T(8,128)S(1)} %get-tuple-element.21.refs_1_, bf16[32,2,32,128]{3,2,1,0:T(8,128)(2,1)S(1)} %get-tuple-element.22.refs_2_, ...), custom_call_target="tpu_custom_call", output_to_operand_aliasing={{}: (1, {})} | custom-call | flops 1000000000 | bytes 1000000 | tf_op jit(solution)/shard_map/far/pallas_call | solution.py:374
  25.5 1.0 %late.1 = (f32[4,8,56,128]{3,2,1,0:T(8,128)S(1)}, f32[4,4,48,128]{3,2,1,0:T(8,128)S(1)}, bf16[4,4,48,128]{3,2,1,0:T(8,128)(2,1)S(1)}) custom-call(bf16[256,128]{1,0:T(8,128)(2,1)S(1)} %pad_maximum_fusion.refs_0_, f32[4,8,56,128]{3,2,1,0:T(8,128)S(1)} %far.1.refs_1_, ...), custom_call_target="tpu_custom_call", output_to_operand_aliasing={{0}: (1, {})} | custom-call | flops 1000000000 | bytes 1000000 | tf_op jit(solution)/shard_map/late/pallas_call | solution.py:374
  26.6 1.4 %collective-permute-done.9.other_ref = bf16[4,4,48,128]{3,2,1,0:T(8,128)(2,1)S(1)} collective-permute-done((bf16[4,4,48,128]{3,2,1,0:T(8,128)(2,1)S(1)}, bf16[4,4,48,128]{3,2,1,0:T(8,128)(2,1)S(1)}, u32[]{:S(2)}, u32[]{:S(2)}) %collective-permute-start.9) | collective-permute-done | bytes 196640 | tf_op jit(solution)/shard_map/ppermute | solution.py:274
  28.1 1.6 %collective-permute-start.10 = (bf16[4,48,128]{2,1,0:T(8,128)(2,1)S(1)}, bf16[4,48,128]{2,1,0:T(8,128)(2,1)S(1)}, u32[]{:S(2)}, u32[]{:S(2)}) collective-permute-start(bf16[4,48,128]{2,1,0:T(8,128)(2,1)S(1)} %get-tuple-element.26), channel_id=1, source_target_pairs={{0,8},{2,10},{4,12},{6,14},{8,0},{10,2},{12,4},{14,6},{1,9},{3,11}... | collective-permute-start | bytes 147464 | tf_op jit(solution)/shard_map/ppermute | solution.py:274
  29.7 3.0 %collective-permute-start.11 = (bf16[4,48,128]{2,1,0:T(8,128)(2,1)S(1)}, bf16[4,48,128]{2,1,0:T(8,128)(2,1)S(1)}, u32[]{:S(2)}, u32[]{:S(2)}) collective-permute-start(bf16[4,48,128]{2,1,0:T(8,128)(2,1)S(1)} %get-tuple-element.27), channel_id=1, source_target_pairs={{0,12},{2,14},{4,8},{6,10},{8,4},{10,6},{12,0},{14,2},{1,13},{3,15... | collective-permute-start | bytes 147464 | tf_op jit(solution)/shard_map/ppermute | solution.py:274
  32.7 0.5 %collective-permute-start.12 = (bf16[4,48,128]{2,1,0:T(8,128)(2,1)S(1)}, bf16[4,48,128]{2,1,0:T(8,128)(2,1)S(1)}, u32[]{:S(2)}, u32[]{:S(2)}) collective-permute-start(bf16[4,48,128]{2,1,0:T(8,128)(2,1)S(1)} %get-tuple-element.28), channel_id=1, source_target_pairs={{0,4},{2,6},{4,0},{6,2},{8,12},{10,14},{12,8},{14,10},{1,5},{3,7},... | collective-permute-start | bytes 147464 | tf_op jit(solution)/shard_map/ppermute | solution.py:274
  33.2 2.6 %collective-permute-done.11 = bf16[4,48,128]{2,1,0:T(8,128)(2,1)S(1)} collective-permute-done((bf16[4,48,128]{2,1,0:T(8,128)(2,1)S(1)}, bf16[4,48,128]{2,1,0:T(8,128)(2,1)S(1)}, u32[]{:S(2)}, u32[]{:S(2)}) %collective-permute-start.11) | collective-permute-done | bytes 49184 | tf_op jit(solution)/shard_map/ppermute | solution.py:274
  35.8 1.0 %collective-permute-done.12 = bf16[4,48,128]{2,1,0:T(8,128)(2,1)S(1)} collective-permute-done((bf16[4,48,128]{2,1,0:T(8,128)(2,1)S(1)}, bf16[4,48,128]{2,1,0:T(8,128)(2,1)S(1)}, u32[]{:S(2)}, u32[]{:S(2)}) %collective-permute-start.12) | collective-permute-done | bytes 49184 | tf_op jit(solution)/shard_map/ppermute | solution.py:274
  36.8 0.7 %add_multiply_fusion = f32[4,48,128]{2,1,0:T(8,128)} fusion(bf16[4,48,128]{2,1,0:T(8,128)(2,1)S(1)} %collective-permute-done.12, bf16[4,48,128]{2,1,0:T(8,128)(2,1)S(1)} %collective-permute-done.11, f32[4,48,128]{2,1,0:T(8,128)S(1)} %get-tuple-element.25, bf16[4,48,128]{2,1,0:T(8,128)(2,1)S(1)} %collective-permute-done.10), kind=kLoop, calls=%fused_computation | loop fusion | flops 172032 | bytes 344064 | tf_op jit(solution)/shard_map/mul | solution.py:401
  (30 shorter events, 1.3 us)
Async XLA Ops:
  0.0 1.0 %copy-start = (bf16[8,128,2,128]{3,2,1,0:T(2,128)(2,1)S(1)}, bf16[8,128,2,128]{3,2,1,0:T(2,128)(2,1)}, u32[]{:S(2)}) copy-start(bf16[8,128,2,128]{3,2,1,0:T(2,128)(2,1)} %param.3) | copy-start | bytes 1572868
  1.0 4.1 %copy-start.1 = (s32[128]{0:T(128)S(1)}, s32[128]{0:T(128)}, u32[]{:S(2)}) copy-start(s32[128]{0:T(128)} %param.5) | copy-start | bytes 1540
  1.1 12.6 %collective-permute-start.2 = (bf16[8,2,32,128]{3,2,1,0:T(8,128)(2,1)S(1)}, bf16[8,2,32,128]{3,2,1,0:T(8,128)(2,1)S(1)}, u32[]{:S(2)}, u32[]{:S(2)}) collective-permute-start(bf16[8,2,32,128]{3,2,1,0:T(8,128)(2,1)S(1)} %split.1.rest_0_), channel_id=1, source_target_pairs={{0,8},{2,10},{4,12},{6,14},{8,0},{10,2},{12,4},{14,6},{1,9},{3,11}... | collective-permute-start | bytes 393224 | tf_op jit(solution)/shard_map/ppermute | solution.py:274
  5.8 1.2 %collective-permute-start = (f32[8,128]{1,0:T(8,128)S(1)}, f32[8,128]{1,0:T(8,128)S(1)}, u32[]{:S(2)}, u32[]{:S(2)}) collective-permute-start(f32[8,128]{1,0:T(8,128)S(1)} %power.1.own_ref), channel_id=1, source_target_pairs={{0,1},{1,0},{2,3},{3,2},{4,5},{5,4},{6,7},{7,6},{8,9},{9,8},{10,11... | collective-permute-start | bytes 12296 | tf_op jit(solution)/shard_map/ppermute | solution.py:274
  5.8 0.7 %copy-start.2 = (s32[8]{0:T(128)S(1)}, s32[8]{0:T(128)}, u32[]{:S(2)}) copy-start(s32[8]{0:T(128)} %param.4) | copy-start | bytes 100
  7.5 6.0 %collective-permute-start.3 = (f32[8,128]{1,0:T(8,128)S(1)}, f32[8,128]{1,0:T(8,128)S(1)}, u32[]{:S(2)}, u32[]{:S(2)}) collective-permute-start(f32[8,128]{1,0:T(8,128)S(1)} %get-tuple-element.19), channel_id=1, source_target_pairs={{0,8},{2,10},{4,12},{6,14},{8,0},{10,2},{12,4},{14,6},{1,9},{3,11}... | collective-permute-start | bytes 12296 | tf_op jit(solution)/shard_map/ppermute | solution.py:274
  8.1 6.5 %collective-permute-start.1 = (bf16[8,2,32,128]{3,2,1,0:T(8,128)(2,1)S(1)}, bf16[8,2,32,128]{3,2,1,0:T(8,128)(2,1)S(1)}, u32[]{:S(2)}, u32[]{:S(2)}) collective-permute-start(bf16[8,2,32,128]{3,2,1,0:T(8,128)(2,1)S(1)} %get-tuple-element.18), channel_id=1, source_target_pairs={{0,4},{2,6},{4,0},{6,2},{8,12},{10,14},{12,8},{14,10},{1,5},{3,7},... | collective-permute-start | bytes 393224 | tf_op jit(solution)/shard_map/ppermute | solution.py:274
  9.7 8.8 %collective-permute-start.4 = (bf16[8,2,32,128]{3,2,1,0:T(8,128)(2,1)S(1)}, bf16[8,2,32,128]{3,2,1,0:T(8,128)(2,1)S(1)}, u32[]{:S(2)}, u32[]{:S(2)}) collective-permute-start(bf16[8,2,32,128]{3,2,1,0:T(8,128)(2,1)S(1)} %get-tuple-element.20), channel_id=1, source_target_pairs={{0,12},{2,14},{4,8},{6,10},{8,4},{10,6},{12,0},{14,2},{1,13},{3,15... | collective-permute-start | bytes 393224 | tf_op jit(solution)/shard_map/ppermute | solution.py:274
  12.0 11.2 %collective-permute-start.5 = (bf16[8,2,32,128]{3,2,1,0:T(8,128)(2,1)S(1)}, bf16[8,2,32,128]{3,2,1,0:T(8,128)(2,1)S(1)}, u32[]{:S(2)}, u32[]{:S(2)}) collective-permute-start(bf16[8,2,32,128]{3,2,1,0:T(8,128)(2,1)S(1)} %get-tuple-element.17.refs_1_), channel_id=1, source_target_pairs={{0,2},{2,0},{4,6},{6,4},{8,10},{10,8},{12,14},{14,12},{1,3},{3,1},... | collective-permute-start | bytes 393224 | tf_op jit(solution)/shard_map/ppermute | solution.py:274
  14.1 9.1 %collective-permute-start.6 = (bf16[8,2,32,128]{3,2,1,0:T(8,128)(2,1)S(1)}, bf16[8,2,32,128]{3,2,1,0:T(8,128)(2,1)S(1)}, u32[]{:S(2)}, u32[]{:S(2)}) collective-permute-start(bf16[8,2,32,128]{3,2,1,0:T(8,128)(2,1)S(1)} %align_raw.1.refs_3_), channel_id=1, source_target_pairs={{0,2},{2,0},{4,6},{6,4},{8,10},{10,8},{12,14},{14,12},{1,3},{3,1},... | collective-permute-start | bytes 393224 | tf_op jit(solution)/shard_map/ppermute | solution.py:274
  14.7 10.4 %collective-permute-start.7 = (bf16[8,2,32,128]{3,2,1,0:T(8,128)(2,1)S(1)}, bf16[8,2,32,128]{3,2,1,0:T(8,128)(2,1)S(1)}, u32[]{:S(2)}, u32[]{:S(2)}) collective-permute-start(bf16[8,2,32,128]{3,2,1,0:T(8,128)(2,1)S(1)} %collective-permute-done.1.refs_2_), channel_id=1, source_target_pairs={{0,2},{2,0},{4,6},{6,4},{8,10},{10,8},{12,14},{14,12},{1,3},{3,1},... | collective-permute-start | bytes 393224 | tf_op jit(solution)/shard_map/ppermute | solution.py:274
  18.5 6.9 %collective-permute-start.8 = (bf16[8,2,32,128]{3,2,1,0:T(8,128)(2,1)S(1)}, bf16[8,2,32,128]{3,2,1,0:T(8,128)(2,1)S(1)}, u32[]{:S(2)}, u32[]{:S(2)}) collective-permute-start(bf16[8,2,32,128]{3,2,1,0:T(8,128)(2,1)S(1)} %collective-permute-done.4.refs_4_), channel_id=1, source_target_pairs={{0,2},{2,0},{4,6},{6,4},{8,10},{10,8},{12,14},{14,12},{1,3},{3,1},... | collective-permute-start | bytes 393224 | tf_op jit(solution)/shard_map/ppermute | solution.py:274
  26.5 1.5 %collective-permute-start.9 = (bf16[4,4,48,128]{3,2,1,0:T(8,128)(2,1)S(1)}, bf16[4,4,48,128]{3,2,1,0:T(8,128)(2,1)S(1)}, u32[]{:S(2)}, u32[]{:S(2)}) collective-permute-start(bf16[4,4,48,128]{3,2,1,0:T(8,128)(2,1)S(1)} %get-tuple-element.24), channel_id=1, source_target_pairs={{0,1},{1,0},{2,3},{3,2},{4,5},{5,4},{6,7},{7,6},{8,9},{9,8},{10,11... | collective-permute-start | bytes 589832 | tf_op jit(solution)/shard_map/ppermute | solution.py:274
  28.1 5.1 %collective-permute-start.10 = (bf16[4,48,128]{2,1,0:T(8,128)(2,1)S(1)}, bf16[4,48,128]{2,1,0:T(8,128)(2,1)S(1)}, u32[]{:S(2)}, u32[]{:S(2)}) collective-permute-start(bf16[4,48,128]{2,1,0:T(8,128)(2,1)S(1)} %get-tuple-element.26), channel_id=1, source_target_pairs={{0,8},{2,10},{4,12},{6,14},{8,0},{10,2},{12,4},{14,6},{1,9},{3,11}... | collective-permute-start | bytes 147464 | tf_op jit(solution)/shard_map/ppermute | solution.py:274
  29.7 6.2 %collective-permute-start.11 = (bf16[4,48,128]{2,1,0:T(8,128)(2,1)S(1)}, bf16[4,48,128]{2,1,0:T(8,128)(2,1)S(1)}, u32[]{:S(2)}, u32[]{:S(2)}) collective-permute-start(bf16[4,48,128]{2,1,0:T(8,128)(2,1)S(1)} %get-tuple-element.27), channel_id=1, source_target_pairs={{0,12},{2,14},{4,8},{6,10},{8,4},{10,6},{12,0},{14,2},{1,13},{3,15... | collective-permute-start | bytes 147464 | tf_op jit(solution)/shard_map/ppermute | solution.py:274
  32.7 4.1 %collective-permute-start.12 = (bf16[4,48,128]{2,1,0:T(8,128)(2,1)S(1)}, bf16[4,48,128]{2,1,0:T(8,128)(2,1)S(1)}, u32[]{:S(2)}, u32[]{:S(2)}) collective-permute-start(bf16[4,48,128]{2,1,0:T(8,128)(2,1)S(1)} %get-tuple-element.28), channel_id=1, source_target_pairs={{0,4},{2,6},{4,0},{6,2},{8,12},{10,14},{12,8},{14,10},{1,5},{3,7},... | collective-permute-start | bytes 147464 | tf_op jit(solution)/shard_map/ppermute | solution.py:274
